TPU v7x, 32 devices: a whole 2x2x4 slice. The times are simulated.
32 devices in a mesh: sub: 8 (over z, x), grp: 4 (over y, core).
Axes of the slice: x: 2, y: 2, z: 4, core: 2. Of those that a mesh axis runs over, the one named last changes fastest.
Arguments:
- flexibility: bfloat16 [8, 4, 512, 512], P('sub', 'grp'), as said below
- dirichlet_schur: bfloat16 [8, 4, 512, 512], P('sub', 'grp'), as said below
- subdomain_loads: bfloat16 [8, 4, 512, 128], P('sub', 'grp'), may hold values from -6 to 6
- coupling: bfloat16 [8, 4, 512, 24], P('sub', 'grp'), may hold values from -0.25 to 0.25
- coarse_rows: bfloat16 [8, 4, 24, 2048], P('sub', 'grp'), as said below
- neighbors: int32 [8, 4, 6], P('sub', 'grp'), may hold values from 0 to 7, as said below
- interface_rows: int32 [8, 4, 6, 16], P('sub', 'grp'), may hold values from 0 to 511, as said below
- coarse_map: int32 [8, 4, 24], P('sub', 'grp'), may hold values from 0 to 2047, as said below
Outputs:
- solution: float32 [8, 4, 512, 128], P('sub', 'grp')
- preconditioned: float32 [8, 4, 512, 128], P('sub', 'grp')
Inputs may be any that keep to these rules, and one draw needn't show every extreme that they name: `neighbors`: each subdomain lists 6 distinct sub indices other than its own, of subdomains with the same grp index; if subdomain (i, g) lists j, then (j, g) lists i. `interface_rows`: the 6 x 16 rows of one subdomain are distinct; the j-th row that s lists for neighbor t and the j-th row that t lists for s are the same interface point. `coarse_map`: the 24 entries of one subdomain are distinct. coarse_rows of subdomain s are the rows coarse_map of s of one symmetric positive definite matrix of order 2048. `flexibility`: each subdomain's block is symmetric positive definite. `dirichlet_schur`: each subdomain's block is symmetric positive definite.
All inputs are finite; a program needn't handle non-finite values.
Results may differ from a plain program's by a relative error of at most 0.0084.
Values may be sent and summed in bfloat16 or wider, within the bound.
No kernel may reach another device: no remote copies, remote signals or barrier semaphores. Data moves between devices by JAX's collectives and lax.ppermute only.
A program may use at most 64 MiB of HBM per device.

v0:
```python
import jax
import jax.numpy as jnp
from jax import lax
from jax.sharding import PartitionSpec as P


def body(
    flexibility,
    dirichlet_schur,
    subdomain_loads,
    coupling,
    coarse_rows,
    neighbors,
    interface_rows,
    coarse_map,
):
    flex_block = flexibility[0, 0]
    schur_block = dirichlet_schur[0, 0]
    loads_block = subdomain_loads[0, 0]
    couple_block = coupling[0, 0]
    coarse_block = coarse_rows[0, 0]
    neighbor_ids = neighbors[0, 0]
    row_lists = interface_rows[0, 0]
    corner_ids = coarse_map[0, 0]
    order_size = flex_block.shape[0]
    column_count = loads_block.shape[1]
    coarse_size = coarse_block.shape[1]
    line_size = lax.axis_size("sub")
    flat_rows = row_lists.reshape(-1)
    destinations = (
        jnp.arange(line_size, dtype=jnp.int32)[:, None] == neighbor_ids[None, :]
    ).astype(jnp.bfloat16)
    pair_mask = jnp.zeros((order_size,), jnp.float32).at[flat_rows].set(1.0)
    weight = (1.0 - 0.5 * pair_mask)[:, None]

    def jump_field(surface):
        picked = surface[flat_rows].reshape(row_lists.shape + (column_count,))
        outgoing = jnp.einsum(
            "dk,kjc->djc", destinations, picked, preferred_element_type=jnp.float32
        ).astype(jnp.bfloat16)
        incoming = lax.all_to_all(outgoing, "sub", split_axis=0, concat_axis=0, tiled=True)
        matched = jnp.einsum(
            "dk,djc->kjc", destinations, incoming, preferred_element_type=jnp.float32
        )
        placed = (
            jnp.zeros((order_size, column_count), jnp.float32)
            .at[flat_rows]
            .set(matched.reshape(-1, column_count))
        )
        return surface.astype(jnp.float32) - placed

    def precondition(residual):
        scaled = (weight * residual).astype(jnp.bfloat16)
        schur_image = jnp.dot(schur_block, scaled, preferred_element_type=jnp.float32).astype(
            jnp.bfloat16
        )
        return weight * jump_field(schur_image)

    def column_dot(first_field, second_field):
        return lax.psum(jnp.sum(weight * first_field * second_field, axis=0), ("sub", "grp"))

    residual = jump_field(loads_block)
    zfield = precondition(residual)
    direction = zfield
    inner = column_dot(residual, zfield)
    dir_half = direction.astype(jnp.bfloat16)
    local_part = jnp.dot(flex_block, dir_half, preferred_element_type=jnp.float32)
    coarse_in = jnp.dot(couple_block.T, dir_half, preferred_element_type=jnp.float32)
    dense_sum = jnp.zeros((coarse_size, column_count), jnp.float32).at[corner_ids].set(coarse_in)
    partial_rows = lax.psum_scatter(dense_sum, "grp", scatter_dimension=0, tiled=True)
    panel_half = lax.psum(partial_rows, "sub").astype(jnp.bfloat16)
    coarse_val = jnp.dot(
        coarse_block,
        lax.all_gather(panel_half, "grp", axis=0, tiled=True),
        preferred_element_type=jnp.float32,
    ).astype(jnp.bfloat16)
    surface = (
        local_part + jnp.dot(couple_block, coarse_val, preferred_element_type=jnp.float32)
    ).astype(jnp.bfloat16)
    operated = jump_field(surface)
    step_size = inner / column_dot(direction, operated)
    solution = step_size * direction
    residual = residual - step_size * operated
    zfield = precondition(residual)
    return (solution[None, None], zfield[None, None])


def solution(mesh):
    placed = (
        P("sub", "grp", None, None),
        P("sub", "grp", None, None),
        P("sub", "grp", None, None),
        P("sub", "grp", None, None),
        P("sub", "grp", None, None),
        P("sub", "grp", None),
        P("sub", "grp", None, None),
        P("sub", "grp", None),
    )
    return jax.shard_map(
        body,
        mesh=mesh,
        in_specs=placed,
        out_specs=(P("sub", "grp", None, None), P("sub", "grp", None, None)),
        check_vma=False,
    )
```

profile of v0, /device:TPU:0, one launch (start us, length us, event | category | flops | bytes accessed | tf_op | source)
XLA Modules:
  0.0 184.6 jit_solution(5719712683515491083)
XLA Ops:
  7.2 0.8 reduce
  8.0 1.6 gather_fusion
  9.6 0.3 convolution_convert_fusion.5
  9.9 0.6 copy.39
  10.5 7.3 %all-to-all-start = ((bf16[8,16,128]{2,1,0:T(8,128)(2,1)}), bf16[8,16,128]{2,1,0:T(8,128)(2,1)S(1)}, u32[]{:S(2)}, u32[]{:S(2)}) async-start(bf16[8,16,128]{2,1,0:T(8,128)(2,1)} %copy.39), calls=%async_computation | async-start | bytes 65536 | tf_op jit(solution)/shard_map/all_to_all | solution.py:41
  17.8 0.9 scatter_custom_fusion
  18.8 5.7 %all-to-all-done = bf16[8,16,128]{2,1,0:T(8,128)(2,1)S(1)} async-done(((bf16[8,16,128]{2,1,0:T(8,128)(2,1)}), bf16[8,16,128]{2,1,0:T(8,128)(2,1)S(1)}, u32[]{:S(2)}, u32[]{:S(2)}) %all-to-all-start) | async-done | bytes 32800 | tf_op jit(solution)/shard_map/all_to_all | solution.py:41
  24.4 0.2 fusion.34
  24.7 0.9 scatter_custom_fusion.1
  25.5 0.1 copy.42
  25.7 0.3 fusion.1
  26.0 0.1 copy.43
  26.1 0.7 gather_fusion.1
  26.8 0.3 convolution_convert_fusion.4
  27.1 0.6 copy.46
  27.7 3.5 %all-to-all-start.1 = ((bf16[8,16,128]{2,1,0:T(8,128)(2,1)}), bf16[8,16,128]{2,1,0:T(8,128)(2,1)S(1)}, u32[]{:S(2)}, u32[]{:S(2)}) async-start(bf16[8,16,128]{2,1,0:T(8,128)(2,1)} %copy.46), calls=%async_computation.1 | async-start | bytes 65536 | tf_op jit(solution)/shard_map/all_to_all | solution.py:41
  31.2 6.6 %all-to-all-done.1 = bf16[8,16,128]{2,1,0:T(8,128)(2,1)S(1)} async-done(((bf16[8,16,128]{2,1,0:T(8,128)(2,1)}), bf16[8,16,128]{2,1,0:T(8,128)(2,1)S(1)}, u32[]{:S(2)}, u32[]{:S(2)}) %all-to-all-start.1) | async-done | bytes 32800 | tf_op jit(solution)/shard_map/all_to_all | solution.py:41
  37.8 0.2 fusion.31
  38.0 0.9 scatter_custom_fusion.2
  38.9 0.1 copy.49
  39.1 0.7 copy-done.4
  39.8 0.2 convolution_bitcast_fusion
  39.9 1.7 scatter_custom_fusion.3
  41.6 22.4 %reduce-scatter.2.cloned.1.call-done = f32[512,128]{1,0:T(8,128)} async-done(((f32[2048,128]{1,0:T(8,128)}), f32[512,128]{1,0:T(8,128)}) %reduce-scatter.2.cloned.1.call-update) | async-done | bytes 262160 | tf_op jit(solution)/shard_map/reduce_scatter | solution.py:70
  64.0 40.6 %all-reduce.2 = bf16[512,128]{1,0:T(8,128)(2,1)S(1)} all-reduce(f32[512,128]{1,0:T(8,128)} %reduce-scatter.2.cloned.1.call-done), channel_id=1, replica_groups=mesh['sub'=8,'grp'=4] {'sub'}, use_global_device_ids=true, to_apply=%region_7.0 | all-reduce | flops 65536 | bytes 393216 | tf_op jit(solution)/shard_map/psum | solution.py:71
  104.6 6.6 %all_gather.3 = bf16[2048,128]{1,0:T(8,128)(2,1)S(1)} all-gather(bf16[512,128]{1,0:T(8,128)(2,1)S(1)} %all-reduce.2), channel_id=1, replica_groups=mesh['sub'=8,'grp'=4] {'grp'}, dimensions={0}, use_global_device_ids=true | all-gather | bytes 655360 | tf_op jit(solution)/shard_map/all_gather | solution.py:74
  111.2 0.4 fusion.4
  111.7 0.6 copy-done.2
  112.3 0.3 fusion.3
  112.7 0.7 gather_fusion.2
  113.4 0.3 convolution_convert_fusion.3
  113.7 9.1 %all_to_all.20 = bf16[8,16,128]{2,1,0:T(8,128)(2,1)S(1)} all-to-all(bf16[8,16,128]{2,1,0:T(8,128)(2,1)S(1)} %copy.53), channel_id=1, replica_groups=mesh['sub'=8,'grp'=4] {'sub'}, dimensions={0} | all-to-all | bytes 65536 | tf_op jit(solution)/shard_map/all_to_all | solution.py:41
  122.8 0.2 fusion.28
  123.0 0.9 scatter_custom_fusion.4
  123.8 0.1 copy.56
  124.0 0.2 multiply_reduce_fusion
  124.1 38.1 %all-reduce = (f32[128]{0:T(128)S(1)}, f32[128]{0:T(128)S(1)}) all-reduce(f32[128]{0:T(128)S(1)} %get-tuple-element.9, f32[128]{0:T(128)S(1)} %get-tuple-element.8), channel_id=1, replica_groups=mesh['sub'=8,'grp'=4] {'sub','grp'}, use_global_device_ids=true, to_apply=%region_4.0 | all-reduce | flops 256 | bytes 2048 | tf_op jit(solution)/shard_map/psum | solution.py:60
  162.3 0.3 fusion.2
  162.7 0.7 gather_fusion.3
  163.4 0.3 convolution_convert_fusion.2
  163.7 0.6 copy.60
  164.3 4.7 %all-to-all-start.3 = ((bf16[8,16,128]{2,1,0:T(8,128)(2,1)}), bf16[8,16,128]{2,1,0:T(8,128)(2,1)S(1)}, u32[]{:S(2)}, u32[]{:S(2)}) async-start(bf16[8,16,128]{2,1,0:T(8,128)(2,1)} %copy.60), calls=%async_computation.4 | async-start | bytes 65536 | tf_op jit(solution)/shard_map/all_to_all | solution.py:41
  169.1 0.8 copy.64
  169.9 5.8 %all-to-all-done.3 = bf16[8,16,128]{2,1,0:T(8,128)(2,1)S(1)} async-done(((bf16[8,16,128]{2,1,0:T(8,128)(2,1)}), bf16[8,16,128]{2,1,0:T(8,128)(2,1)S(1)}, u32[]{:S(2)}, u32[]{:S(2)}) %all-to-all-start.3) | async-done | bytes 32800 | tf_op jit(solution)/shard_map/all_to_all | solution.py:41
  175.7 0.2 fusion.25
  175.9 0.9 scatter_custom_fusion.5
  176.8 0.1 copy.63
  176.9 0.8 copy.65
  (32 shorter events, 0.7 us)
Async XLA Ops:
  7.2 18.5 %copy-start = (bf16[1,1,512,512]{3,2,1,0:T(8,128)(2,1)S(1)}, bf16[1,1,512,512]{3,2,1,0:T(8,128)(2,1)}, u32[]{:S(2)}) copy-start(bf16[1,1,512,512]{3,2,1,0:T(8,128)(2,1)} %param.9) | copy-start | bytes 1572868
  8.0 1.6 copy-start.5
  9.6 9.1 %copy-start.1 = (bf16[1,1,512,128]{3,2,1,0:T(8,128)(2,1)S(1)}, bf16[1,1,512,128]{3,2,1,0:T(8,128)(2,1)}, u32[]{:S(2)}) copy-start(bf16[1,1,512,128]{3,2,1,0:T(8,128)(2,1)} %param.10) | copy-start | bytes 393220
  10.5 13.9 %all-to-all-start = ((bf16[8,16,128]{2,1,0:T(8,128)(2,1)}), bf16[8,16,128]{2,1,0:T(8,128)(2,1)S(1)}, u32[]{:S(2)}, u32[]{:S(2)}) async-start(bf16[8,16,128]{2,1,0:T(8,128)(2,1)} %copy.39), calls=%async_computation | async-start | bytes 65536 | tf_op jit(solution)/shard_map/all_to_all | solution.py:41
  27.7 3.5 %copy-start.6 = (s32[1,1,24]{2,1,0:T(1,128)S(1)}, s32[1,1,24]{2,1,0:T(1,128)}, u32[]{:S(2)}) copy-start(s32[1,1,24]{2,1,0:T(1,128)} %param.15) | copy-start | bytes 292
  27.7 10.1 %all-to-all-start.1 = ((bf16[8,16,128]{2,1,0:T(8,128)(2,1)}), bf16[8,16,128]{2,1,0:T(8,128)(2,1)S(1)}, u32[]{:S(2)}, u32[]{:S(2)}) async-start(bf16[8,16,128]{2,1,0:T(8,128)(2,1)} %copy.46), calls=%async_computation.1 | async-start | bytes 65536 | tf_op jit(solution)/shard_map/all_to_all | solution.py:41
  31.2 32.8 %reduce-scatter.2.cloned.1.call-start = ((), (), s32[]{:S(2)}) async-start(), calls=%async_computation.5 | async-start | bytes 1310720 | tf_op jit(solution)/shard_map/reduce_scatter | solution.py:70
  39.0 0.7 copy-start.4
  104.6 6.7 %copy-start.3 = (bf16[1,1,24,2048]{3,2,1,0:T(8,128)(2,1)S(1)}, bf16[1,1,24,2048]{3,2,1,0:T(8,128)(2,1)}, u32[]{:S(2)}) copy-start(bf16[1,1,24,2048]{3,2,1,0:T(8,128)(2,1)} %param.12) | copy-start | bytes 294916
  111.2 1.0 copy-start.2
  164.3 11.4 %all-to-all-start.3 = ((bf16[8,16,128]{2,1,0:T(8,128)(2,1)}), bf16[8,16,128]{2,1,0:T(8,128)(2,1)S(1)}, u32[]{:S(2)}, u32[]{:S(2)}) async-start(bf16[8,16,128]{2,1,0:T(8,128)(2,1)} %copy.60), calls=%async_computation.4 | async-start | bytes 65536 | tf_op jit(solution)/shard_map/all_to_all | solution.py:41
Sparse Core Ops, SparseCore 0:
  41.7 22.2 reduce-scatter.1
where the time goes:
time: 185 us
  blocking collectives  94.4 us (51%)
  waiting for transfers between devices  40.4 us (22%)
  local copies, waits for them, and re-layouts  15.6 us (8%)
  starting transfers between devices  15.5 us (8%)
  between operations  14.3 us (8%)
  matrix products  3.3 us (2%)
    psum x1, blocking collectives, body(): panel_half = lax.psum(partial_rows, 'sub').astype(jnp.bfloat16)  40.6 us
    psum x1, blocking collectives, column_dot(): lax.psum(jnp.sum(weight * first_field * second_field, axis=0), ('sub', 'g...  38.1 us
    reduce_scatter x1, waiting for transfers between devices, body(): lax.psum_scatter(dense_sum, 'grp', scatter_dimension=0, tiled=True)  22.4 us
    all_to_all x3, waiting for transfers between devices, jump_field(): lax.all_to_all(outgoing, 'sub', split_axis=0, concat_axis=0, tiled=True)  18 us
    all_to_all x3, starting transfers between devices, jump_field(): lax.all_to_all(outgoing, 'sub', split_axis=0, concat_axis=0, tiled=True)  15.4 us
    all_to_all x1, blocking collectives, jump_field(): lax.all_to_all(outgoing, 'sub', split_axis=0, concat_axis=0, tiled=True)  9.06 us
    all_gather x1, blocking collectives, body(): lax.all_gather(panel_half, 'grp', axis=0, tiled=True)  6.64 us
    scatter x8, local copies, waits for them, and re-layouts, jump_field(): placed = jnp.zeros((order_size, column_count), jnp.float32).at[flat_rows]...  4 us
  transfers between devices with their start and end apart: 4, of which 4 were waited for; matrix products, arithmetic and copies ran while one was open for 1% of the time, Pallas kernels for 0%

commit v1 on v0

--- a/solution.py
+++ b/solution.py
@@ -1,10 +1,411 @@
+import functools
+
 import jax
 import jax.numpy as jnp
 from jax import lax
+from jax.experimental import pallas as pl
+from jax.experimental.pallas import tpu as pltpu
 from jax.sharding import PartitionSpec as P
 
-
-def body(
+F32 = jnp.float32
+BF16 = jnp.bfloat16
+VMEM_BYTES = 24 * 1024 * 1024
+
+
+def round_up(value, unit):
+    return -(-value // unit) * unit
+
+
+class Plan:
+    def __init__(self, line, groups, order, columns, corners, coarse, neighbors, each):
+        self.line, self.groups = line, groups
+        self.order, self.columns = order, columns
+        self.corners, self.coarse = corners, coarse
+        self.neighbors, self.each = neighbors, each
+        self.pairs = (line - 1) * each
+        self.wide = round_up(self.pairs, 128)
+        self.image_at = self.pairs
+        self.schur_at = 2 * self.pairs
+        self.coarse_at = 3 * self.pairs
+        self.tail = round_up(3 * corners + 8, 16)
+        self.first = self.coarse_at + self.tail
+        self.input_at = groups * corners
+        self.dots_at = self.input_at + corners
+        self.second = round_up(self.dots_at + 8, 16)
+        self.own_at = self.pairs
+        self.sums_at = self.pairs + each
+        self.third = self.sums_at + 16
+        self.spread = round_up(corners, 32)
+
+    def served(self):
+        return (
+            self.line * self.pairs <= self.coarse
+            and self.each % 16 == 0
+            and self.columns == 128
+            and self.wide == 128
+            and self.corners % 8 == 0
+            and 128 % self.spread == 0
+            and (self.line * self.spread) % 128 == 0
+            and self.order % 128 == 0
+            and self.coarse % 128 == 0
+            and self.coarse <= 128 * 256
+        )
+
+    @staticmethod
+    def slot(s, t):
+        return t - (1 if t > s else 0)
+
+    @staticmethod
+    def moving_slot(s, t):
+        return t - jnp.where(t > s, 1, 0).astype(jnp.int32)
+
+    def shift(self, index, step):
+        if self.groups & (self.groups - 1) == 0:
+            return index ^ step
+        return (index + step) % self.groups
+
+    def back(self, step):
+        if self.groups & (self.groups - 1) == 0:
+            return step
+        return (-step) % self.groups
+
+
+def dot(a, b):
+    return jnp.dot(a, b, preferred_element_type=F32)
+
+
+def split(value):
+    high = value.astype(BF16).astype(F32)
+    return high, value - high
+
+
+def whole_weight(place):
+    ones = jnp.ones((place.shape[1], 128), BF16)
+    return 1.0 - 0.5 * dot(place, ones)
+
+
+def prepare_kernel(plan, neighbors, rows, corner_map, schur, loads, coupling_t, message, place, rows_pad, map_pad):
+    me = lax.axis_index("sub")
+    each, pairs, wide, corners = plan.each, plan.pairs, plan.wide, plan.corners
+    rows_pad[...] = jnp.full(rows_pad.shape, -1, jnp.int32)
+    rows_pad[0 : plan.neighbors, 0:each] = rows[...]
+    index = jnp.full((1, wide), -1, jnp.int32)
+    for k in range(plan.neighbors):
+        at = each * plan.moving_slot(me, neighbors[0, k])
+        index = jnp.maximum(index, pltpu.roll(rows_pad[k : k + 1, :], at, 1))
+    wide_index = jnp.broadcast_to(index.astype(F32), (wide, wide))
+    tall_index = wide_index.T.astype(jnp.int32)
+    order_rows = lax.broadcasted_iota(jnp.int32, (plan.order, wide), 0)
+    place_f = jnp.where(order_rows == index, 1.0, 0.0)
+    place_v = place_f.astype(BF16)
+    place[...] = place_v
+    lane = lax.broadcasted_iota(jnp.int32, (wide, plan.order), 1)
+    pick_f = jnp.where(lane == tall_index[:, 0:1], 1.0, 0.0)
+    weight_row = 1.0 - 0.5 * jnp.sum(pick_f, axis=0, keepdims=True)
+    pick = pick_f.astype(BF16)
+    weight = whole_weight(place_v)
+    load = loads[...]
+    weighted = (weight * load.astype(F32)).astype(BF16)
+    image = dot(schur[...], jnp.concatenate([weighted, place_v], axis=1)).astype(BF16)
+    couple = coupling_t[...]
+    couple_w = (couple.astype(F32) * weight_row).astype(BF16)
+    first = dot(pick, image)
+    first_c = dot(couple_w, image)
+    picked = dot(pick, load)
+    edge = dot(couple, place_v)
+    map_pad[...] = jnp.zeros(map_pad.shape, F32)
+    corner_ids = corner_map[...]
+    map_pad[0:1, 0:corners] = (corner_ids // 128).astype(F32)
+    map_pad[1:2, 0:corners] = (corner_ids % 128).astype(F32)
+    tail = [first_c[:, :128], 0.5 * first_c[:, 128:], 0.5 * edge, map_pad[...]]
+    if plan.tail > 3 * corners + 8:
+        tail.append(jnp.zeros((plan.tail - 3 * corners - 8, 128), F32))
+    tail = jnp.concatenate(tail, axis=0).astype(BF16)
+    loads_part = picked[:pairs].astype(BF16)
+    image_part = first[:pairs, :128].astype(BF16)
+    schur_part = (0.5 * first[:pairs, 128:]).astype(BF16)
+    for d in range(plan.line):
+        message[d, 0:pairs, :] = loads_part
+        message[d, plan.image_at : plan.image_at + pairs, :] = image_part
+        message[d, plan.schur_at : plan.schur_at + pairs, :] = schur_part
+        message[d, plan.coarse_at : plan.coarse_at + plan.tail, :] = tail
+
+
+def direction_kernel(plan, *refs):
+    received, schur, flexibility, loads, place = refs[:5]
+    coarse_refs = refs[5 : 5 + plan.groups]
+    message, residual, direction, local_part, far_image = refs[5 + plan.groups : 10 + plan.groups]
+    moved, images, moved_images, inputs = refs[10 + plan.groups :]
+    me = lax.axis_index("sub")
+    line, each, pairs, corners = plan.line, plan.each, plan.pairs, plan.corners
+    zero_rows = plan.wide - pairs
+    codes = []
+    per_tile = 128 // plan.spread
+    lane = lax.broadcasted_iota(jnp.int32, (8, 128), 1)
+    for first in range(0, line, per_tile):
+        code = jnp.full((1, 128), -1, jnp.int32)
+        for u in range(first, first + per_tile):
+            tail = received[u, plan.coarse_at : plan.coarse_at + plan.tail, :].astype(F32)
+            pair_of_rows = tail[3 * corners : 3 * corners + 8]
+            number = (128.0 * pair_of_rows[0:1] + pair_of_rows[1:2]).astype(jnp.int32)
+            number = jnp.where(lane[0:1] < corners, number, -1)
+            code = jnp.maximum(code, pltpu.roll(number, (u - first) * plan.spread, 1))
+        codes.append(code)
+    codes = jnp.concatenate(codes, axis=1)
+    coarse_rows = lax.broadcasted_iota(jnp.int32, (plan.coarse, codes.shape[1]), 0)
+    chooser = jnp.where(coarse_rows == codes, 1.0, 0.0).astype(BF16)
+    coarse_all = jnp.concatenate([ref[...] for ref in coarse_refs], axis=0)
+    coarse_matrix = dot(coarse_all, chooser).astype(BF16)
+
+    tails = []
+    for t in range(line):
+        for d in range(line):
+            if d == t:
+                continue
+            source, target = each * plan.slot(d, t), each * plan.slot(t, d)
+            moved[t, target : target + each, :] = received[d, source : source + each, :]
+        if zero_rows:
+            moved[t, pairs:, :] = jnp.zeros((zero_rows, 128), BF16)
+        result = dot(received[t, plan.schur_at :, :], moved[t])
+        image = received[t, plan.image_at : plan.image_at + pairs, :].astype(F32) - result[:pairs]
+        images[t] = image
+        tails.append(result[pairs + corners : pairs + 2 * corners])
+    for t in range(line):
+        for d in range(line):
+            if d == t:
+                continue
+            source, target = each * plan.slot(d, t), each * plan.slot(t, d)
+            moved_images[t, target : target + each, :] = images[d, source : source + each, :]
+        if zero_rows:
+            moved_images[t, pairs:, :] = jnp.zeros((zero_rows, 128), F32)
+        tail = received[t, plan.coarse_at :, :]
+        edge = dot(tail, moved_images[t].astype(BF16))
+        entry = tail.astype(F32)[:corners] - tails[t] - edge[2 * corners : 3 * corners]
+        parts = [entry]
+        if plan.spread > corners:
+            parts.append(jnp.zeros((plan.spread - corners, 128), F32))
+        inputs[t] = jnp.concatenate(parts, axis=0)
+    coarse_in = inputs[...].reshape(line * plan.spread, 128).astype(BF16)
+    coarse_out = dot(coarse_matrix, coarse_in)
+
+    place_v = place[...]
+    weight = whole_weight(place_v)
+    right = loads[...].astype(F32) - dot(place_v, moved[me])
+    image = dot(schur[...], (weight * right).astype(BF16)).astype(BF16)
+    mine = moved_images[me]
+    far_image[...] = mine
+    field = weight * (image.astype(F32) - dot(place_v, mine.astype(BF16)))
+    residual[...] = right
+    direction[...] = field
+    local = dot(flexibility[...], field.astype(BF16))
+    local_part[...] = local
+    inner_high, inner_low = split(jnp.sum(weight * right * field, axis=0, keepdims=True))
+    square_high, square_low = split(jnp.sum(field * local, axis=0, keepdims=True))
+    row = lax.broadcasted_iota(jnp.int32, (8, 128), 0)
+    dots = jnp.zeros((8, 128), F32)
+    for at, value in enumerate((inner_high, inner_low, square_high, square_low)):
+        dots = jnp.where(row == at, value, dots)
+    parts = [coarse_out, inputs[me][:corners], dots]
+    if plan.second > plan.dots_at + 8:
+        parts.append(jnp.zeros((plan.second - plan.dots_at - 8, 128), F32))
+    message[...] = jnp.concatenate(parts, axis=0).astype(BF16)
+
+
+def surface_kernel(plan, *refs):
+    groups, corners, each, pairs = plan.groups, plan.corners, plan.each, plan.pairs
+    heard = [ref[...].astype(F32) for ref in refs[:groups]]
+    schur, coupling_t, place, local_part = refs[groups : groups + 4]
+    message, surface = refs[groups + 4 : groups + 6]
+    (image_rows,) = refs[groups + 6 :]
+    me = lax.axis_index("sub")
+    dots = sum(block[plan.dots_at : plan.dots_at + 8] for block in heard)
+    inner = dots[0:1] + dots[1:2]
+    square = dots[2:3] + dots[3:4]
+    own = None
+    for m in range(groups):
+        value = 0.0
+        for d in range(groups):
+            at = corners * plan.shift(m, d)
+            value = value + heard[d][at : at + corners]
+        value = value.astype(BF16)
+        if m == 0:
+            own = value
+        entry = heard[plan.back(m)][plan.input_at : plan.input_at + corners]
+        square = square + jnp.sum(entry * value.astype(F32), axis=0, keepdims=True)
+    lifted = lax.dot_general(
+        coupling_t[...], own, (((0,), (0,)), ((), ())), preferred_element_type=F32
+    )
+    field = (local_part[...] + lifted).astype(BF16)
+    surface[...] = field
+    place_v = place[...]
+    weight = whole_weight(place_v)
+    scaled = (weight * field.astype(F32)).astype(BF16)
+    image = dot(schur[...], scaled).astype(BF16)
+    both = lax.dot_general(
+        place_v,
+        jnp.concatenate([field, image], axis=1),
+        (((0,), (0,)), ((), ())),
+        preferred_element_type=F32,
+    )[:pairs]
+    surface_part = both[:, :128].astype(BF16)
+    image_rows[...] = both[:, 128:].reshape(plan.line - 1, each, 128)
+    inner_high, inner_low = split(inner)
+    square_high, square_low = split(square)
+    row = lax.broadcasted_iota(jnp.int32, (16, 128), 0)
+    sums = jnp.zeros((16, 128), F32)
+    for at, value in enumerate((inner_high, inner_low, square_high, square_low)):
+        sums = jnp.where(row == at, value, sums)
+    sums = sums.astype(BF16)
+    for d in range(plan.line):
+        at = jnp.minimum(plan.moving_slot(me, d), plan.line - 2)
+        message[d, 0:pairs, :] = surface_part
+        message[d, plan.own_at : plan.own_at + each, :] = image_rows[at].astype(BF16)
+        message[d, plan.sums_at :, :] = sums
+
+
+def result_kernel(
+    plan,
+    received,
+    first,
+    far_image,
+    residual,
+    direction,
+    surface,
+    schur,
+    place,
+    solution_out,
+    preconditioned,
+    moved,
+    far_rows,
+):
+    me = lax.axis_index("sub")
+    line, each, pairs = plan.line, plan.each, plan.pairs
+    zero_rows = plan.wide - pairs
+    sums = 0.0
+    for u in range(line):
+        sums = sums + received[u, plan.sums_at : plan.sums_at + 16, :].astype(F32)
+    step = (sums[0:1] + sums[1:2]) / (sums[2:3] + sums[3:4])
+    far_rows[...] = jnp.zeros(far_rows.shape, F32)
+    for t in range(line):
+        for d in range(line):
+            if d == t:
+                continue
+            source, target = each * plan.slot(d, t), each * plan.slot(t, d)
+            moved[t, target : target + each, :] = received[d, source : source + each, :]
+        if zero_rows:
+            moved[t, pairs:, :] = jnp.zeros((zero_rows, 128), BF16)
+    for t in range(line):
+        at = jnp.minimum(plan.moving_slot(t, me), line - 2)
+        block = first[t, pl.ds(pl.multiple_of(plan.schur_at + each * at, 16), each), :]
+        change = received[t, plan.own_at : plan.own_at + each, :].astype(F32) - dot(block, moved[t])
+        there = jnp.where(me == t, line - 1, plan.moving_slot(me, t))
+        far_rows[there] = change
+    far = far_image[...] - step * far_rows[...].reshape(line * each, 128)[: plan.wide]
+    place_v = place[...]
+    weight = whole_weight(place_v)
+    operated = surface[...].astype(F32) - dot(place_v, moved[me])
+    remaining = residual[...] - step * operated
+    image = dot(schur[...], (weight * remaining).astype(BF16)).astype(BF16)
+    row = lax.broadcasted_iota(jnp.int32, far.shape, 0)
+    far = jnp.where(row < pairs, far, 0.0).astype(BF16)
+    preconditioned[...] = weight * (image.astype(F32) - dot(place_v, far))
+    solution_out[...] = step * direction[...]
+
+
+def line_body(
+    plan,
+    flexibility,
+    dirichlet_schur,
+    subdomain_loads,
+    coupling,
+    coarse_rows,
+    neighbors,
+    interface_rows,
+    coarse_map,
+):
+    line, order = plan.line, plan.order
+    flex, schur, loads = flexibility[0, 0], dirichlet_schur[0, 0], subdomain_loads[0, 0]
+    coupling_t = coupling[0, 0].T
+    coarse = coarse_rows[0, 0]
+    whole = pl.BlockSpec(memory_space=pltpu.VMEM)
+    params = pltpu.CompilerParams(vmem_limit_bytes=VMEM_BYTES)
+
+    def shape(*dims, kind=F32):
+        return jax.ShapeDtypeStruct(dims, kind)
+
+    def turn(value, step):
+        pairs = [(g, plan.shift(g, step)) for g in range(plan.groups)]
+        return lax.ppermute(value, "grp", pairs)
+
+    coarse_all = [coarse]
+    for step in range(1, plan.groups):
+        coarse_all.append(turn(coarse, plan.back(step)))
+
+    message, place = pl.pallas_call(
+        functools.partial(prepare_kernel, plan),
+        out_shape=(shape(line, plan.first, 128, kind=BF16), shape(order, plan.wide, kind=BF16)),
+        in_specs=[pl.BlockSpec(memory_space=pltpu.SMEM)] + [whole] * 5,
+        out_specs=(whole, whole),
+        scratch_shapes=[
+            pltpu.VMEM((round_up(plan.neighbors, 8), 128), jnp.int32),
+            pltpu.VMEM((8, 128), F32),
+        ],
+        compiler_params=params,
+        name="prepare",
+    )(neighbors[0], interface_rows[0, 0], coarse_map[0], schur, loads, coupling_t)
+    first = lax.all_to_all(message, "sub", split_axis=0, concat_axis=0, tiled=True)
+
+    message, residual, direction, local_part, far_image = pl.pallas_call(
+        functools.partial(direction_kernel, plan),
+        out_shape=(
+            shape(plan.second, 128, kind=BF16),
+            shape(order, 128),
+            shape(order, 128),
+            shape(order, 128),
+            shape(plan.wide, 128),
+        ),
+        in_specs=[whole] * (5 + plan.groups),
+        out_specs=(whole,) * 5,
+        scratch_shapes=[
+            pltpu.VMEM((line, plan.wide, 128), BF16),
+            pltpu.VMEM((line, plan.pairs, 128), F32),
+            pltpu.VMEM((line, plan.wide, 128), F32),
+            pltpu.VMEM((line, plan.spread, 128), F32),
+        ],
+        compiler_params=params,
+        name="direction",
+    )(first, schur, flex, loads, place, *coarse_all)
+    heard = [message]
+    for step in range(1, plan.groups):
+        heard.append(turn(message, step))
+
+    message, surface = pl.pallas_call(
+        functools.partial(surface_kernel, plan),
+        out_shape=(shape(line, plan.third, 128, kind=BF16), shape(order, 128, kind=BF16)),
+        in_specs=[whole] * (plan.groups + 4),
+        out_specs=(whole, whole),
+        scratch_shapes=[pltpu.VMEM((line - 1, plan.each, 128), F32)],
+        compiler_params=params,
+        name="surface",
+    )(*heard, schur, coupling_t, place, local_part)
+    last = lax.all_to_all(message, "sub", split_axis=0, concat_axis=0, tiled=True)
+
+    solved, preconditioned = pl.pallas_call(
+        functools.partial(result_kernel, plan),
+        out_shape=(shape(order, 128), shape(order, 128)),
+        in_specs=[whole] * 8,
+        out_specs=(whole, whole),
+        scratch_shapes=[
+            pltpu.VMEM((line, plan.wide, 128), BF16),
+            pltpu.VMEM((line, plan.each, 128), F32),
+        ],
+        compiler_params=params,
+        name="result",
+    )(last, first, far_image, residual, direction, surface, schur, place)
+    return solved[None, None], preconditioned[None, None]
+
+
+def wide_body(
     flexibility,
     dirichlet_schur,
     subdomain_loads,
@@ -85,6 +486,23 @@
     return (solution[None, None], zfield[None, None])
 
 
+def body(*arrays):
+    flexibility, _, loads, _, coarse_rows, neighbors, interface_rows, _ = arrays
+    plan = Plan(
+        line=lax.axis_size("sub"),
+        groups=lax.axis_size("grp"),
+        order=flexibility.shape[2],
+        columns=loads.shape[3],
+        corners=coarse_rows.shape[2],
+        coarse=coarse_rows.shape[3],
+        neighbors=neighbors.shape[2],
+        each=interface_rows.shape[3],
+    )
+    if plan.served():
+        return line_body(plan, *arrays)
+    return wide_body(*arrays)
+
+
 def solution(mesh):
     placed = (
         P("sub", "grp", None, None),

time: 185 us -> 58.3 us (0.32)
  blocking collectives: 94.4 us -> 14.2 us
  waiting for transfers between devices: 40.4 us -> 21.9 us
  between operations: 14.3 us -> 0.68 us
  local copies, waits for them, and re-layouts: 15.6 us -> 4.06 us
  Pallas kernels: 0 us -> 5.88 us
  starting transfers between devices: 15.5 us -> 11.2 us
  matrix products: 3.3 us -> 0 us
    psum x2 -> x0, blocking collectives: 78.7 us -> none  [the longest x1 40.6 us: body(): panel_half = lax.psum(partial_rows, 'sub').astype(jnp.bfloat16)]
    reduce_scatter x1 -> x0, waiting for transfers between devices: 22.4 us -> none  [body(): lax.psum_scatter(dense_sum, 'grp', scatter_dimension=0, tiled=True)]
    all_to_all x3 -> x1, starting transfers between devices: 15.4 us -> 7.4 us  [line_body(): lax.all_to_all(message, 'sub', split_axis=0, concat_axis=0, tiled=True)]
    ppermute x0 -> x6, waiting for transfers between devices: none -> 7.52 us  [turn(): return lax.ppermute(value, 'grp', pairs)]
    all_gather x1 -> x0, blocking collectives: 6.64 us -> none  [body(): lax.all_gather(panel_half, 'grp', axis=0, tiled=True)]
    scatter x10 -> x0, local copies, waits for them, and re-layouts: 6.54 us -> none  [the longest x8 4 us: jump_field(): placed = jnp.zeros((order_size, column_count), jnp.float32).at[flat_rows]...]
    pallas_call x0 -> x4, Pallas kernels: none -> 5.88 us  [the longest x1 2.39 us: line_body(): pl.pallas_call(functools.partial(prepare_kernel, plan), out_shape=(shape(...]
    all_to_all x1, blocking collectives: 9.06 us -> 14.2 us  [line_body(): lax.all_to_all(message, 'sub', split_axis=0, concat_axis=0, tiled=True)]
  transfers between devices with their start and end apart: 4 -> 7, of which waited for: 4 -> 5; matrix products, arithmetic and copies ran while one was open for 1% -> 0% of each run, Pallas kernels for 0% -> 0%
where the time goes in v1:
time: 58.3 us; the launch traced here: 57.9 us
  waiting for transfers between devices  21.9 us (38%)
  blocking collectives  14.2 us (24%)
  starting transfers between devices  11.2 us (19%)
  Pallas kernels  5.88 us (10%)
  local copies, waits for them, and re-layouts  4.06 us (7%)
  between operations  0.68 us (1%)
    all_to_all x1, waiting for transfers between devices, line_body(): lax.all_to_all(message, 'sub', split_axis=0, concat_axis=0, tiled=True)  14.4 us
    all_to_all x1, blocking collectives, line_body(): lax.all_to_all(message, 'sub', split_axis=0, concat_axis=0, tiled=True)  14.2 us
    ppermute x6, waiting for transfers between devices, turn(): return lax.ppermute(value, 'grp', pairs)  7.52 us
    all_to_all x1, starting transfers between devices, line_body(): lax.all_to_all(message, 'sub', split_axis=0, concat_axis=0, tiled=True)  7.4 us
    unnamed x21, local copies, waits for them, and re-layouts  4.06 us
    ppermute x6, starting transfers between devices, turn(): return lax.ppermute(value, 'grp', pairs)  3.85 us
    pallas_call x1, Pallas kernels, line_body(): pl.pallas_call(functools.partial(prepare_kernel, plan), out_shape=(shape(...  2.39 us
    pallas_call x1, Pallas kernels, line_body(): pl.pallas_call(functools.partial(direction_kernel, plan), out_shape=(shap...  1.48 us
  transfers between devices with their start and end apart: 7, of which 5 were waited for; matrix products, arithmetic and copies ran while one was open for 0% of the time, Pallas kernels for 0%

profile of v1, /device:TPU:0, one launch (start us, length us, event | category | flops | bytes accessed | tf_op | source)
XLA Modules:
  0.0 57.9 jit_solution(580345352404579738)
XLA Ops:
  0.6 0.7 %copy.12 = s32[1,1,6,16]{3,2,1,0:T(8,128)S(1)} copy(s32[1,1,6,16]{3,1,2,0:T(1,128)} %param.14) | data formatting | bytes 768
  1.3 0.0 copy-start.8
  1.3 0.0 copy-start.9
  1.3 0.7 %copy-done.8 = s32[1,1,6]{2,1,0:T(1,128)S(1)} copy-done((s32[1,1,6]{2,1,0:T(1,128)S(1)}, s32[1,1,6]{2,1,0:T(1,128)}, u32[]{:S(2)}) %copy-start.8) | copy-done | bytes 48
  2.0 0.0 copy-done.9
  2.0 0.0 copy-start
  2.0 1.0 %copy-done = bf16[1,1,512,512]{3,2,1,0:T(8,128)(2,1)S(1)} copy-done((bf16[1,1,512,512]{3,2,1,0:T(8,128)(2,1)S(1)}, bf16[1,1,512,512]{3,2,1,0:T(8,128)(2,1)}, u32[]{:S(2)}) %copy-start) | copy-done | bytes 524312
  3.0 0.0 copy-start.3
  3.0 0.9 %copy-done.3 = bf16[1,1,512,128]{3,2,1,0:T(8,128)(2,1)S(1)} copy-done((bf16[1,1,512,128]{3,2,1,0:T(8,128)(2,1)S(1)}, bf16[1,1,512,128]{3,2,1,0:T(8,128)(2,1)}, u32[]{:S(2)}) %copy-start.3) | copy-done | bytes 131096
  3.9 0.0 copy-start.6
  3.9 0.7 %copy-done.6 = bf16[1,1,512,24]{2,3,1,0:T(8,128)(2,1)S(1)} copy-done((bf16[1,1,512,24]{2,3,1,0:T(8,128)(2,1)S(1)}, bf16[1,1,512,24]{2,3,1,0:T(8,128)(2,1)}, u32[]{:S(2)}) %copy-start.6) | copy-done | bytes 24600
  4.7 2.4 %prepare.1 = (bf16[8,416,128]{2,1,0:T(8,128)(2,1)}, bf16[512,128]{1,0:T(8,128)(2,1)S(1)}) custom-call(s32[1,6]{1,0:T(1,128)S(1)} %bitcast.28, s32[6,16]{1,0:T(8,128)S(1)} %bitcast.27, s32[1,24]{1,0:T(1,128)S(1)} %bitcast.29, bf16[512,512]{1,0:T(8,128)(2,1)S(1)} %bitcast.14, bf16[512,128]{1,0:T(8,128)(2,1)S(1)} %bitcast.19, bf16[24,512]{1,0:T(8,128)(2,1)S(1)} %bitcast.25), custom_call_target="tpu_custom_call" | custom-call | tf_op jit(solution)/shard_map/prepare/pallas_call | solution.py:344
  7.1 0.0 copy-start.5
  7.1 0.0 copy-start.1
  7.1 0.0 copy-start.2
  7.1 0.0 copy-start.4
  7.1 7.4 %all-to-all-start = ((bf16[8,416,128]{2,1,0:T(8,128)(2,1)}), bf16[8,416,128]{2,1,0:T(8,128)(2,1)S(1)}, u32[]{:S(2)}, u32[]{:S(2)}) async-start(bf16[8,416,128]{2,1,0:T(8,128)(2,1)} %get-tuple-element.13), calls=%async_computation | async-start | bytes 1703936 | tf_op jit(solution)/shard_map/all_to_all | solution.py:356
  14.5 0.0 copy-done.5
  14.5 0.7 %collective-permute-start.2 = (bf16[24,2048]{1,0:T(8,128)(2,1)S(1)}, bf16[24,2048]{1,0:T(8,128)(2,1)S(1)}, u32[]{:S(2)}, u32[]{:S(2)}) collective-permute-start(bf16[24,2048]{1,0:T(8,128)(2,1)S(1)} %bitcast.21), channel_id=1, source_target_pairs={{0,3},{1,2},{2,1},{3,0},{4,7},{5,6},{6,5},{7,4},{8,11},{9,10},{10,... | collective-permute-start | bytes 294920 | tf_op jit(solution)/shard_map/ppermute | solution.py:338
  15.2 0.9 %collective-permute-start.1 = (bf16[24,2048]{1,0:T(8,128)(2,1)S(1)}, bf16[24,2048]{1,0:T(8,128)(2,1)S(1)}, u32[]{:S(2)}, u32[]{:S(2)}) collective-permute-start(bf16[24,2048]{1,0:T(8,128)(2,1)S(1)} %bitcast.22), channel_id=1, source_target_pairs={{0,2},{1,3},{2,0},{3,1},{4,6},{5,7},{6,4},{7,5},{8,10},{9,11},{10,... | collective-permute-start | bytes 294920 | tf_op jit(solution)/shard_map/ppermute | solution.py:338
  16.1 0.3 collective-permute-start
  16.4 3.2 %collective-permute-done.2.refs_8_ = bf16[24,2048]{1,0:T(8,128)(2,1)S(1)} collective-permute-done((bf16[24,2048]{1,0:T(8,128)(2,1)S(1)}, bf16[24,2048]{1,0:T(8,128)(2,1)S(1)}, u32[]{:S(2)}, u32[]{:S(2)}) %collective-permute-start.2) | collective-permute-done | bytes 98336 | tf_op jit(solution)/shard_map/ppermute | solution.py:338
  19.6 2.2 %collective-permute-done.1.refs_7_ = bf16[24,2048]{1,0:T(8,128)(2,1)S(1)} collective-permute-done((bf16[24,2048]{1,0:T(8,128)(2,1)S(1)}, bf16[24,2048]{1,0:T(8,128)(2,1)S(1)}, u32[]{:S(2)}, u32[]{:S(2)}) %collective-permute-start.1) | collective-permute-done | bytes 98336 | tf_op jit(solution)/shard_map/ppermute | solution.py:338
  21.7 0.0 collective-permute-done.refs_6_
  21.7 14.4 %all-to-all-done.refs_0_.first = bf16[8,416,128]{2,1,0:T(8,128)(2,1)S(1)} async-done(((bf16[8,416,128]{2,1,0:T(8,128)(2,1)}), bf16[8,416,128]{2,1,0:T(8,128)(2,1)S(1)}, u32[]{:S(2)}, u32[]{:S(2)}) %all-to-all-start) | async-done | bytes 852000 | tf_op jit(solution)/shard_map/all_to_all | solution.py:356
  36.1 0.0 copy-done.1
  36.1 0.0 copy-done.2
  36.1 0.0 copy-done.4
  36.1 0.0 copy-start.7
  36.1 1.5 %direction.1 = (bf16[128,128]{1,0:T(8,128)(2,1)S(1)}, f32[512,128]{1,0:T(8,128)S(1)}, f32[512,128]{1,0:T(8,128)S(1)}, f32[512,128]{1,0:T(8,128)S(1)}, f32[128,128]{1,0:T(8,128)S(1)}) custom-call(bf16[8,416,128]{2,1,0:T(8,128)(2,1)S(1)} %all-to-all-done.refs_0_.first, bf16[512,512]{1,0:T(8,128)(2,1)S(1)} %bitcast.15, bf16[512,512]{1,0:T(8,128)(2,1)S(1)} %bitcast.18, ...), custom_call_target="tpu_custom_call" | custom-call | tf_op jit(solution)/shard_map/direction/pallas_call | solution.py:358
  37.6 0.1 collective-permute-start.5
  37.7 1.6 %collective-permute-start.4 = (bf16[128,128]{1,0:T(8,128)(2,1)S(1)}, bf16[128,128]{1,0:T(8,128)(2,1)S(1)}, u32[]{:S(2)}, u32[]{:S(2)}) collective-permute-start(bf16[128,128]{1,0:T(8,128)(2,1)S(1)} %get-tuple-element.15.refs_0_), channel_id=1, source_target_pairs={{0,2},{1,3},{2,0},{3,1},{4,6},{5,7},{6,4},{7,5},{8,10},{9,11},{10,... | collective-permute-start | bytes 98312 | tf_op jit(solution)/shard_map/ppermute | solution.py:338
  39.3 0.3 collective-permute-start.3
  39.5 1.8 %collective-permute-done.5.refs_3_ = bf16[128,128]{1,0:T(8,128)(2,1)S(1)} collective-permute-done((bf16[128,128]{1,0:T(8,128)(2,1)S(1)}, bf16[128,128]{1,0:T(8,128)(2,1)S(1)}, u32[]{:S(2)}, u32[]{:S(2)}) %collective-permute-start.5) | collective-permute-done | bytes 32800 | tf_op jit(solution)/shard_map/ppermute | solution.py:338
  41.3 0.4 collective-permute-done.4.refs_2_
  41.7 0.0 collective-permute-done.3.refs_1_
  41.7 0.0 copy-done.7
  41.7 0.7 %surface.1 = (bf16[8,144,128]{2,1,0:T(8,128)(2,1)S(1)}, bf16[512,128]{1,0:T(8,128)(2,1)S(1)}) custom-call(bf16[128,128]{1,0:T(8,128)(2,1)S(1)} %get-tuple-element.15.refs_0_, bf16[128,128]{1,0:T(8,128)(2,1)S(1)} %collective-permute-done.3.refs_1_, bf16[128,128]{1,0:T(8,128)(2,1)S(1)} %collective-permute-done.4.refs_2_, ...), custom_call_target="tpu_custom_call" | custom-call | tf_op jit(solution)/shard_map/surface/pallas_call | solution.py:382
  42.4 14.2 %all_to_all.10.received = bf16[8,144,128]{2,1,0:T(8,128)(2,1)S(1)} all-to-all(bf16[8,144,128]{2,1,0:T(8,128)(2,1)S(1)} %get-tuple-element.17), channel_id=1, replica_groups=mesh['sub'=8,'grp'=4] {'sub'}, dimensions={0} | all-to-all | bytes 589824 | tf_op jit(solution)/shard_map/all_to_all | solution.py:391
  56.6 1.3 %result.1 = (f32[512,128]{1,0:T(8,128)}, f32[512,128]{1,0:T(8,128)}) custom-call(bf16[8,144,128]{2,1,0:T(8,128)(2,1)S(1)} %all_to_all.10.received, bf16[8,416,128]{2,1,0:T(8,128)(2,1)S(1)} %all-to-all-done.refs_0_.first, f32[128,128]{1,0:T(8,128)S(1)} %get-tuple-element.18.far_image, f32[512,128]{1,0:T(8,128)S(1)} %get-tuple-element.19.residual, ...), custom_call_target="tpu_custom_call" | custom-call | tf_op jit(solution)/shard_map/result/pallas_call | solution.py:393
Async XLA Ops:
  1.3 0.7 %copy-start.8 = (s32[1,1,6]{2,1,0:T(1,128)S(1)}, s32[1,1,6]{2,1,0:T(1,128)}, u32[]{:S(2)}) copy-start(s32[1,1,6]{2,1,0:T(1,128)} %param.13) | copy-start | bytes 76
  1.3 0.7 %copy-start.9 = (s32[1,1,24]{2,1,0:T(1,128)S(1)}, s32[1,1,24]{2,1,0:T(1,128)}, u32[]{:S(2)}) copy-start(s32[1,1,24]{2,1,0:T(1,128)} %param.15) | copy-start | bytes 292
  2.0 1.0 %copy-start = (bf16[1,1,512,512]{3,2,1,0:T(8,128)(2,1)S(1)}, bf16[1,1,512,512]{3,2,1,0:T(8,128)(2,1)}, u32[]{:S(2)}) copy-start(bf16[1,1,512,512]{3,2,1,0:T(8,128)(2,1)} %param.9) | copy-start | bytes 1572868
  3.0 0.9 %copy-start.3 = (bf16[1,1,512,128]{3,2,1,0:T(8,128)(2,1)S(1)}, bf16[1,1,512,128]{3,2,1,0:T(8,128)(2,1)}, u32[]{:S(2)}) copy-start(bf16[1,1,512,128]{3,2,1,0:T(8,128)(2,1)} %param.10) | copy-start | bytes 393220
  3.9 0.7 %copy-start.6 = (bf16[1,1,512,24]{2,3,1,0:T(8,128)(2,1)S(1)}, bf16[1,1,512,24]{2,3,1,0:T(8,128)(2,1)}, u32[]{:S(2)}) copy-start(bf16[1,1,512,24]{2,3,1,0:T(8,128)(2,1)} %param.11) | copy-start | bytes 73732
  7.1 7.4 %copy-start.5 = (bf16[1,1,24,2048]{3,2,1,0:T(8,128)(2,1)S(1)}, bf16[1,1,24,2048]{3,2,1,0:T(8,128)(2,1)}, u32[]{:S(2)}) copy-start(bf16[1,1,24,2048]{3,2,1,0:T(8,128)(2,1)} %param.12) | copy-start | bytes 294916
  7.1 29.0 %copy-start.1 = (bf16[1,1,512,512]{3,2,1,0:T(8,128)(2,1)S(1)}, bf16[1,1,512,512]{3,2,1,0:T(8,128)(2,1)}, u32[]{:S(2)}) copy-start(bf16[1,1,512,512]{3,2,1,0:T(8,128)(2,1)} %param.9) | copy-start | bytes 1572868
  7.1 29.0 %copy-start.2 = (bf16[1,1,512,512]{3,2,1,0:T(8,128)(2,1)S(1)}, bf16[1,1,512,512]{3,2,1,0:T(8,128)(2,1)}, u32[]{:S(2)}) copy-start(bf16[1,1,512,512]{3,2,1,0:T(8,128)(2,1)} %param.8) | copy-start | bytes 1572868
  7.1 29.0 %copy-start.4 = (bf16[1,1,512,128]{3,2,1,0:T(8,128)(2,1)S(1)}, bf16[1,1,512,128]{3,2,1,0:T(8,128)(2,1)}, u32[]{:S(2)}) copy-start(bf16[1,1,512,128]{3,2,1,0:T(8,128)(2,1)} %param.10) | copy-start | bytes 393220
  7.1 29.0 %all-to-all-start = ((bf16[8,416,128]{2,1,0:T(8,128)(2,1)}), bf16[8,416,128]{2,1,0:T(8,128)(2,1)S(1)}, u32[]{:S(2)}, u32[]{:S(2)}) async-start(bf16[8,416,128]{2,1,0:T(8,128)(2,1)} %get-tuple-element.13), calls=%async_computation | async-start | bytes 1703936 | tf_op jit(solution)/shard_map/all_to_all | solution.py:356
  14.5 5.1 %collective-permute-start.2 = (bf16[24,2048]{1,0:T(8,128)(2,1)S(1)}, bf16[24,2048]{1,0:T(8,128)(2,1)S(1)}, u32[]{:S(2)}, u32[]{:S(2)}) collective-permute-start(bf16[24,2048]{1,0:T(8,128)(2,1)S(1)} %bitcast.21), channel_id=1, source_target_pairs={{0,3},{1,2},{2,1},{3,0},{4,7},{5,6},{6,5},{7,4},{8,11},{9,10},{10,... | collective-permute-start | bytes 294920 | tf_op jit(solution)/shard_map/ppermute | solution.py:338
  15.2 6.5 %collective-permute-start.1 = (bf16[24,2048]{1,0:T(8,128)(2,1)S(1)}, bf16[24,2048]{1,0:T(8,128)(2,1)S(1)}, u32[]{:S(2)}, u32[]{:S(2)}) collective-permute-start(bf16[24,2048]{1,0:T(8,128)(2,1)S(1)} %bitcast.22), channel_id=1, source_target_pairs={{0,2},{1,3},{2,0},{3,1},{4,6},{5,7},{6,4},{7,5},{8,10},{9,11},{10,... | collective-permute-start | bytes 294920 | tf_op jit(solution)/shard_map/ppermute | solution.py:338
  16.1 5.6 %collective-permute-start = (bf16[24,2048]{1,0:T(8,128)(2,1)S(1)}, bf16[24,2048]{1,0:T(8,128)(2,1)S(1)}, u32[]{:S(2)}, u32[]{:S(2)}) collective-permute-start(bf16[24,2048]{1,0:T(8,128)(2,1)S(1)} %bitcast.23), channel_id=1, source_target_pairs={{0,1},{1,0},{2,3},{3,2},{4,5},{5,4},{6,7},{7,6},{8,9},{9,8},{10,11... | collective-permute-start | bytes 294920 | tf_op jit(solution)/shard_map/ppermute | solution.py:338
  36.1 5.6 %copy-start.7 = (bf16[1,1,512,24]{2,3,1,0:T(8,128)(2,1)S(1)}, bf16[1,1,512,24]{2,3,1,0:T(8,128)(2,1)}, u32[]{:S(2)}) copy-start(bf16[1,1,512,24]{2,3,1,0:T(8,128)(2,1)} %param.11) | copy-start | bytes 73732
  37.6 3.7 %collective-permute-start.5 = (bf16[128,128]{1,0:T(8,128)(2,1)S(1)}, bf16[128,128]{1,0:T(8,128)(2,1)S(1)}, u32[]{:S(2)}, u32[]{:S(2)}) collective-permute-start(bf16[128,128]{1,0:T(8,128)(2,1)S(1)} %get-tuple-element.15.refs_0_), channel_id=1, source_target_pairs={{0,3},{1,2},{2,1},{3,0},{4,7},{5,6},{6,5},{7,4},{8,11},{9,10},{10,... | collective-permute-start | bytes 98312 | tf_op jit(solution)/shard_map/ppermute | solution.py:338
  37.7 4.0 %collective-permute-start.4 = (bf16[128,128]{1,0:T(8,128)(2,1)S(1)}, bf16[128,128]{1,0:T(8,128)(2,1)S(1)}, u32[]{:S(2)}, u32[]{:S(2)}) collective-permute-start(bf16[128,128]{1,0:T(8,128)(2,1)S(1)} %get-tuple-element.15.refs_0_), channel_id=1, source_target_pairs={{0,2},{1,3},{2,0},{3,1},{4,6},{5,7},{6,4},{7,5},{8,10},{9,11},{10,... | collective-permute-start | bytes 98312 | tf_op jit(solution)/shard_map/ppermute | solution.py:338
  39.3 2.4 %collective-permute-start.3 = (bf16[128,128]{1,0:T(8,128)(2,1)S(1)}, bf16[128,128]{1,0:T(8,128)(2,1)S(1)}, u32[]{:S(2)}, u32[]{:S(2)}) collective-permute-start(bf16[128,128]{1,0:T(8,128)(2,1)S(1)} %get-tuple-element.15.refs_0_), channel_id=1, source_target_pairs={{0,1},{1,0},{2,3},{3,2},{4,5},{5,4},{6,7},{7,6},{8,9},{9,8},{10,11... | collective-permute-start | bytes 98312 | tf_op jit(solution)/shard_map/ppermute | solution.py:338

commit v2 on v1

--- a/solution.py
+++ b/solution.py
@@ -32,14 +32,16 @@
         self.input_at = groups * corners
         self.dots_at = self.input_at + corners
         self.second = round_up(self.dots_at + 8, 16)
-        self.own_at = self.pairs
-        self.sums_at = self.pairs + each
+        self.sums_at = 2 * self.pairs
         self.third = self.sums_at + 16
         self.spread = round_up(corners, 32)
 
     def served(self):
         return (
             self.line * self.pairs <= self.coarse
+            and self.line >= 4
+            and self.line & (self.line - 1) == 0
+            and self.groups & (self.groups - 1) == 0
             and self.each % 16 == 0
             and self.columns == 128
             and self.wide == 128
@@ -51,23 +53,11 @@
             and self.coarse <= 128 * 256
         )
 
-    @staticmethod
-    def slot(s, t):
-        return t - (1 if t > s else 0)
-
-    @staticmethod
-    def moving_slot(s, t):
-        return t - jnp.where(t > s, 1, 0).astype(jnp.int32)
-
-    def shift(self, index, step):
-        if self.groups & (self.groups - 1) == 0:
-            return index ^ step
-        return (index + step) % self.groups
-
-    def back(self, step):
-        if self.groups & (self.groups - 1) == 0:
-            return step
-        return (-step) % self.groups
+    def slot(self, a, b):
+        return self.each * ((a ^ b) - 1)
+
+    def others(self, a):
+        return [b for b in range(self.line) if b != a]
 
 
 def dot(a, b):
@@ -84,60 +74,98 @@
     return 1.0 - 0.5 * dot(place, ones)
 
 
-def prepare_kernel(plan, neighbors, rows, corner_map, schur, loads, coupling_t, message, place, rows_pad, map_pad):
+def prepare_kernel(
+    plan,
+    neighbors_in,
+    rows_in,
+    corner_map_in,
+    schur_in,
+    loads_in,
+    coupling_in,
+    flexibility_in,
+    message,
+    place,
+    schur,
+    loads,
+    coupling_t,
+    flexibility,
+    neighbors,
+    rows,
+    corner_map,
+    rows_pad,
+    map_pad,
+    arrived,
+):
     me = lax.axis_index("sub")
     each, pairs, wide, corners = plan.each, plan.pairs, plan.wide, plan.corners
-    rows_pad[...] = jnp.full(rows_pad.shape, -1, jnp.int32)
-    rows_pad[0 : plan.neighbors, 0:each] = rows[...]
+    sources = (neighbors_in, rows_in, corner_map_in, loads_in, coupling_in, schur_in)
+    targets = (neighbors, rows, corner_map, loads, coupling_t, schur)
+    sources += (flexibility_in,)
+    targets += (flexibility,)
+    copies = [
+        pltpu.make_async_copy(source, target, arrived.at[at])
+        for at, (source, target) in enumerate(zip(sources, targets))
+    ]
+    for copy in copies:
+        copy.start()
+    rows_pad[...] = jnp.zeros(rows_pad.shape, jnp.int32)
+    map_pad[...] = jnp.zeros(map_pad.shape, F32)
+    copies[0].wait()
+    copies[1].wait()
+    for k in range(plan.neighbors):
+        rows_pad[k : k + 1, 0:each] = rows[k]
+    spread = rows_pad[...]
+    reach = each
+    while reach < wide:
+        spread = spread + pltpu.roll(spread, reach, 1)
+        reach *= 2
+    lane = lax.broadcasted_iota(jnp.int32, (1, wide), 1)
+    slots = neighbors[...] ^ me
     index = jnp.full((1, wide), -1, jnp.int32)
     for k in range(plan.neighbors):
-        at = each * plan.moving_slot(me, neighbors[0, k])
-        index = jnp.maximum(index, pltpu.roll(rows_pad[k : k + 1, :], at, 1))
+        index = jnp.where(lane // each + 1 == slots[0:1, k : k + 1], spread[k : k + 1], index)
     wide_index = jnp.broadcast_to(index.astype(F32), (wide, wide))
     tall_index = wide_index.T.astype(jnp.int32)
     order_rows = lax.broadcasted_iota(jnp.int32, (plan.order, wide), 0)
-    place_f = jnp.where(order_rows == index, 1.0, 0.0)
-    place_v = place_f.astype(BF16)
+    place_v = jnp.where(order_rows == index, 1.0, 0.0).astype(BF16)
     place[...] = place_v
-    lane = lax.broadcasted_iota(jnp.int32, (wide, plan.order), 1)
-    pick_f = jnp.where(lane == tall_index[:, 0:1], 1.0, 0.0)
+    order_lanes = lax.broadcasted_iota(jnp.int32, (wide, plan.order), 1)
+    pick_f = jnp.where(order_lanes == tall_index[:, 0:1], 1.0, 0.0)
     weight_row = 1.0 - 0.5 * jnp.sum(pick_f, axis=0, keepdims=True)
     pick = pick_f.astype(BF16)
     weight = whole_weight(place_v)
-    load = loads[...]
-    weighted = (weight * load.astype(F32)).astype(BF16)
-    image = dot(schur[...], jnp.concatenate([weighted, place_v], axis=1)).astype(BF16)
-    couple = coupling_t[...]
-    couple_w = (couple.astype(F32) * weight_row).astype(BF16)
-    first = dot(pick, image)
-    first_c = dot(couple_w, image)
-    picked = dot(pick, load)
-    edge = dot(couple, place_v)
-    map_pad[...] = jnp.zeros(map_pad.shape, F32)
+    copies[2].wait()
     corner_ids = corner_map[...]
     map_pad[0:1, 0:corners] = (corner_ids // 128).astype(F32)
     map_pad[1:2, 0:corners] = (corner_ids % 128).astype(F32)
+    copies[3].wait()
+    load = loads[...]
+    weighted = (weight * load.astype(F32)).astype(BF16)
+    message[0:pairs, :] = dot(pick, load)[:pairs].astype(BF16)
+    copies[4].wait()
+    couple = coupling_t[...]
+    couple_w = (couple.astype(F32) * weight_row).astype(BF16)
+    edge = dot(couple, place_v)
+    copies[5].wait()
+    image = dot(schur[...], jnp.concatenate([weighted, place_v], axis=1)).astype(BF16)
+    first = dot(pick, image)
+    first_c = dot(couple_w, image)
     tail = [first_c[:, :128], 0.5 * first_c[:, 128:], 0.5 * edge, map_pad[...]]
     if plan.tail > 3 * corners + 8:
         tail.append(jnp.zeros((plan.tail - 3 * corners - 8, 128), F32))
-    tail = jnp.concatenate(tail, axis=0).astype(BF16)
-    loads_part = picked[:pairs].astype(BF16)
-    image_part = first[:pairs, :128].astype(BF16)
-    schur_part = (0.5 * first[:pairs, 128:]).astype(BF16)
-    for d in range(plan.line):
-        message[d, 0:pairs, :] = loads_part
-        message[d, plan.image_at : plan.image_at + pairs, :] = image_part
-        message[d, plan.schur_at : plan.schur_at + pairs, :] = schur_part
-        message[d, plan.coarse_at : plan.coarse_at + plan.tail, :] = tail
+    message[plan.image_at : plan.image_at + pairs, :] = first[:pairs, :128].astype(BF16)
+    message[plan.schur_at : plan.schur_at + pairs, :] = (0.5 * first[:pairs, 128:]).astype(BF16)
+    message[plan.coarse_at :, :] = jnp.concatenate(tail, axis=0).astype(BF16)
+    copies[6].wait()
 
 
 def direction_kernel(plan, *refs):
-    received, schur, flexibility, loads, place = refs[:5]
-    coarse_refs = refs[5 : 5 + plan.groups]
-    message, residual, direction, local_part, far_image = refs[5 + plan.groups : 10 + plan.groups]
-    moved, images, moved_images, inputs = refs[10 + plan.groups :]
-    me = lax.axis_index("sub")
     line, each, pairs, corners = plan.line, plan.each, plan.pairs, plan.corners
+    received, refs = refs[:line], refs[line:]
+    coarse_refs, refs = refs[: plan.groups], refs[plan.groups :]
+    schur, flexibility, loads, place = refs[:4]
+    message, residual, direction, local_part, far_image = refs[4:9]
+    moved, images, moved_images, inputs = refs[9:]
     zero_rows = plan.wide - pairs
     codes = []
     per_tile = 128 // plan.spread
@@ -145,7 +173,7 @@
     for first in range(0, line, per_tile):
         code = jnp.full((1, 128), -1, jnp.int32)
         for u in range(first, first + per_tile):
-            tail = received[u, plan.coarse_at : plan.coarse_at + plan.tail, :].astype(F32)
+            tail = received[u][plan.coarse_at :, :].astype(F32)
             pair_of_rows = tail[3 * corners : 3 * corners + 8]
             number = (128.0 * pair_of_rows[0:1] + pair_of_rows[1:2]).astype(jnp.int32)
             number = jnp.where(lane[0:1] < corners, number, -1)
@@ -159,26 +187,22 @@
 
     tails = []
     for t in range(line):
-        for d in range(line):
-            if d == t:
-                continue
-            source, target = each * plan.slot(d, t), each * plan.slot(t, d)
-            moved[t, target : target + each, :] = received[d, source : source + each, :]
+        for d in plan.others(t):
+            at = plan.slot(t, d)
+            moved[t, at : at + each, :] = received[d][at : at + each, :]
         if zero_rows:
             moved[t, pairs:, :] = jnp.zeros((zero_rows, 128), BF16)
-        result = dot(received[t, plan.schur_at :, :], moved[t])
-        image = received[t, plan.image_at : plan.image_at + pairs, :].astype(F32) - result[:pairs]
+        result = dot(received[t][plan.schur_at :, :], moved[t])
+        image = received[t][plan.image_at : plan.image_at + pairs, :].astype(F32) - result[:pairs]
         images[t] = image
         tails.append(result[pairs + corners : pairs + 2 * corners])
     for t in range(line):
-        for d in range(line):
-            if d == t:
-                continue
-            source, target = each * plan.slot(d, t), each * plan.slot(t, d)
-            moved_images[t, target : target + each, :] = images[d, source : source + each, :]
+        for d in plan.others(t):
+            at = plan.slot(t, d)
+            moved_images[t, at : at + each, :] = images[d, at : at + each, :]
         if zero_rows:
             moved_images[t, pairs:, :] = jnp.zeros((zero_rows, 128), F32)
-        tail = received[t, plan.coarse_at :, :]
+        tail = received[t][plan.coarse_at :, :]
         edge = dot(tail, moved_images[t].astype(BF16))
         entry = tail.astype(F32)[:corners] - tails[t] - edge[2 * corners : 3 * corners]
         parts = [entry]
@@ -190,9 +214,9 @@
 
     place_v = place[...]
     weight = whole_weight(place_v)
-    right = loads[...].astype(F32) - dot(place_v, moved[me])
+    right = loads[...].astype(F32) - dot(place_v, moved[0])
     image = dot(schur[...], (weight * right).astype(BF16)).astype(BF16)
-    mine = moved_images[me]
+    mine = moved_images[0]
     far_image[...] = mine
     field = weight * (image.astype(F32) - dot(place_v, mine.astype(BF16)))
     residual[...] = right
@@ -205,19 +229,17 @@
     dots = jnp.zeros((8, 128), F32)
     for at, value in enumerate((inner_high, inner_low, square_high, square_low)):
         dots = jnp.where(row == at, value, dots)
-    parts = [coarse_out, inputs[me][:corners], dots]
+    parts = [coarse_out, inputs[0][:corners], dots]
     if plan.second > plan.dots_at + 8:
         parts.append(jnp.zeros((plan.second - plan.dots_at - 8, 128), F32))
     message[...] = jnp.concatenate(parts, axis=0).astype(BF16)
 
 
 def surface_kernel(plan, *refs):
-    groups, corners, each, pairs = plan.groups, plan.corners, plan.each, plan.pairs
+    groups, corners, pairs = plan.groups, plan.corners, plan.pairs
     heard = [ref[...].astype(F32) for ref in refs[:groups]]
     schur, coupling_t, place, local_part = refs[groups : groups + 4]
-    message, surface = refs[groups + 4 : groups + 6]
-    (image_rows,) = refs[groups + 6 :]
-    me = lax.axis_index("sub")
+    message, surface = refs[groups + 4 :]
     dots = sum(block[plan.dots_at : plan.dots_at + 8] for block in heard)
     inner = dots[0:1] + dots[1:2]
     square = dots[2:3] + dots[3:4]
@@ -225,12 +247,12 @@
     for m in range(groups):
         value = 0.0
         for d in range(groups):
-            at = corners * plan.shift(m, d)
+            at = corners * (m ^ d)
             value = value + heard[d][at : at + corners]
         value = value.astype(BF16)
         if m == 0:
             own = value
-        entry = heard[plan.back(m)][plan.input_at : plan.input_at + corners]
+        entry = heard[m][plan.input_at : plan.input_at + corners]
         square = square + jnp.sum(entry * value.astype(F32), axis=0, keepdims=True)
     lifted = lax.dot_general(
         coupling_t[...], own, (((0,), (0,)), ((), ())), preferred_element_type=F32
@@ -247,68 +269,47 @@
         (((0,), (0,)), ((), ())),
         preferred_element_type=F32,
     )[:pairs]
-    surface_part = both[:, :128].astype(BF16)
-    image_rows[...] = both[:, 128:].reshape(plan.line - 1, each, 128)
+    message[0:pairs, :] = both[:, :128].astype(BF16)
+    message[pairs : 2 * pairs, :] = both[:, 128:].astype(BF16)
     inner_high, inner_low = split(inner)
     square_high, square_low = split(square)
     row = lax.broadcasted_iota(jnp.int32, (16, 128), 0)
     sums = jnp.zeros((16, 128), F32)
     for at, value in enumerate((inner_high, inner_low, square_high, square_low)):
         sums = jnp.where(row == at, value, sums)
-    sums = sums.astype(BF16)
-    for d in range(plan.line):
-        at = jnp.minimum(plan.moving_slot(me, d), plan.line - 2)
-        message[d, 0:pairs, :] = surface_part
-        message[d, plan.own_at : plan.own_at + each, :] = image_rows[at].astype(BF16)
-        message[d, plan.sums_at :, :] = sums
-
-
-def result_kernel(
-    plan,
-    received,
-    first,
-    far_image,
-    residual,
-    direction,
-    surface,
-    schur,
-    place,
-    solution_out,
-    preconditioned,
-    moved,
-    far_rows,
-):
-    me = lax.axis_index("sub")
+    message[plan.sums_at :, :] = sums.astype(BF16)
+
+
+def result_kernel(plan, *refs):
     line, each, pairs = plan.line, plan.each, plan.pairs
+    received, first, refs = refs[:line], refs[line : 2 * line - 1], refs[2 * line - 1 :]
+    far_image, residual, direction, surface, schur, place = refs[:6]
+    solution_out, preconditioned, moved, far_rows = refs[6:]
     zero_rows = plan.wide - pairs
     sums = 0.0
-    for u in range(line):
-        sums = sums + received[u, plan.sums_at : plan.sums_at + 16, :].astype(F32)
+    for block in received:
+        sums = sums + block[plan.sums_at :, :].astype(F32)
     step = (sums[0:1] + sums[1:2]) / (sums[2:3] + sums[3:4])
-    far_rows[...] = jnp.zeros(far_rows.shape, F32)
     for t in range(line):
-        for d in range(line):
-            if d == t:
-                continue
-            source, target = each * plan.slot(d, t), each * plan.slot(t, d)
-            moved[t, target : target + each, :] = received[d, source : source + each, :]
+        for d in plan.others(t):
+            at = plan.slot(t, d)
+            moved[t, at : at + each, :] = received[d][at : at + each, :]
         if zero_rows:
             moved[t, pairs:, :] = jnp.zeros((zero_rows, 128), BF16)
-    for t in range(line):
-        at = jnp.minimum(plan.moving_slot(t, me), line - 2)
-        block = first[t, pl.ds(pl.multiple_of(plan.schur_at + each * at, 16), each), :]
-        change = received[t, plan.own_at : plan.own_at + each, :].astype(F32) - dot(block, moved[t])
-        there = jnp.where(me == t, line - 1, plan.moving_slot(me, t))
-        far_rows[there] = change
-    far = far_image[...] - step * far_rows[...].reshape(line * each, 128)[: plan.wide]
+    if zero_rows:
+        far_rows[pairs:, :] = jnp.zeros((zero_rows, 128), F32)
+    for t in range(1, line):
+        at = plan.slot(0, t)
+        block = first[t - 1][plan.schur_at + at : plan.schur_at + at + each, :]
+        image = received[t][pairs + at : pairs + at + each, :].astype(F32)
+        far_rows[at : at + each, :] = image - dot(block, moved[t])
+    far = far_image[...] - step * far_rows[...]
     place_v = place[...]
     weight = whole_weight(place_v)
-    operated = surface[...].astype(F32) - dot(place_v, moved[me])
+    operated = surface[...].astype(F32) - dot(place_v, moved[0])
     remaining = residual[...] - step * operated
     image = dot(schur[...], (weight * remaining).astype(BF16)).astype(BF16)
-    row = lax.broadcasted_iota(jnp.int32, far.shape, 0)
-    far = jnp.where(row < pairs, far, 0.0).astype(BF16)
-    preconditioned[...] = weight * (image.astype(F32) - dot(place_v, far))
+    preconditioned[...] = weight * (image.astype(F32) - dot(place_v, far.astype(BF16)))
     solution_out[...] = step * direction[...]
 
 
@@ -327,33 +328,57 @@
     flex, schur, loads = flexibility[0, 0], dirichlet_schur[0, 0], subdomain_loads[0, 0]
     coupling_t = coupling[0, 0].T
     coarse = coarse_rows[0, 0]
+    rows = jnp.transpose(interface_rows, (0, 2, 1, 3))[0]
     whole = pl.BlockSpec(memory_space=pltpu.VMEM)
+    outside = pl.BlockSpec(memory_space=pltpu.HBM)
     params = pltpu.CompilerParams(vmem_limit_bytes=VMEM_BYTES)
 
     def shape(*dims, kind=F32):
         return jax.ShapeDtypeStruct(dims, kind)
 
-    def turn(value, step):
-        pairs = [(g, plan.shift(g, step)) for g in range(plan.groups)]
-        return lax.ppermute(value, "grp", pairs)
-
-    coarse_all = [coarse]
-    for step in range(1, plan.groups):
-        coarse_all.append(turn(coarse, plan.back(step)))
-
-    message, place = pl.pallas_call(
+    def swap(value, axis, distance):
+        size = lax.axis_size(axis)
+        return lax.ppermute(value, axis, [(at, at ^ distance) for at in range(size)])
+
+    def line_blocks(value, riders=()):
+        blocks = [value] + [None] * (line - 1)
+        moved = []
+        for far in reversed(range(2, line, 2)):
+            blocks[far] = swap(value, "sub", far)
+        blocks[1] = swap(value, "sub", 1)
+        for far in reversed(range(2, line, 2)):
+            block = blocks[far]
+            if len(moved) < len(riders):
+                rider, distance = riders[len(moved)]
+                block, rider = lax.optimization_barrier((block, rider))
+                moved.append(swap(rider, "grp", distance))
+                blocks[far] = block
+            blocks[far + 1] = swap(block, "sub", 1)
+        for rider, distance in riders[len(moved) :]:
+            moved.append(swap(rider, "grp", distance))
+        return blocks, moved
+
+    lists = (neighbors[0], rows, coarse_map[0])
+    kept = (schur, loads, coupling_t, flex)
+    kept = tuple(pltpu.with_memory_space_constraint(array, pltpu.HBM) for array in kept)
+    message, place, schur, loads, coupling_t, flex = pl.pallas_call(
         functools.partial(prepare_kernel, plan),
-        out_shape=(shape(line, plan.first, 128, kind=BF16), shape(order, plan.wide, kind=BF16)),
-        in_specs=[pl.BlockSpec(memory_space=pltpu.SMEM)] + [whole] * 5,
-        out_specs=(whole, whole),
-        scratch_shapes=[
-            pltpu.VMEM((round_up(plan.neighbors, 8), 128), jnp.int32),
+        out_shape=(shape(plan.first, 128, kind=BF16), shape(order, plan.wide, kind=BF16))
+        + tuple(shape(*array.shape, kind=BF16) for array in kept),
+        in_specs=[outside] * 7,
+        out_specs=(whole,) * 6,
+        scratch_shapes=[pltpu.VMEM(array.shape, array.dtype) for array in lists]
+        + [
+            pltpu.VMEM((round_up(plan.neighbors, 8), plan.wide), jnp.int32),
             pltpu.VMEM((8, 128), F32),
+            pltpu.SemaphoreType.DMA((7,)),
         ],
         compiler_params=params,
         name="prepare",
-    )(neighbors[0], interface_rows[0, 0], coarse_map[0], schur, loads, coupling_t)
-    first = lax.all_to_all(message, "sub", split_axis=0, concat_axis=0, tiled=True)
+    )(*lists, *kept)
+    riders = [(coarse, distance) for distance in reversed(range(1, plan.groups))]
+    first, moved = line_blocks(message, riders)
+    coarse_all = [coarse] + moved[::-1]
 
     message, residual, direction, local_part, far_image = pl.pallas_call(
         functools.partial(direction_kernel, plan),
@@ -364,7 +389,7 @@
             shape(order, 128),
             shape(plan.wide, 128),
         ),
-        in_specs=[whole] * (5 + plan.groups),
+        in_specs=[whole] * (line + plan.groups + 4),
         out_specs=(whole,) * 5,
         scratch_shapes=[
             pltpu.VMEM((line, plan.wide, 128), BF16),
@@ -374,34 +399,33 @@
         ],
         compiler_params=params,
         name="direction",
-    )(first, schur, flex, loads, place, *coarse_all)
+    )(*first, *coarse_all, schur, flex, loads, place)
     heard = [message]
     for step in range(1, plan.groups):
-        heard.append(turn(message, step))
+        heard.append(swap(message, "grp", step))
 
     message, surface = pl.pallas_call(
         functools.partial(surface_kernel, plan),
-        out_shape=(shape(line, plan.third, 128, kind=BF16), shape(order, 128, kind=BF16)),
+        out_shape=(shape(plan.third, 128, kind=BF16), shape(order, 128, kind=BF16)),
         in_specs=[whole] * (plan.groups + 4),
         out_specs=(whole, whole),
-        scratch_shapes=[pltpu.VMEM((line - 1, plan.each, 128), F32)],
         compiler_params=params,
         name="surface",
     )(*heard, schur, coupling_t, place, local_part)
-    last = lax.all_to_all(message, "sub", split_axis=0, concat_axis=0, tiled=True)
+    last, _ = line_blocks(message)
 
     solved, preconditioned = pl.pallas_call(
         functools.partial(result_kernel, plan),
         out_shape=(shape(order, 128), shape(order, 128)),
-        in_specs=[whole] * 8,
+        in_specs=[whole] * (2 * line + 5),
         out_specs=(whole, whole),
         scratch_shapes=[
             pltpu.VMEM((line, plan.wide, 128), BF16),
-            pltpu.VMEM((line, plan.each, 128), F32),
+            pltpu.VMEM((plan.wide, 128), F32),
         ],
         compiler_params=params,
         name="result",
-    )(last, first, far_image, residual, direction, surface, schur, place)
+    )(*last, *first[1:], far_image, residual, direction, surface, schur, place)
     return solved[None, None], preconditioned[None, None]
 
 

time: 58.3 us -> 47.6 us (0.82)
  blocking collectives: 14.2 us -> 0 us
  starting transfers between devices: 11.2 us -> 24.2 us
  waiting for transfers between devices: 21.9 us -> 16.4 us
  local copies, waits for them, and re-layouts: 4.06 us -> 0.67 us
    ppermute x6 -> x20, starting transfers between devices: 3.85 us -> 24.2 us  [swap(): lax.ppermute(value, axis, [(at, at ^ distance) for at in range(size)])]
    all_to_all x1 -> x0, waiting for transfers between devices: 14.4 us -> none  [line_body(): lax.all_to_all(message, 'sub', split_axis=0, concat_axis=0, tiled=True)]
    all_to_all x1 -> x0, blocking collectives: 14.2 us -> none  [line_body(): lax.all_to_all(message, 'sub', split_axis=0, concat_axis=0, tiled=True)]
    ppermute x6 -> x20, waiting for transfers between devices: 7.52 us -> 16.4 us  [swap(): lax.ppermute(value, axis, [(at, at ^ distance) for at in range(size)])]
    all_to_all x1 -> x0, starting transfers between devices: 7.4 us -> none  [line_body(): lax.all_to_all(message, 'sub', split_axis=0, concat_axis=0, tiled=True)]
    unnamed x21 -> x8, local copies, waits for them, and re-layouts: 4.06 us -> 0.67 us
  transfers between devices with their start and end apart: 7 -> 20, of which waited for: 5 -> 8; matrix products, arithmetic and copies ran while one was open for 0% -> 0% of each run, Pallas kernels for 0% -> 0%
where the time goes in v2:
time: 47.6 us; the launch traced here: 47.4 us
  starting transfers between devices  24.2 us (51%)
  waiting for transfers between devices  16.4 us (34%)
  Pallas kernels  5.41 us (11%)
  between operations  0.71 us (1%)
  local copies, waits for them, and re-layouts  0.67 us (1%)
    ppermute x20, starting transfers between devices, swap(): lax.ppermute(value, axis, [(at, at ^ distance) for at in range(size)])  24.2 us
    ppermute x20, waiting for transfers between devices, swap(): lax.ppermute(value, axis, [(at, at ^ distance) for at in range(size)])  16.4 us
    pallas_call x1, Pallas kernels, line_body(): pl.pallas_call(functools.partial(prepare_kernel, plan), out_shape=(shape(...  1.89 us
    pallas_call x1, Pallas kernels, line_body(): pl.pallas_call(functools.partial(direction_kernel, plan), out_shape=(shap...  1.52 us
    pallas_call x1, Pallas kernels, line_body(): pl.pallas_call(functools.partial(result_kernel, plan), out_shape=(shape(o...  1.32 us
  transfers between devices with their start and end apart: 20, of which 8 were waited for; matrix products, arithmetic and copies ran while one was open for 0% of the time, Pallas kernels for 0%

profile of v2, /device:TPU:0, one launch (start us, length us, event | category | flops | bytes accessed | tf_op | source)
XLA Modules:
  0.0 47.4 jit_solution(10896975898037097283)
XLA Ops:
  0.6 0.0 copy-start.1
  0.6 0.0 copy-start.2
  0.7 0.7 %copy-done.1 = s32[1,1,6,16]{3,1,2,0:T(1,128)S(1)} copy-done((s32[1,1,6,16]{3,1,2,0:T(1,128)S(1)}, s32[1,1,6,16]{3,1,2,0:T(1,128)}, u32[]{:S(2)}) %copy-start.1) | copy-done | bytes 408
  1.3 0.0 copy-done.2
  1.3 1.9 %prepare.1 = (bf16[416,128]{1,0:T(8,128)(2,1)S(1)}, bf16[512,128]{1,0:T(8,128)(2,1)S(1)}, bf16[512,512]{1,0:T(8,128)(2,1)S(1)}, bf16[512,128]{1,0:T(8,128)(2,1)S...) custom-call(s32[1,6]{1,0:T(1,128)S(1)} %bitcast.17, s32[6,1,16]{2,1,0:T(1,128)S(1)} %bitcast.16, ...), custom_call_target="tpu_custom_call" | custom-call | tf_op jit(solution)/shard_map/prepare/pallas_call | solution.py:364
  3.2 5.1 %collective-permute-start.5 = (bf16[416,128]{1,0:T(8,128)(2,1)S(1)}, bf16[416,128]{1,0:T(8,128)(2,1)S(1)}, u32[]{:S(2)}, u32[]{:S(2)}) collective-permute-start(bf16[416,128]{1,0:T(8,128)(2,1)S(1)} %get-tuple-element.23.refs_0_), channel_id=1, source_target_pairs={{0,24},{4,28},{8,16},{12,20},{16,8},{20,12},{24,0},{28,4},{1,25},{... | collective-permute-start | bytes 319496 | tf_op jit(solution)/shard_map/ppermute | solution.py:341
  8.3 0.0 collective-permute-start.3
  8.3 0.6 %collective-permute-start.1 = (bf16[416,128]{1,0:T(8,128)(2,1)S(1)}, bf16[416,128]{1,0:T(8,128)(2,1)S(1)}, u32[]{:S(2)}, u32[]{:S(2)}) collective-permute-start(bf16[416,128]{1,0:T(8,128)(2,1)S(1)} %get-tuple-element.23.refs_0_), channel_id=1, source_target_pairs={{0,8},{4,12},{8,0},{12,4},{16,24},{20,28},{24,16},{28,20},{1,9},{5... | collective-permute-start | bytes 319496 | tf_op jit(solution)/shard_map/ppermute | solution.py:341
  9.0 1.6 %collective-permute-start = (bf16[416,128]{1,0:T(8,128)(2,1)S(1)}, bf16[416,128]{1,0:T(8,128)(2,1)S(1)}, u32[]{:S(2)}, u32[]{:S(2)}) collective-permute-start(bf16[416,128]{1,0:T(8,128)(2,1)S(1)} %get-tuple-element.23.refs_0_), channel_id=1, source_target_pairs={{0,4},{4,0},{8,12},{12,8},{16,20},{20,16},{24,28},{28,24},{1,5},{5... | collective-permute-start | bytes 319496 | tf_op jit(solution)/shard_map/ppermute | solution.py:341
  10.6 1.6 %collective-permute-done.5.refs_6_.refs_13_ = bf16[416,128]{1,0:T(8,128)(2,1)S(1)} collective-permute-done((bf16[416,128]{1,0:T(8,128)(2,1)S(1)}, bf16[416,128]{1,0:T(8,128)(2,1)S(1)}, u32[]{:S(2)}, u32[]{:S(2)}) %collective-permute-start.5) | collective-permute-done | bytes 106528 | tf_op jit(solution)/shard_map/ppermute | solution.py:341
  12.2 0.0 collective-permute-start.9
  12.2 1.6 %collective-permute-start.6 = (bf16[416,128]{1,0:T(8,128)(2,1)S(1)}, bf16[416,128]{1,0:T(8,128)(2,1)S(1)}, u32[]{:S(2)}, u32[]{:S(2)}) collective-permute-start(bf16[416,128]{1,0:T(8,128)(2,1)S(1)} %collective-permute-done.5.refs_6_.refs_13_), channel_id=1, source_target_pairs={{0,4},{4,0},{8,12},{12,8},{16,20},{20,16},{24,28},{28,24},{1,5},{5... | collective-permute-start | bytes 319496 | tf_op jit(solution)/shard_map/ppermute | solution.py:341
  13.9 3.4 %collective-permute-done.3.refs_4_.refs_11_ = bf16[416,128]{1,0:T(8,128)(2,1)S(1)} collective-permute-done((bf16[416,128]{1,0:T(8,128)(2,1)S(1)}, bf16[416,128]{1,0:T(8,128)(2,1)S(1)}, u32[]{:S(2)}, u32[]{:S(2)}) %collective-permute-start.3) | collective-permute-done | bytes 106528 | tf_op jit(solution)/shard_map/ppermute | solution.py:341
  17.3 1.5 %collective-permute-start.4 = (bf16[416,128]{1,0:T(8,128)(2,1)S(1)}, bf16[416,128]{1,0:T(8,128)(2,1)S(1)}, u32[]{:S(2)}, u32[]{:S(2)}) collective-permute-start(bf16[416,128]{1,0:T(8,128)(2,1)S(1)} %collective-permute-done.3.refs_4_.refs_11_), channel_id=1, source_target_pairs={{0,4},{4,0},{8,12},{12,8},{16,20},{20,16},{24,28},{28,24},{1,5},{5... | collective-permute-start | bytes 319496 | tf_op jit(solution)/shard_map/ppermute | solution.py:341
  18.8 0.0 collective-permute-done.1.refs_2_.refs_9_
  18.8 0.6 %collective-permute-start.2 = (bf16[416,128]{1,0:T(8,128)(2,1)S(1)}, bf16[416,128]{1,0:T(8,128)(2,1)S(1)}, u32[]{:S(2)}, u32[]{:S(2)}) collective-permute-start(bf16[416,128]{1,0:T(8,128)(2,1)S(1)} %collective-permute-done.1.refs_2_.refs_9_), channel_id=1, source_target_pairs={{0,4},{4,0},{8,12},{12,8},{16,20},{20,16},{24,28},{28,24},{1,5},{5... | collective-permute-start | bytes 319496 | tf_op jit(solution)/shard_map/ppermute | solution.py:341
  19.4 0.0 collective-permute-done.refs_1_.refs_8_
  19.4 1.5 %collective-permute-start.8 = (bf16[24,2048]{1,0:T(8,128)(2,1)S(1)}, bf16[24,2048]{1,0:T(8,128)(2,1)S(1)}, u32[]{:S(2)}, u32[]{:S(2)}) collective-permute-start(bf16[24,2048]{1,0:T(8,128)(2,1)S(1)} %bitcast.13), channel_id=1, source_target_pairs={{0,2},{1,3},{2,0},{3,1},{4,6},{5,7},{6,4},{7,5},{8,10},{9,11},{10,... | collective-permute-start | bytes 294920 | tf_op jit(solution)/shard_map/ppermute | solution.py:341
  20.9 0.0 collective-permute-done.9.refs_11_
  20.9 0.0 collective-permute-start.7
  20.9 3.1 %collective-permute-done.8.refs_10_ = bf16[24,2048]{1,0:T(8,128)(2,1)S(1)} collective-permute-done((bf16[24,2048]{1,0:T(8,128)(2,1)S(1)}, bf16[24,2048]{1,0:T(8,128)(2,1)S(1)}, u32[]{:S(2)}, u32[]{:S(2)}) %collective-permute-start.8) | collective-permute-done | bytes 98336 | tf_op jit(solution)/shard_map/ppermute | solution.py:341
  24.0 0.0 collective-permute-done.7.refs_9_
  24.0 0.0 collective-permute-done.6.refs_7_.refs_14_
  24.0 0.0 collective-permute-done.4.refs_5_.refs_12_
  24.0 0.0 collective-permute-done.2.refs_3_.refs_10_
  24.0 1.5 %direction.1 = (bf16[128,128]{1,0:T(8,128)(2,1)S(1)}, f32[512,128]{1,0:T(8,128)S(1)}, f32[512,128]{1,0:T(8,128)S(1)}, f32[512,128]{1,0:T(8,128)S(1)}, f32[128,128]{1,0:T(8,128)S(1)}) custom-call(bf16[416,128]{1,0:T(8,128)(2,1)S(1)} %get-tuple-element.23.refs_0_, bf16[416,128]{1,0:T(8,128)(2,1)S(1)} %collective-permute-done.refs_1_.refs_8_, ...), custom_call_target="tpu_custom_call" | custom-call | tf_op jit(solution)/shard_map/direction/pallas_call | solution.py:383
  25.5 0.1 collective-permute-start.12
  25.6 1.6 %collective-permute-start.11 = (bf16[128,128]{1,0:T(8,128)(2,1)S(1)}, bf16[128,128]{1,0:T(8,128)(2,1)S(1)}, u32[]{:S(2)}, u32[]{:S(2)}) collective-permute-start(bf16[128,128]{1,0:T(8,128)(2,1)S(1)} %get-tuple-element.34.refs_0_), channel_id=1, source_target_pairs={{0,2},{1,3},{2,0},{3,1},{4,6},{5,7},{6,4},{7,5},{8,10},{9,11},{10,... | collective-permute-start | bytes 98312 | tf_op jit(solution)/shard_map/ppermute | solution.py:341
  27.2 0.3 collective-permute-start.10
  27.4 1.8 %collective-permute-done.12.refs_3_ = bf16[128,128]{1,0:T(8,128)(2,1)S(1)} collective-permute-done((bf16[128,128]{1,0:T(8,128)(2,1)S(1)}, bf16[128,128]{1,0:T(8,128)(2,1)S(1)}, u32[]{:S(2)}, u32[]{:S(2)}) %collective-permute-start.12) | collective-permute-done | bytes 32800 | tf_op jit(solution)/shard_map/ppermute | solution.py:341
  29.2 0.4 collective-permute-done.11.refs_2_
  29.6 0.0 collective-permute-done.10.refs_1_
  29.6 0.7 %surface.1 = (bf16[240,128]{1,0:T(8,128)(2,1)S(1)}, bf16[512,128]{1,0:T(8,128)(2,1)S(1)}) custom-call(bf16[128,128]{1,0:T(8,128)(2,1)S(1)} %get-tuple-element.34.refs_0_, bf16[128,128]{1,0:T(8,128)(2,1)S(1)} %collective-permute-done.10.refs_1_, bf16[128,128]{1,0:T(8,128)(2,1)S(1)} %collective-permute-done.11.refs_2_, ...), custom_call_target="tpu_custom_call" | custom-call | tf_op jit(solution)/shard_map/surface/pallas_call | solution.py:407
  30.3 2.5 %collective-permute-start.18 = (bf16[240,128]{1,0:T(8,128)(2,1)S(1)}, bf16[240,128]{1,0:T(8,128)(2,1)S(1)}, u32[]{:S(2)}, u32[]{:S(2)}) collective-permute-start(bf16[240,128]{1,0:T(8,128)(2,1)S(1)} %get-tuple-element.37.refs_0_), channel_id=1, source_target_pairs={{0,24},{4,28},{8,16},{12,20},{16,8},{20,12},{24,0},{28,4},{1,25},{... | collective-permute-start | bytes 184328 | tf_op jit(solution)/shard_map/ppermute | solution.py:341
  32.9 2.5 %collective-permute-start.16 = (bf16[240,128]{1,0:T(8,128)(2,1)S(1)}, bf16[240,128]{1,0:T(8,128)(2,1)S(1)}, u32[]{:S(2)}, u32[]{:S(2)}) collective-permute-start(bf16[240,128]{1,0:T(8,128)(2,1)S(1)} %get-tuple-element.37.refs_0_), channel_id=1, source_target_pairs={{0,16},{4,20},{8,24},{12,28},{16,0},{20,4},{24,8},{28,12},{1,17},{... | collective-permute-start | bytes 184328 | tf_op jit(solution)/shard_map/ppermute | solution.py:341
  35.3 0.3 collective-permute-start.14
  35.7 1.5 %collective-permute-start.13 = (bf16[240,128]{1,0:T(8,128)(2,1)S(1)}, bf16[240,128]{1,0:T(8,128)(2,1)S(1)}, u32[]{:S(2)}, u32[]{:S(2)}) collective-permute-start(bf16[240,128]{1,0:T(8,128)(2,1)S(1)} %get-tuple-element.37.refs_0_), channel_id=1, source_target_pairs={{0,4},{4,0},{8,12},{12,8},{16,20},{20,16},{24,28},{28,24},{1,5},{5... | collective-permute-start | bytes 184328 | tf_op jit(solution)/shard_map/ppermute | solution.py:341
  37.2 0.0 collective-permute-done.18.refs_6_
  37.2 0.8 %collective-permute-start.19 = (bf16[240,128]{1,0:T(8,128)(2,1)S(1)}, bf16[240,128]{1,0:T(8,128)(2,1)S(1)}, u32[]{:S(2)}, u32[]{:S(2)}) collective-permute-start(bf16[240,128]{1,0:T(8,128)(2,1)S(1)} %collective-permute-done.18.refs_6_), channel_id=1, source_target_pairs={{0,4},{4,0},{8,12},{12,8},{16,20},{20,16},{24,28},{28,24},{1,5},{5... | collective-permute-start | bytes 184328 | tf_op jit(solution)/shard_map/ppermute | solution.py:341
  38.0 2.4 %collective-permute-done.16.refs_4_ = bf16[240,128]{1,0:T(8,128)(2,1)S(1)} collective-permute-done((bf16[240,128]{1,0:T(8,128)(2,1)S(1)}, bf16[240,128]{1,0:T(8,128)(2,1)S(1)}, u32[]{:S(2)}, u32[]{:S(2)}) %collective-permute-start.16) | collective-permute-done | bytes 61472 | tf_op jit(solution)/shard_map/ppermute | solution.py:341
  40.4 1.5 %collective-permute-start.17 = (bf16[240,128]{1,0:T(8,128)(2,1)S(1)}, bf16[240,128]{1,0:T(8,128)(2,1)S(1)}, u32[]{:S(2)}, u32[]{:S(2)}) collective-permute-start(bf16[240,128]{1,0:T(8,128)(2,1)S(1)} %collective-permute-done.16.refs_4_), channel_id=1, source_target_pairs={{0,4},{4,0},{8,12},{12,8},{16,20},{20,16},{24,28},{28,24},{1,5},{5... | collective-permute-start | bytes 184328 | tf_op jit(solution)/shard_map/ppermute | solution.py:341
  41.9 0.0 collective-permute-done.14.refs_2_
  41.9 0.5 %collective-permute-start.15 = (bf16[240,128]{1,0:T(8,128)(2,1)S(1)}, bf16[240,128]{1,0:T(8,128)(2,1)S(1)}, u32[]{:S(2)}, u32[]{:S(2)}) collective-permute-start(bf16[240,128]{1,0:T(8,128)(2,1)S(1)} %collective-permute-done.14.refs_2_), channel_id=1, source_target_pairs={{0,4},{4,0},{8,12},{12,8},{16,20},{20,16},{24,28},{28,24},{1,5},{5... | collective-permute-start | bytes 184328 | tf_op jit(solution)/shard_map/ppermute | solution.py:341
  42.4 0.0 collective-permute-done.13.refs_1_
  42.4 0.0 collective-permute-done.19.refs_7_
  42.4 2.2 %collective-permute-done.17.refs_5_ = bf16[240,128]{1,0:T(8,128)(2,1)S(1)} collective-permute-done((bf16[240,128]{1,0:T(8,128)(2,1)S(1)}, bf16[240,128]{1,0:T(8,128)(2,1)S(1)}, u32[]{:S(2)}, u32[]{:S(2)}) %collective-permute-start.17) | collective-permute-done | bytes 61472 | tf_op jit(solution)/shard_map/ppermute | solution.py:341
  44.6 1.5 %collective-permute-done.15.refs_3_ = bf16[240,128]{1,0:T(8,128)(2,1)S(1)} collective-permute-done((bf16[240,128]{1,0:T(8,128)(2,1)S(1)}, bf16[240,128]{1,0:T(8,128)(2,1)S(1)}, u32[]{:S(2)}, u32[]{:S(2)}) %collective-permute-start.15) | collective-permute-done | bytes 61472 | tf_op jit(solution)/shard_map/ppermute | solution.py:341
  46.1 1.3 %result.1 = (f32[512,128]{1,0:T(8,128)}, f32[512,128]{1,0:T(8,128)}) custom-call(bf16[240,128]{1,0:T(8,128)(2,1)S(1)} %get-tuple-element.37.refs_0_, bf16[240,128]{1,0:T(8,128)(2,1)S(1)} %collective-permute-done.13.refs_1_, bf16[240,128]{1,0:T(8,128)(2,1)S(1)} %collective-permute-done.14.refs_2_, bf16[240,128]{1,0:T(8,128)(2,1)S(1)} %collective-permute-done.15.refs_3_, ...), custom_call_target="tpu_custom_call" | custom-call | tf_op jit(solution)/shard_map/result/pallas_call | solution.py:417
  (4 shorter events, 0.0 us)
Async XLA Ops:
  0.6 0.7 %copy-start.1 = (s32[1,1,6,16]{3,1,2,0:T(1,128)S(1)}, s32[1,1,6,16]{3,1,2,0:T(1,128)}, u32[]{:S(2)}) copy-start(s32[1,1,6,16]{3,1,2,0:T(1,128)} %param.14) | copy-start | bytes 1156
  0.6 0.7 %copy-start.2 = (s32[1,1,6]{2,1,0:T(1,128)S(1)}, s32[1,1,6]{2,1,0:T(1,128)}, u32[]{:S(2)}) copy-start(s32[1,1,6]{2,1,0:T(1,128)} %param.13) | copy-start | bytes 76
  0.7 0.7 %copy-start.3 = (s32[1,1,24]{2,1,0:T(1,128)S(1)}, s32[1,1,24]{2,1,0:T(1,128)}, u32[]{:S(2)}) copy-start(s32[1,1,24]{2,1,0:T(1,128)} %param.15) | copy-start | bytes 292
  1.3 10.9 %copy-start = (bf16[1,1,24,2048]{3,2,1,0:T(8,128)(2,1)S(1)}, bf16[1,1,24,2048]{3,2,1,0:T(8,128)(2,1)}, u32[]{:S(2)}) copy-start(bf16[1,1,24,2048]{3,2,1,0:T(8,128)(2,1)} %param.12) | copy-start | bytes 294916
  3.2 9.0 %collective-permute-start.5 = (bf16[416,128]{1,0:T(8,128)(2,1)S(1)}, bf16[416,128]{1,0:T(8,128)(2,1)S(1)}, u32[]{:S(2)}, u32[]{:S(2)}) collective-permute-start(bf16[416,128]{1,0:T(8,128)(2,1)S(1)} %get-tuple-element.23.refs_0_), channel_id=1, source_target_pairs={{0,24},{4,28},{8,16},{12,20},{16,8},{20,12},{24,0},{28,4},{1,25},{... | collective-permute-start | bytes 319496 | tf_op jit(solution)/shard_map/ppermute | solution.py:341
  8.3 9.0 %collective-permute-start.3 = (bf16[416,128]{1,0:T(8,128)(2,1)S(1)}, bf16[416,128]{1,0:T(8,128)(2,1)S(1)}, u32[]{:S(2)}, u32[]{:S(2)}) collective-permute-start(bf16[416,128]{1,0:T(8,128)(2,1)S(1)} %get-tuple-element.23.refs_0_), channel_id=1, source_target_pairs={{0,16},{4,20},{8,24},{12,28},{16,0},{20,4},{24,8},{28,12},{1,17},{... | collective-permute-start | bytes 319496 | tf_op jit(solution)/shard_map/ppermute | solution.py:341
  8.3 10.5 %collective-permute-start.1 = (bf16[416,128]{1,0:T(8,128)(2,1)S(1)}, bf16[416,128]{1,0:T(8,128)(2,1)S(1)}, u32[]{:S(2)}, u32[]{:S(2)}) collective-permute-start(bf16[416,128]{1,0:T(8,128)(2,1)S(1)} %get-tuple-element.23.refs_0_), channel_id=1, source_target_pairs={{0,8},{4,12},{8,0},{12,4},{16,24},{20,28},{24,16},{28,20},{1,9},{5... | collective-permute-start | bytes 319496 | tf_op jit(solution)/shard_map/ppermute | solution.py:341
  9.0 10.4 %collective-permute-start = (bf16[416,128]{1,0:T(8,128)(2,1)S(1)}, bf16[416,128]{1,0:T(8,128)(2,1)S(1)}, u32[]{:S(2)}, u32[]{:S(2)}) collective-permute-start(bf16[416,128]{1,0:T(8,128)(2,1)S(1)} %get-tuple-element.23.refs_0_), channel_id=1, source_target_pairs={{0,4},{4,0},{8,12},{12,8},{16,20},{20,16},{24,28},{28,24},{1,5},{5... | collective-permute-start | bytes 319496 | tf_op jit(solution)/shard_map/ppermute | solution.py:341
  12.2 8.6 %collective-permute-start.9 = (bf16[24,2048]{1,0:T(8,128)(2,1)S(1)}, bf16[24,2048]{1,0:T(8,128)(2,1)S(1)}, u32[]{:S(2)}, u32[]{:S(2)}) collective-permute-start(bf16[24,2048]{1,0:T(8,128)(2,1)S(1)} %bitcast.12), channel_id=1, source_target_pairs={{0,3},{1,2},{2,1},{3,0},{4,7},{5,6},{6,5},{7,4},{8,11},{9,10},{10,... | collective-permute-start | bytes 294920 | tf_op jit(solution)/shard_map/ppermute | solution.py:341
  12.2 11.7 %collective-permute-start.6 = (bf16[416,128]{1,0:T(8,128)(2,1)S(1)}, bf16[416,128]{1,0:T(8,128)(2,1)S(1)}, u32[]{:S(2)}, u32[]{:S(2)}) collective-permute-start(bf16[416,128]{1,0:T(8,128)(2,1)S(1)} %collective-permute-done.5.refs_6_.refs_13_), channel_id=1, source_target_pairs={{0,4},{4,0},{8,12},{12,8},{16,20},{20,16},{24,28},{28,24},{1,5},{5... | collective-permute-start | bytes 319496 | tf_op jit(solution)/shard_map/ppermute | solution.py:341
  17.3 6.7 %collective-permute-start.4 = (bf16[416,128]{1,0:T(8,128)(2,1)S(1)}, bf16[416,128]{1,0:T(8,128)(2,1)S(1)}, u32[]{:S(2)}, u32[]{:S(2)}) collective-permute-start(bf16[416,128]{1,0:T(8,128)(2,1)S(1)} %collective-permute-done.3.refs_4_.refs_11_), channel_id=1, source_target_pairs={{0,4},{4,0},{8,12},{12,8},{16,20},{20,16},{24,28},{28,24},{1,5},{5... | collective-permute-start | bytes 319496 | tf_op jit(solution)/shard_map/ppermute | solution.py:341
  18.8 5.2 %collective-permute-start.2 = (bf16[416,128]{1,0:T(8,128)(2,1)S(1)}, bf16[416,128]{1,0:T(8,128)(2,1)S(1)}, u32[]{:S(2)}, u32[]{:S(2)}) collective-permute-start(bf16[416,128]{1,0:T(8,128)(2,1)S(1)} %collective-permute-done.1.refs_2_.refs_9_), channel_id=1, source_target_pairs={{0,4},{4,0},{8,12},{12,8},{16,20},{20,16},{24,28},{28,24},{1,5},{5... | collective-permute-start | bytes 319496 | tf_op jit(solution)/shard_map/ppermute | solution.py:341
  19.4 4.6 %collective-permute-start.8 = (bf16[24,2048]{1,0:T(8,128)(2,1)S(1)}, bf16[24,2048]{1,0:T(8,128)(2,1)S(1)}, u32[]{:S(2)}, u32[]{:S(2)}) collective-permute-start(bf16[24,2048]{1,0:T(8,128)(2,1)S(1)} %bitcast.13), channel_id=1, source_target_pairs={{0,2},{1,3},{2,0},{3,1},{4,6},{5,7},{6,4},{7,5},{8,10},{9,11},{10,... | collective-permute-start | bytes 294920 | tf_op jit(solution)/shard_map/ppermute | solution.py:341
  20.9 3.1 %collective-permute-start.7 = (bf16[24,2048]{1,0:T(8,128)(2,1)S(1)}, bf16[24,2048]{1,0:T(8,128)(2,1)S(1)}, u32[]{:S(2)}, u32[]{:S(2)}) collective-permute-start(bf16[24,2048]{1,0:T(8,128)(2,1)S(1)} %bitcast.14), channel_id=1, source_target_pairs={{0,1},{1,0},{2,3},{3,2},{4,5},{5,4},{6,7},{7,6},{8,9},{9,8},{10,11... | collective-permute-start | bytes 294920 | tf_op jit(solution)/shard_map/ppermute | solution.py:341
  25.5 3.7 %collective-permute-start.12 = (bf16[128,128]{1,0:T(8,128)(2,1)S(1)}, bf16[128,128]{1,0:T(8,128)(2,1)S(1)}, u32[]{:S(2)}, u32[]{:S(2)}) collective-permute-start(bf16[128,128]{1,0:T(8,128)(2,1)S(1)} %get-tuple-element.34.refs_0_), channel_id=1, source_target_pairs={{0,3},{1,2},{2,1},{3,0},{4,7},{5,6},{6,5},{7,4},{8,11},{9,10},{10,... | collective-permute-start | bytes 98312 | tf_op jit(solution)/shard_map/ppermute | solution.py:341
  25.6 4.0 %collective-permute-start.11 = (bf16[128,128]{1,0:T(8,128)(2,1)S(1)}, bf16[128,128]{1,0:T(8,128)(2,1)S(1)}, u32[]{:S(2)}, u32[]{:S(2)}) collective-permute-start(bf16[128,128]{1,0:T(8,128)(2,1)S(1)} %get-tuple-element.34.refs_0_), channel_id=1, source_target_pairs={{0,2},{1,3},{2,0},{3,1},{4,6},{5,7},{6,4},{7,5},{8,10},{9,11},{10,... | collective-permute-start | bytes 98312 | tf_op jit(solution)/shard_map/ppermute | solution.py:341
  27.2 2.4 %collective-permute-start.10 = (bf16[128,128]{1,0:T(8,128)(2,1)S(1)}, bf16[128,128]{1,0:T(8,128)(2,1)S(1)}, u32[]{:S(2)}, u32[]{:S(2)}) collective-permute-start(bf16[128,128]{1,0:T(8,128)(2,1)S(1)} %get-tuple-element.34.refs_0_), channel_id=1, source_target_pairs={{0,1},{1,0},{2,3},{3,2},{4,5},{5,4},{6,7},{7,6},{8,9},{9,8},{10,11... | collective-permute-start | bytes 98312 | tf_op jit(solution)/shard_map/ppermute | solution.py:341
  30.3 6.8 %collective-permute-start.18 = (bf16[240,128]{1,0:T(8,128)(2,1)S(1)}, bf16[240,128]{1,0:T(8,128)(2,1)S(1)}, u32[]{:S(2)}, u32[]{:S(2)}) collective-permute-start(bf16[240,128]{1,0:T(8,128)(2,1)S(1)} %get-tuple-element.37.refs_0_), channel_id=1, source_target_pairs={{0,24},{4,28},{8,16},{12,20},{16,8},{20,12},{24,0},{28,4},{1,25},{... | collective-permute-start | bytes 184328 | tf_op jit(solution)/shard_map/ppermute | solution.py:341
  32.9 7.5 %collective-permute-start.16 = (bf16[240,128]{1,0:T(8,128)(2,1)S(1)}, bf16[240,128]{1,0:T(8,128)(2,1)S(1)}, u32[]{:S(2)}, u32[]{:S(2)}) collective-permute-start(bf16[240,128]{1,0:T(8,128)(2,1)S(1)} %get-tuple-element.37.refs_0_), channel_id=1, source_target_pairs={{0,16},{4,20},{8,24},{12,28},{16,0},{20,4},{24,8},{28,12},{1,17},{... | collective-permute-start | bytes 184328 | tf_op jit(solution)/shard_map/ppermute | solution.py:341
  35.3 6.5 %collective-permute-start.14 = (bf16[240,128]{1,0:T(8,128)(2,1)S(1)}, bf16[240,128]{1,0:T(8,128)(2,1)S(1)}, u32[]{:S(2)}, u32[]{:S(2)}) collective-permute-start(bf16[240,128]{1,0:T(8,128)(2,1)S(1)} %get-tuple-element.37.refs_0_), channel_id=1, source_target_pairs={{0,8},{4,12},{8,0},{12,4},{16,24},{20,28},{24,16},{28,20},{1,9},{5... | collective-permute-start | bytes 184328 | tf_op jit(solution)/shard_map/ppermute | solution.py:341
  35.7 6.8 %collective-permute-start.13 = (bf16[240,128]{1,0:T(8,128)(2,1)S(1)}, bf16[240,128]{1,0:T(8,128)(2,1)S(1)}, u32[]{:S(2)}, u32[]{:S(2)}) collective-permute-start(bf16[240,128]{1,0:T(8,128)(2,1)S(1)} %get-tuple-element.37.refs_0_), channel_id=1, source_target_pairs={{0,4},{4,0},{8,12},{12,8},{16,20},{20,16},{24,28},{28,24},{1,5},{5... | collective-permute-start | bytes 184328 | tf_op jit(solution)/shard_map/ppermute | solution.py:341
  37.2 5.3 %collective-permute-start.19 = (bf16[240,128]{1,0:T(8,128)(2,1)S(1)}, bf16[240,128]{1,0:T(8,128)(2,1)S(1)}, u32[]{:S(2)}, u32[]{:S(2)}) collective-permute-start(bf16[240,128]{1,0:T(8,128)(2,1)S(1)} %collective-permute-done.18.refs_6_), channel_id=1, source_target_pairs={{0,4},{4,0},{8,12},{12,8},{16,20},{20,16},{24,28},{28,24},{1,5},{5... | collective-permute-start | bytes 184328 | tf_op jit(solution)/shard_map/ppermute | solution.py:341
  40.4 4.2 %collective-permute-start.17 = (bf16[240,128]{1,0:T(8,128)(2,1)S(1)}, bf16[240,128]{1,0:T(8,128)(2,1)S(1)}, u32[]{:S(2)}, u32[]{:S(2)}) collective-permute-start(bf16[240,128]{1,0:T(8,128)(2,1)S(1)} %collective-permute-done.16.refs_4_), channel_id=1, source_target_pairs={{0,4},{4,0},{8,12},{12,8},{16,20},{20,16},{24,28},{28,24},{1,5},{5... | collective-permute-start | bytes 184328 | tf_op jit(solution)/shard_map/ppermute | solution.py:341
  41.9 4.2 %collective-permute-start.15 = (bf16[240,128]{1,0:T(8,128)(2,1)S(1)}, bf16[240,128]{1,0:T(8,128)(2,1)S(1)}, u32[]{:S(2)}, u32[]{:S(2)}) collective-permute-start(bf16[240,128]{1,0:T(8,128)(2,1)S(1)} %collective-permute-done.14.refs_2_), channel_id=1, source_target_pairs={{0,4},{4,0},{8,12},{12,8},{16,20},{20,16},{24,28},{28,24},{1,5},{5... | collective-permute-start | bytes 184328 | tf_op jit(solution)/shard_map/ppermute | solution.py:341

commit v3 on v2

--- a/solution.py
+++ b/solution.py
@@ -22,30 +22,33 @@
         self.order, self.columns = order, columns
         self.corners, self.coarse = corners, coarse
         self.neighbors, self.each = neighbors, each
-        self.pairs = (line - 1) * each
+        self.last = line - 1
+        self.pairs = neighbors * each
         self.wide = round_up(self.pairs, 128)
         self.image_at = self.pairs
         self.schur_at = 2 * self.pairs
         self.coarse_at = 3 * self.pairs
-        self.tail = round_up(3 * corners + 8, 16)
+        self.tail = round_up(2 * corners, 16)
         self.first = self.coarse_at + self.tail
         self.input_at = groups * corners
         self.dots_at = self.input_at + corners
         self.second = round_up(self.dots_at + 8, 16)
-        self.sums_at = 2 * self.pairs
+        self.sums_at = self.pairs + 2 * each
         self.third = self.sums_at + 16
         self.spread = round_up(corners, 32)
 
     def served(self):
         return (
-            self.line * self.pairs <= self.coarse
-            and self.line >= 4
+            self.line >= 4
             and self.line & (self.line - 1) == 0
             and self.groups & (self.groups - 1) == 0
+            and self.neighbors == self.line - 2
             and self.each % 16 == 0
             and self.columns == 128
             and self.wide == 128
+            and self.pairs + self.corners <= 128
             and self.corners % 8 == 0
+            and self.corners >= 8
             and 128 % self.spread == 0
             and (self.line * self.spread) % 128 == 0
             and self.order % 128 == 0
@@ -53,15 +56,23 @@
             and self.coarse <= 128 * 256
         )
 
-    def slot(self, a, b):
-        return self.each * ((a ^ b) - 1)
-
-    def others(self, a):
-        return [b for b in range(self.line) if b != a]
+    def slots(self):
+        return range(self.neighbors)
+
+    def rows(self, slot):
+        return slice(self.each * slot, self.each * (slot + 1))
 
 
 def dot(a, b):
     return jnp.dot(a, b, preferred_element_type=F32)
+
+
+def dot_over_rows(a, b):
+    return lax.dot_general(a, b, (((0,), (0,)), ((), ())), preferred_element_type=F32)
+
+
+def dot_over_lanes(a, b):
+    return lax.dot_general(a, b, (((1,), (1,)), ((), ())), preferred_element_type=F32)
 
 
 def split(value):
@@ -69,9 +80,37 @@
     return high, value - high
 
 
+def stack_rows(values, height):
+    row = lax.broadcasted_iota(jnp.int32, (height, 128), 0)
+    stacked = jnp.zeros((height, 128), F32)
+    for at, value in enumerate(values):
+        stacked = jnp.where(row == at, value, stacked)
+    return stacked
+
+
 def whole_weight(place):
     ones = jnp.ones((place.shape[1], 128), BF16)
     return 1.0 - 0.5 * dot(place, ones)
+
+
+def missing_of(plan, tail):
+    at = plan.corners + 2
+    return jnp.broadcast_to(tail[at : at + 1, plan.pairs : plan.pairs + 1], (plan.each, 128))
+
+
+def last_block(plan, missing, blocks):
+    found = jnp.zeros((plan.each, 128), F32)
+    for slot in plan.slots():
+        found = jnp.where(missing == slot + 1.0, blocks(slot), found)
+    return found
+
+
+def gather_pairs(plan, t, missing, blocks, store):
+    far = t ^ plan.last
+    last = last_block(plan, missing[far], functools.partial(blocks, far))
+    for slot in plan.slots():
+        value = blocks(t ^ (slot + 1), slot)
+        store(slot, jnp.where(missing[t] == slot + 1.0, last, value))
 
 
 def prepare_kernel(
@@ -94,6 +133,7 @@
     corner_map,
     rows_pad,
     map_pad,
+    couple_pad,
     arrived,
 ):
     me = lax.axis_index("sub")
@@ -110,6 +150,7 @@
         copy.start()
     rows_pad[...] = jnp.zeros(rows_pad.shape, jnp.int32)
     map_pad[...] = jnp.zeros(map_pad.shape, F32)
+    couple_pad[...] = jnp.zeros(couple_pad.shape, BF16)
     copies[0].wait()
     copies[1].wait()
     for k in range(plan.neighbors):
@@ -120,10 +161,15 @@
         spread = spread + pltpu.roll(spread, reach, 1)
         reach *= 2
     lane = lax.broadcasted_iota(jnp.int32, (1, wide), 1)
-    slots = neighbors[...] ^ me
+    distances = neighbors[...] ^ me
+    missing = jnp.full((1, 1), plan.line * (plan.line - 1) // 2, jnp.int32)
+    for k in range(plan.neighbors):
+        missing = missing - distances[0:1, k : k + 1]
     index = jnp.full((1, wide), -1, jnp.int32)
     for k in range(plan.neighbors):
-        index = jnp.where(lane // each + 1 == slots[0:1, k : k + 1], spread[k : k + 1], index)
+        distance = distances[0:1, k : k + 1]
+        home = jnp.where(distance == plan.last, missing, distance)
+        index = jnp.where(lane // each + 1 == home, spread[k : k + 1], index)
     wide_index = jnp.broadcast_to(index.astype(F32), (wide, wide))
     tall_index = wide_index.T.astype(jnp.int32)
     order_rows = lax.broadcasted_iota(jnp.int32, (plan.order, wide), 0)
@@ -132,51 +178,63 @@
     order_lanes = lax.broadcasted_iota(jnp.int32, (wide, plan.order), 1)
     pick_f = jnp.where(order_lanes == tall_index[:, 0:1], 1.0, 0.0)
     weight_row = 1.0 - 0.5 * jnp.sum(pick_f, axis=0, keepdims=True)
-    pick = pick_f.astype(BF16)
+    pick = pick_f.astype(BF16)[:pairs]
     weight = whole_weight(place_v)
     copies[2].wait()
     corner_ids = corner_map[...]
     map_pad[0:1, 0:corners] = (corner_ids // 128).astype(F32)
     map_pad[1:2, 0:corners] = (corner_ids % 128).astype(F32)
+    map_pad[2:3, :] = jnp.broadcast_to(missing.astype(F32), (1, 128))
+    extra_lane = lax.broadcasted_iota(jnp.int32, (8, 128), 1)
+    extra = jnp.where(extra_lane >= pairs, pltpu.roll(map_pad[...], pairs, 1), 0.0)
     copies[3].wait()
     load = loads[...]
     weighted = (weight * load.astype(F32)).astype(BF16)
-    message[0:pairs, :] = dot(pick, load)[:pairs].astype(BF16)
+    message[0:pairs, :] = dot(pick, load).astype(BF16)
     copies[4].wait()
     couple = coupling_t[...]
     couple_w = (couple.astype(F32) * weight_row).astype(BF16)
-    edge = dot(couple, place_v)
+    room = round_up(corners, 16)
+    padded = couple
+    if room > corners:
+        zeros = jnp.zeros((room - corners, plan.order), F32)
+        padded = jnp.concatenate([couple.astype(F32), zeros], axis=0).astype(BF16)
+    couple_pad[pairs : pairs + room, :] = padded
+    edge = dot_over_lanes(pick, couple_pad[...])
     copies[5].wait()
     image = dot(schur[...], jnp.concatenate([weighted, place_v], axis=1)).astype(BF16)
     first = dot(pick, image)
     first_c = dot(couple_w, image)
-    tail = [first_c[:, :128], 0.5 * first_c[:, 128:], 0.5 * edge, map_pad[...]]
-    if plan.tail > 3 * corners + 8:
-        tail.append(jnp.zeros((plan.tail - 3 * corners - 8, 128), F32))
-    message[plan.image_at : plan.image_at + pairs, :] = first[:pairs, :128].astype(BF16)
-    message[plan.schur_at : plan.schur_at + pairs, :] = (0.5 * first[:pairs, 128:]).astype(BF16)
+    pair_part = 0.5 * first_c[:, 128:]
+    tail = [first_c[:, :128], pair_part[:8] + extra]
+    if corners > 8:
+        tail.append(pair_part[8:])
+    if plan.tail > 2 * corners:
+        tail.append(jnp.zeros((plan.tail - 2 * corners, 128), F32))
+    message[plan.image_at : plan.image_at + pairs, :] = first[:, :128].astype(BF16)
+    message[plan.schur_at : plan.coarse_at, :] = (0.5 * (first[:, 128:] + edge)).astype(BF16)
     message[plan.coarse_at :, :] = jnp.concatenate(tail, axis=0).astype(BF16)
     copies[6].wait()
 
 
 def direction_kernel(plan, *refs):
-    line, each, pairs, corners = plan.line, plan.each, plan.pairs, plan.corners
+    line, pairs, corners = plan.line, plan.pairs, plan.corners
     received, refs = refs[:line], refs[line:]
     coarse_refs, refs = refs[: plan.groups], refs[plan.groups :]
     schur, flexibility, loads, place = refs[:4]
     message, residual, direction, local_part, far_image = refs[4:9]
     moved, images, moved_images, inputs = refs[9:]
-    zero_rows = plan.wide - pairs
+    tails = [block[plan.coarse_at :, :].astype(F32) for block in received]
+    missing = [missing_of(plan, tail) for tail in tails]
     codes = []
     per_tile = 128 // plan.spread
-    lane = lax.broadcasted_iota(jnp.int32, (8, 128), 1)
+    lane = lax.broadcasted_iota(jnp.int32, (1, 128), 1)
     for first in range(0, line, per_tile):
         code = jnp.full((1, 128), -1, jnp.int32)
         for u in range(first, first + per_tile):
-            tail = received[u][plan.coarse_at :, :].astype(F32)
-            pair_of_rows = tail[3 * corners : 3 * corners + 8]
-            number = (128.0 * pair_of_rows[0:1] + pair_of_rows[1:2]).astype(jnp.int32)
-            number = jnp.where(lane[0:1] < corners, number, -1)
+            number = pltpu.roll(tails[u][corners : corners + 8], 128 - pairs, 1)
+            number = (128.0 * number[0:1] + number[1:2]).astype(jnp.int32)
+            number = jnp.where(lane < corners, number, -1)
             code = jnp.maximum(code, pltpu.roll(number, (u - first) * plan.spread, 1))
         codes.append(code)
     codes = jnp.concatenate(codes, axis=1)
@@ -185,26 +243,34 @@
     coarse_all = jnp.concatenate([ref[...] for ref in coarse_refs], axis=0)
     coarse_matrix = dot(coarse_all, chooser).astype(BF16)
 
-    tails = []
+    def loads_block(d, slot):
+        return received[d][plan.rows(slot), :].astype(F32)
+
+    def image_block(d, slot):
+        return images[d, plan.rows(slot), :]
+
+    changes = []
     for t in range(line):
-        for d in plan.others(t):
-            at = plan.slot(t, d)
-            moved[t, at : at + each, :] = received[d][at : at + each, :]
-        if zero_rows:
-            moved[t, pairs:, :] = jnp.zeros((zero_rows, 128), BF16)
+
+        def store_loads(slot, value, t=t):
+            moved[t, plan.rows(slot), :] = value.astype(BF16)
+
+        gather_pairs(plan, t, missing, loads_block, store_loads)
+        if plan.wide > pairs:
+            moved[t, pairs:, :] = jnp.zeros((plan.wide - pairs, 128), BF16)
         result = dot(received[t][plan.schur_at :, :], moved[t])
-        image = received[t][plan.image_at : plan.image_at + pairs, :].astype(F32) - result[:pairs]
-        images[t] = image
-        tails.append(result[pairs + corners : pairs + 2 * corners])
+        image = received[t][plan.image_at : plan.schur_at, :].astype(F32)
+        images[t] = image - result[:pairs]
+        changes.append(result[pairs + corners : pairs + 2 * corners])
     for t in range(line):
-        for d in plan.others(t):
-            at = plan.slot(t, d)
-            moved_images[t, at : at + each, :] = images[d, at : at + each, :]
-        if zero_rows:
-            moved_images[t, pairs:, :] = jnp.zeros((zero_rows, 128), F32)
-        tail = received[t][plan.coarse_at :, :]
-        edge = dot(tail, moved_images[t].astype(BF16))
-        entry = tail.astype(F32)[:corners] - tails[t] - edge[2 * corners : 3 * corners]
+
+        def store_image(slot, value, t=t):
+            moved_images[t, plan.rows(slot), :] = value
+
+        gather_pairs(plan, t, missing, image_block, store_image)
+        coupled = received[t][plan.schur_at : plan.coarse_at, :]
+        edge = dot_over_rows(coupled, moved_images[t].astype(BF16))
+        entry = tails[t][:corners] - changes[t] - edge[pairs : pairs + corners]
         parts = [entry]
         if plan.spread > corners:
             parts.append(jnp.zeros((plan.spread - corners, 128), F32))
@@ -217,19 +283,17 @@
     right = loads[...].astype(F32) - dot(place_v, moved[0])
     image = dot(schur[...], (weight * right).astype(BF16)).astype(BF16)
     mine = moved_images[0]
+    if plan.wide > pairs:
+        mine = jnp.concatenate([mine, jnp.zeros((plan.wide - pairs, 128), F32)], axis=0)
     far_image[...] = mine
     field = weight * (image.astype(F32) - dot(place_v, mine.astype(BF16)))
     residual[...] = right
     direction[...] = field
     local = dot(flexibility[...], field.astype(BF16))
     local_part[...] = local
-    inner_high, inner_low = split(jnp.sum(weight * right * field, axis=0, keepdims=True))
-    square_high, square_low = split(jnp.sum(field * local, axis=0, keepdims=True))
-    row = lax.broadcasted_iota(jnp.int32, (8, 128), 0)
-    dots = jnp.zeros((8, 128), F32)
-    for at, value in enumerate((inner_high, inner_low, square_high, square_low)):
-        dots = jnp.where(row == at, value, dots)
-    parts = [coarse_out, inputs[0][:corners], dots]
+    inner = split(jnp.sum(weight * right * field, axis=0, keepdims=True))
+    square = split(jnp.sum(field * local, axis=0, keepdims=True))
+    parts = [coarse_out, inputs[0][:corners], stack_rows(inner + square, 8)]
     if plan.second > plan.dots_at + 8:
         parts.append(jnp.zeros((plan.second - plan.dots_at - 8, 128), F32))
     message[...] = jnp.concatenate(parts, axis=0).astype(BF16)
@@ -238,8 +302,8 @@
 def surface_kernel(plan, *refs):
     groups, corners, pairs = plan.groups, plan.corners, plan.pairs
     heard = [ref[...].astype(F32) for ref in refs[:groups]]
-    schur, coupling_t, place, local_part = refs[groups : groups + 4]
-    message, surface = refs[groups + 4 :]
+    own_first, schur, coupling_t, place, local_part = refs[groups : groups + 5]
+    surface, messages = refs[groups + 5], refs[groups + 6 :]
     dots = sum(block[plan.dots_at : plan.dots_at + 8] for block in heard)
     inner = dots[0:1] + dots[1:2]
     square = dots[2:3] + dots[3:4]
@@ -254,55 +318,77 @@
             own = value
         entry = heard[m][plan.input_at : plan.input_at + corners]
         square = square + jnp.sum(entry * value.astype(F32), axis=0, keepdims=True)
-    lifted = lax.dot_general(
-        coupling_t[...], own, (((0,), (0,)), ((), ())), preferred_element_type=F32
-    )
-    field = (local_part[...] + lifted).astype(BF16)
+    field = (local_part[...] + dot_over_rows(coupling_t[...], own)).astype(BF16)
     surface[...] = field
     place_v = place[...]
     weight = whole_weight(place_v)
     scaled = (weight * field.astype(F32)).astype(BF16)
     image = dot(schur[...], scaled).astype(BF16)
-    both = lax.dot_general(
-        place_v,
-        jnp.concatenate([field, image], axis=1),
-        (((0,), (0,)), ((), ())),
-        preferred_element_type=F32,
-    )[:pairs]
-    message[0:pairs, :] = both[:, :128].astype(BF16)
-    message[pairs : 2 * pairs, :] = both[:, 128:].astype(BF16)
-    inner_high, inner_low = split(inner)
-    square_high, square_low = split(square)
-    row = lax.broadcasted_iota(jnp.int32, (16, 128), 0)
-    sums = jnp.zeros((16, 128), F32)
-    for at, value in enumerate((inner_high, inner_low, square_high, square_low)):
-        sums = jnp.where(row == at, value, sums)
-    message[plan.sums_at :, :] = sums.astype(BF16)
+    both = dot_over_rows(place_v, jnp.concatenate([field, image], axis=1))[:pairs]
+    surface_part = both[:, :128].astype(BF16)
+    sums = stack_rows(split(inner) + split(square), 16).astype(BF16)
+    missing = missing_of(plan, own_first[plan.coarse_at :, :].astype(F32))
+
+    def image_part(distance):
+        if distance == 0:
+            return jnp.zeros((plan.each, 128), F32)
+        if distance == plan.last:
+            return last_block(plan, missing, lambda slot: image_part(slot + 1))
+        return both[plan.rows(distance - 1), 128:]
+
+    for far, message in zip(range(0, plan.line, 2), messages):
+        message[0:pairs, :] = surface_part
+        message[pairs : pairs + plan.each, :] = image_part(far).astype(BF16)
+        message[pairs + plan.each : plan.sums_at, :] = image_part(far + 1).astype(BF16)
+        message[plan.sums_at :, :] = sums
 
 
 def result_kernel(plan, *refs):
-    line, each, pairs = plan.line, plan.each, plan.pairs
-    received, first, refs = refs[:line], refs[line : 2 * line - 1], refs[2 * line - 1 :]
+    line, pairs, each = plan.line, plan.pairs, plan.each
+    received, first, refs = refs[:line], refs[line : 2 * line], refs[2 * line :]
     far_image, residual, direction, surface, schur, place = refs[:6]
-    solution_out, preconditioned, moved, far_rows = refs[6:]
-    zero_rows = plan.wide - pairs
+    solution_out, preconditioned_out = refs[6:8]
+    moved, far_rows, solved, preconditioned, sent = refs[8:]
     sums = 0.0
     for block in received:
         sums = sums + block[plan.sums_at :, :].astype(F32)
     step = (sums[0:1] + sums[1:2]) / (sums[2:3] + sums[3:4])
+    solved[...] = step * direction[...]
+    solution_copy = pltpu.make_async_copy(solved, solution_out, sent.at[0])
+    solution_copy.start()
+    missing = [missing_of(plan, block[plan.coarse_at :, :].astype(F32)) for block in first]
+
+    def surface_block(d, slot):
+        return received[d][plan.rows(slot), :].astype(F32)
+
+    changes = []
     for t in range(line):
-        for d in plan.others(t):
-            at = plan.slot(t, d)
-            moved[t, at : at + each, :] = received[d][at : at + each, :]
-        if zero_rows:
-            moved[t, pairs:, :] = jnp.zeros((zero_rows, 128), BF16)
-    if zero_rows:
-        far_rows[pairs:, :] = jnp.zeros((zero_rows, 128), F32)
-    for t in range(1, line):
-        at = plan.slot(0, t)
-        block = first[t - 1][plan.schur_at + at : plan.schur_at + at + each, :]
-        image = received[t][pairs + at : pairs + at + each, :].astype(F32)
-        far_rows[at : at + each, :] = image - dot(block, moved[t])
+
+        def store_surface(slot, value, t=t):
+            moved[t, plan.rows(slot), :] = value.astype(BF16)
+
+        gather_pairs(plan, t, missing, surface_block, store_surface)
+        if plan.wide > pairs:
+            moved[t, pairs:, :] = jnp.zeros((plan.wide - pairs, 128), BF16)
+        if t == 0:
+            continue
+
+        def schur_block(slot, t=t):
+            return first[t][plan.schur_at :, :][plan.rows(slot), :].astype(F32)
+
+        if t == plan.last:
+            block = last_block(plan, missing[t], schur_block).astype(BF16)
+        else:
+            block = first[t][plan.schur_at :, :][plan.rows(t - 1), :]
+        at = pairs + each * (t % 2)
+        image = received[t][at : at + each, :].astype(F32)
+        changes.append(image - dot(block, moved[t]))
+    for slot in plan.slots():
+        far_rows[plan.rows(slot), :] = jnp.where(
+            missing[0] == slot + 1.0, changes[plan.last - 1], changes[slot]
+        )
+    if plan.wide > pairs:
+        far_rows[pairs:, :] = jnp.zeros((plan.wide - pairs, 128), F32)
     far = far_image[...] - step * far_rows[...]
     place_v = place[...]
     weight = whole_weight(place_v)
@@ -310,7 +396,10 @@
     remaining = residual[...] - step * operated
     image = dot(schur[...], (weight * remaining).astype(BF16)).astype(BF16)
     preconditioned[...] = weight * (image.astype(F32) - dot(place_v, far.astype(BF16)))
-    solution_out[...] = step * direction[...]
+    last_copy = pltpu.make_async_copy(preconditioned, preconditioned_out, sent.at[1])
+    last_copy.start()
+    solution_copy.wait()
+    last_copy.wait()
 
 
 def line_body(
@@ -325,8 +414,6 @@
     coarse_map,
 ):
     line, order = plan.line, plan.order
-    flex, schur, loads = flexibility[0, 0], dirichlet_schur[0, 0], subdomain_loads[0, 0]
-    coupling_t = coupling[0, 0].T
     coarse = coarse_rows[0, 0]
     rows = jnp.transpose(interface_rows, (0, 2, 1, 3))[0]
     whole = pl.BlockSpec(memory_space=pltpu.VMEM)
@@ -340,27 +427,22 @@
         size = lax.axis_size(axis)
         return lax.ppermute(value, axis, [(at, at ^ distance) for at in range(size)])
 
-    def line_blocks(value, riders=()):
-        blocks = [value] + [None] * (line - 1)
-        moved = []
+    def line_blocks(messages, riders=()):
+        blocks = [messages[0]] + [None] * (line - 1)
+        carried = []
         for far in reversed(range(2, line, 2)):
-            blocks[far] = swap(value, "sub", far)
-        blocks[1] = swap(value, "sub", 1)
+            blocks[far] = swap(messages[far // 2], "sub", far)
+        blocks[1] = swap(messages[0], "sub", 1)
         for far in reversed(range(2, line, 2)):
-            block = blocks[far]
-            if len(moved) < len(riders):
-                rider, distance = riders[len(moved)]
-                block, rider = lax.optimization_barrier((block, rider))
-                moved.append(swap(rider, "grp", distance))
-                blocks[far] = block
-            blocks[far + 1] = swap(block, "sub", 1)
-        for rider, distance in riders[len(moved) :]:
-            moved.append(swap(rider, "grp", distance))
-        return blocks, moved
+            for rider, distance in riders[len(carried) : 0 if far > 2 else None]:
+                blocks[far], rider = lax.optimization_barrier((blocks[far], rider))
+                carried.append(swap(rider, "grp", distance))
+            blocks[far + 1] = swap(blocks[far], "sub", 1)
+        return blocks, carried
 
     lists = (neighbors[0], rows, coarse_map[0])
-    kept = (schur, loads, coupling_t, flex)
-    kept = tuple(pltpu.with_memory_space_constraint(array, pltpu.HBM) for array in kept)
+    kept = (dirichlet_schur[0, 0], subdomain_loads[0, 0], coupling[0, 0].T, flexibility[0, 0])
+    inputs = [pltpu.with_memory_space_constraint(array, pltpu.HBM) for array in lists + kept]
     message, place, schur, loads, coupling_t, flex = pl.pallas_call(
         functools.partial(prepare_kernel, plan),
         out_shape=(shape(plan.first, 128, kind=BF16), shape(order, plan.wide, kind=BF16))
@@ -371,14 +453,15 @@
         + [
             pltpu.VMEM((round_up(plan.neighbors, 8), plan.wide), jnp.int32),
             pltpu.VMEM((8, 128), F32),
+            pltpu.VMEM((plan.wide, order), BF16),
             pltpu.SemaphoreType.DMA((7,)),
         ],
         compiler_params=params,
         name="prepare",
-    )(*lists, *kept)
+    )(*inputs)
     riders = [(coarse, distance) for distance in reversed(range(1, plan.groups))]
-    first, moved = line_blocks(message, riders)
-    coarse_all = [coarse] + moved[::-1]
+    first, carried = line_blocks([message] * (line // 2), riders)
+    coarse_all = [coarse] + carried[::-1]
 
     message, residual, direction, local_part, far_image = pl.pallas_call(
         functools.partial(direction_kernel, plan),
@@ -394,7 +477,7 @@
         scratch_shapes=[
             pltpu.VMEM((line, plan.wide, 128), BF16),
             pltpu.VMEM((line, plan.pairs, 128), F32),
-            pltpu.VMEM((line, plan.wide, 128), F32),
+            pltpu.VMEM((line, plan.pairs, 128), F32),
             pltpu.VMEM((line, plan.spread, 128), F32),
         ],
         compiler_params=params,
@@ -404,28 +487,32 @@
     for step in range(1, plan.groups):
         heard.append(swap(message, "grp", step))
 
-    message, surface = pl.pallas_call(
+    surface, *messages = pl.pallas_call(
         functools.partial(surface_kernel, plan),
-        out_shape=(shape(plan.third, 128, kind=BF16), shape(order, 128, kind=BF16)),
-        in_specs=[whole] * (plan.groups + 4),
-        out_specs=(whole, whole),
+        out_shape=(shape(order, 128, kind=BF16),)
+        + (shape(plan.third, 128, kind=BF16),) * (line // 2),
+        in_specs=[whole] * (plan.groups + 5),
+        out_specs=(whole,) * (1 + line // 2),
         compiler_params=params,
         name="surface",
-    )(*heard, schur, coupling_t, place, local_part)
-    last, _ = line_blocks(message)
+    )(*heard, first[0], schur, coupling_t, place, local_part)
+    last, _ = line_blocks(messages)
 
     solved, preconditioned = pl.pallas_call(
         functools.partial(result_kernel, plan),
         out_shape=(shape(order, 128), shape(order, 128)),
-        in_specs=[whole] * (2 * line + 5),
-        out_specs=(whole, whole),
+        in_specs=[whole] * (2 * line + 6),
+        out_specs=(outside, outside),
         scratch_shapes=[
             pltpu.VMEM((line, plan.wide, 128), BF16),
             pltpu.VMEM((plan.wide, 128), F32),
+            pltpu.VMEM((order, 128), F32),
+            pltpu.VMEM((order, 128), F32),
+            pltpu.SemaphoreType.DMA((2,)),
         ],
         compiler_params=params,
         name="result",
-    )(*last, *first[1:], far_image, residual, direction, surface, schur, place)
+    )(*last, *first, far_image, residual, direction, surface, schur, place)
     return solved[None, None], preconditioned[None, None]
 
 

time: 47.6 us -> 44.7 us (0.939)
  waiting for transfers between devices: 16.4 us -> 14 us
  Pallas kernels: 5.41 us -> 6.18 us
  local copies, waits for them, and re-layouts: 0.67 us -> 0.01 us
    ppermute x20, waiting for transfers between devices: 16.4 us -> 14 us  [swap(): lax.ppermute(value, axis, [(at, at ^ distance) for at in range(size)])]
    unnamed x8 -> x2, local copies, waits for them, and re-layouts: 0.67 us -> 0.01 us
  transfers between devices with their start and end apart: 20 -> 20, of which waited for: 8 -> 9; matrix products, arithmetic and copies ran while one was open for 0% -> 0% of each run, Pallas kernels for 0% -> 0%
where the time goes in v3:
time: 44.7 us; the launch traced here: 44.6 us
  starting transfers between devices  23.8 us (53%)
  waiting for transfers between devices  14 us (31%)
  Pallas kernels  6.18 us (14%)
  between operations  0.68 us (2%)
    ppermute x20, starting transfers between devices, swap(): lax.ppermute(value, axis, [(at, at ^ distance) for at in range(size)])  23.8 us
    ppermute x20, waiting for transfers between devices, swap(): lax.ppermute(value, axis, [(at, at ^ distance) for at in range(size)])  14 us
    pallas_call x1, Pallas kernels, line_body(): pl.pallas_call(functools.partial(prepare_kernel, plan), out_shape=(shape(...  2.34 us
    pallas_call x1, Pallas kernels, line_body(): pl.pallas_call(functools.partial(direction_kernel, plan), out_shape=(shap...  1.68 us
    pallas_call x1, Pallas kernels, line_body(): pl.pallas_call(functools.partial(result_kernel, plan), out_shape=(shape(o...  1.49 us
  transfers between devices with their start and end apart: 20, of which 9 were waited for; matrix products, arithmetic and copies ran while one was open for 0% of the time, Pallas kernels for 0%

profile of v3, /device:TPU:0, one launch (start us, length us, event | category | flops | bytes accessed | tf_op | source)
XLA Modules:
  0.0 44.6 jit_solution(2783256305037931562)
XLA Ops:
  0.6 0.0 copy-start
  0.6 2.3 %prepare.1 = (bf16[336,128]{1,0:T(8,128)(2,1)S(1)}, bf16[512,128]{1,0:T(8,128)(2,1)S(1)}, bf16[512,512]{1,0:T(8,128)(2,1)S(1)}, bf16[512,128]{1,0:T(8,128)(2,1)S...) custom-call(s32[1,6]{1,0:T(1,128)} %bitcast.21, s32[6,1,16]{2,1,0:T(1,128)} %bitcast.20, ...), custom_call_target="tpu_custom_call" | custom-call | tf_op jit(solution)/shard_map/prepare/pallas_call | solution.py:446
  3.0 5.1 %collective-permute-start.5 = (bf16[336,128]{1,0:T(8,128)(2,1)S(1)}, bf16[336,128]{1,0:T(8,128)(2,1)S(1)}, u32[]{:S(2)}, u32[]{:S(2)}) collective-permute-start(bf16[336,128]{1,0:T(8,128)(2,1)S(1)} %get-tuple-element.26.refs_0_.refs_4_.refs_8_), channel_id=1, source_target_pairs={{0,24},{4,28},{8,16},{12,20},{16,8},{20,12},{24,0},{28,4},{1,25},{... | collective-permute-start | bytes 258056 | tf_op jit(solution)/shard_map/ppermute | solution.py:428
  8.1 0.0 collective-permute-start.1
  8.1 0.6 %collective-permute-start.3 = (bf16[336,128]{1,0:T(8,128)(2,1)S(1)}, bf16[336,128]{1,0:T(8,128)(2,1)S(1)}, u32[]{:S(2)}, u32[]{:S(2)}) collective-permute-start(bf16[336,128]{1,0:T(8,128)(2,1)S(1)} %get-tuple-element.26.refs_0_.refs_4_.refs_8_), channel_id=1, source_target_pairs={{0,16},{4,20},{8,24},{12,28},{16,0},{20,4},{24,8},{28,12},{1,17},{... | collective-permute-start | bytes 258056 | tf_op jit(solution)/shard_map/ppermute | solution.py:428
  8.7 1.6 %collective-permute-start = (bf16[336,128]{1,0:T(8,128)(2,1)S(1)}, bf16[336,128]{1,0:T(8,128)(2,1)S(1)}, u32[]{:S(2)}, u32[]{:S(2)}) collective-permute-start(bf16[336,128]{1,0:T(8,128)(2,1)S(1)} %get-tuple-element.26.refs_0_.refs_4_.refs_8_), channel_id=1, source_target_pairs={{0,4},{4,0},{8,12},{12,8},{16,20},{20,16},{24,28},{28,24},{1,5},{5... | collective-permute-start | bytes 258056 | tf_op jit(solution)/shard_map/ppermute | solution.py:428
  10.4 1.2 %collective-permute-done.5.refs_6_.refs_14_ = bf16[336,128]{1,0:T(8,128)(2,1)S(1)} collective-permute-done((bf16[336,128]{1,0:T(8,128)(2,1)S(1)}, bf16[336,128]{1,0:T(8,128)(2,1)S(1)}, u32[]{:S(2)}, u32[]{:S(2)}) %collective-permute-start.5) | collective-permute-done | bytes 86048 | tf_op jit(solution)/shard_map/ppermute | solution.py:428
  11.5 1.6 %collective-permute-start.6 = (bf16[336,128]{1,0:T(8,128)(2,1)S(1)}, bf16[336,128]{1,0:T(8,128)(2,1)S(1)}, u32[]{:S(2)}, u32[]{:S(2)}) collective-permute-start(bf16[336,128]{1,0:T(8,128)(2,1)S(1)} %collective-permute-done.5.refs_6_.refs_14_), channel_id=1, source_target_pairs={{0,4},{4,0},{8,12},{12,8},{16,20},{20,16},{24,28},{28,24},{1,5},{5... | collective-permute-start | bytes 258056 | tf_op jit(solution)/shard_map/ppermute | solution.py:428
  13.1 1.2 %collective-permute-done.1.refs_2_.refs_10_ = bf16[336,128]{1,0:T(8,128)(2,1)S(1)} collective-permute-done((bf16[336,128]{1,0:T(8,128)(2,1)S(1)}, bf16[336,128]{1,0:T(8,128)(2,1)S(1)}, u32[]{:S(2)}, u32[]{:S(2)}) %collective-permute-start.1) | collective-permute-done | bytes 86048 | tf_op jit(solution)/shard_map/ppermute | solution.py:428
  14.3 0.0 copy-done
  14.3 0.0 collective-permute-start.7
  14.3 1.6 %collective-permute-start.8 = (bf16[24,2048]{1,0:T(8,128)(2,1)S(1)}, bf16[24,2048]{1,0:T(8,128)(2,1)S(1)}, u32[]{:S(2)}, u32[]{:S(2)}) collective-permute-start(bf16[24,2048]{1,0:T(8,128)(2,1)S(1)} %bitcast.13), channel_id=1, source_target_pairs={{0,2},{1,3},{2,0},{3,1},{4,6},{5,7},{6,4},{7,5},{8,10},{9,11},{10,... | collective-permute-start | bytes 294920 | tf_op jit(solution)/shard_map/ppermute | solution.py:428
  15.9 0.0 collective-permute-done.3.refs_4_.refs_12_
  15.9 0.2 collective-permute-start.9
  16.2 0.0 collective-permute-done.refs_1_.refs_9_
  16.2 1.6 %collective-permute-start.4 = (bf16[336,128]{1,0:T(8,128)(2,1)S(1)}, bf16[336,128]{1,0:T(8,128)(2,1)S(1)}, u32[]{:S(2)}, u32[]{:S(2)}) collective-permute-start(bf16[336,128]{1,0:T(8,128)(2,1)S(1)} %collective-permute-done.3.refs_4_.refs_12_), channel_id=1, source_target_pairs={{0,4},{4,0},{8,12},{12,8},{16,20},{20,16},{24,28},{28,24},{1,5},{5... | collective-permute-start | bytes 258056 | tf_op jit(solution)/shard_map/ppermute | solution.py:428
  17.8 0.0 collective-permute-done.6.refs_7_.refs_15_
  17.8 0.4 collective-permute-start.2
  18.2 3.4 %collective-permute-done.4.refs_5_.refs_13_ = bf16[336,128]{1,0:T(8,128)(2,1)S(1)} collective-permute-done((bf16[336,128]{1,0:T(8,128)(2,1)S(1)}, bf16[336,128]{1,0:T(8,128)(2,1)S(1)}, u32[]{:S(2)}, u32[]{:S(2)}) %collective-permute-start.4) | collective-permute-done | bytes 86048 | tf_op jit(solution)/shard_map/ppermute | solution.py:428
  21.6 1.7 %collective-permute-done.2.refs_3_.refs_11_ = bf16[336,128]{1,0:T(8,128)(2,1)S(1)} collective-permute-done((bf16[336,128]{1,0:T(8,128)(2,1)S(1)}, bf16[336,128]{1,0:T(8,128)(2,1)S(1)}, u32[]{:S(2)}, u32[]{:S(2)}) %collective-permute-start.2) | collective-permute-done | bytes 86048 | tf_op jit(solution)/shard_map/ppermute | solution.py:428
  23.2 0.0 collective-permute-done.7.refs_9_
  23.2 0.0 collective-permute-done.8.refs_10_
  23.2 0.0 collective-permute-done.9.refs_11_
  23.2 1.7 %direction.1 = (bf16[128,128]{1,0:T(8,128)(2,1)S(1)}, f32[512,128]{1,0:T(8,128)S(1)}, f32[512,128]{1,0:T(8,128)S(1)}, f32[512,128]{1,0:T(8,128)S(1)}, f32[128,128]{1,0:T(8,128)S(1)}) custom-call(bf16[336,128]{1,0:T(8,128)(2,1)S(1)} %get-tuple-element.26.refs_0_.refs_4_.refs_8_, bf16[336,128]{1,0:T(8,128)(2,1)S(1)} %collective-permute-done.refs_1_.refs_9_, ...), custom_call_target="tpu_custom_call" | custom-call | tf_op jit(solution)/shard_map/direction/pallas_call | solution.py:466
  24.9 0.3 collective-permute-start.12
  25.2 1.4 %collective-permute-start.11 = (bf16[128,128]{1,0:T(8,128)(2,1)S(1)}, bf16[128,128]{1,0:T(8,128)(2,1)S(1)}, u32[]{:S(2)}, u32[]{:S(2)}) collective-permute-start(bf16[128,128]{1,0:T(8,128)(2,1)S(1)} %get-tuple-element.37.refs_0_), channel_id=1, source_target_pairs={{0,2},{1,3},{2,0},{3,1},{4,6},{5,7},{6,4},{7,5},{8,10},{9,11},{10,... | collective-permute-start | bytes 98312 | tf_op jit(solution)/shard_map/ppermute | solution.py:428
  26.6 0.3 collective-permute-start.10
  26.9 1.7 %collective-permute-done.12.refs_3_ = bf16[128,128]{1,0:T(8,128)(2,1)S(1)} collective-permute-done((bf16[128,128]{1,0:T(8,128)(2,1)S(1)}, bf16[128,128]{1,0:T(8,128)(2,1)S(1)}, u32[]{:S(2)}, u32[]{:S(2)}) %collective-permute-start.12) | collective-permute-done | bytes 32800 | tf_op jit(solution)/shard_map/ppermute | solution.py:428
  28.6 0.8 %collective-permute-done.11.refs_2_ = bf16[128,128]{1,0:T(8,128)(2,1)S(1)} collective-permute-done((bf16[128,128]{1,0:T(8,128)(2,1)S(1)}, bf16[128,128]{1,0:T(8,128)(2,1)S(1)}, u32[]{:S(2)}, u32[]{:S(2)}) %collective-permute-start.11) | collective-permute-done | bytes 32800 | tf_op jit(solution)/shard_map/ppermute | solution.py:428
  29.4 0.0 collective-permute-done.10.refs_1_
  29.4 0.7 %surface.1 = (bf16[512,128]{1,0:T(8,128)(2,1)S(1)}, bf16[144,128]{1,0:T(8,128)(2,1)S(1)}, bf16[144,128]{1,0:T(8,128)(2,1)S(1)}, bf16[144,128]{1,0:T(8,128)(2,1)S(1)}, bf16[144,128]{1,0:T(8,128)(2,1)S(1)}) custom-call(bf16[128,128]{1,0:T(8,128)(2,1)S(1)} %get-tuple-element.37.refs_0_, bf16[128,128]{1,0:T(8,128)(2,1)S(1)} %collective-permute-done.10.refs_1_, ...), custom_call_target="tpu_custom_call" | custom-call | tf_op jit(solution)/shard_map/surface/pallas_call | solution.py:490
  30.1 0.8 %collective-permute-start.14 = (bf16[144,128]{1,0:T(8,128)(2,1)S(1)}, bf16[144,128]{1,0:T(8,128)(2,1)S(1)}, u32[]{:S(2)}, u32[]{:S(2)}) collective-permute-start(bf16[144,128]{1,0:T(8,128)(2,1)S(1)} %get-tuple-element.41), channel_id=1, source_target_pairs={{0,8},{4,12},{8,0},{12,4},{16,24},{20,28},{24,16},{28,20},{1,9},{5... | collective-permute-start | bytes 110600 | tf_op jit(solution)/shard_map/ppermute | solution.py:428
  30.9 2.5 %collective-permute-start.16 = (bf16[144,128]{1,0:T(8,128)(2,1)S(1)}, bf16[144,128]{1,0:T(8,128)(2,1)S(1)}, u32[]{:S(2)}, u32[]{:S(2)}) collective-permute-start(bf16[144,128]{1,0:T(8,128)(2,1)S(1)} %get-tuple-element.42), channel_id=1, source_target_pairs={{0,16},{4,20},{8,24},{12,28},{16,0},{20,4},{24,8},{28,12},{1,17},{... | collective-permute-start | bytes 110600 | tf_op jit(solution)/shard_map/ppermute | solution.py:428
  33.4 1.2 %collective-permute-start.18 = (bf16[144,128]{1,0:T(8,128)(2,1)S(1)}, bf16[144,128]{1,0:T(8,128)(2,1)S(1)}, u32[]{:S(2)}, u32[]{:S(2)}) collective-permute-start(bf16[144,128]{1,0:T(8,128)(2,1)S(1)} %get-tuple-element.43), channel_id=1, source_target_pairs={{0,24},{4,28},{8,16},{12,20},{16,8},{20,12},{24,0},{28,4},{1,25},{... | collective-permute-start | bytes 110600 | tf_op jit(solution)/shard_map/ppermute | solution.py:428
  34.6 1.5 %collective-permute-start.13 = (bf16[144,128]{1,0:T(8,128)(2,1)S(1)}, bf16[144,128]{1,0:T(8,128)(2,1)S(1)}, u32[]{:S(2)}, u32[]{:S(2)}) collective-permute-start(bf16[144,128]{1,0:T(8,128)(2,1)S(1)} %get-tuple-element.40.refs_0_), channel_id=1, source_target_pairs={{0,4},{4,0},{8,12},{12,8},{16,20},{20,16},{24,28},{28,24},{1,5},{5... | collective-permute-start | bytes 110600 | tf_op jit(solution)/shard_map/ppermute | solution.py:428
  36.0 0.0 collective-permute-done.14.refs_2_
  36.0 0.6 %collective-permute-start.15 = (bf16[144,128]{1,0:T(8,128)(2,1)S(1)}, bf16[144,128]{1,0:T(8,128)(2,1)S(1)}, u32[]{:S(2)}, u32[]{:S(2)}) collective-permute-start(bf16[144,128]{1,0:T(8,128)(2,1)S(1)} %collective-permute-done.14.refs_2_), channel_id=1, source_target_pairs={{0,4},{4,0},{8,12},{12,8},{16,20},{20,16},{24,28},{28,24},{1,5},{5... | collective-permute-start | bytes 110600 | tf_op jit(solution)/shard_map/ppermute | solution.py:428
  36.6 0.0 collective-permute-done.16.refs_4_
  36.6 1.5 %collective-permute-start.17 = (bf16[144,128]{1,0:T(8,128)(2,1)S(1)}, bf16[144,128]{1,0:T(8,128)(2,1)S(1)}, u32[]{:S(2)}, u32[]{:S(2)}) collective-permute-start(bf16[144,128]{1,0:T(8,128)(2,1)S(1)} %collective-permute-done.16.refs_4_), channel_id=1, source_target_pairs={{0,4},{4,0},{8,12},{12,8},{16,20},{20,16},{24,28},{28,24},{1,5},{5... | collective-permute-start | bytes 110600 | tf_op jit(solution)/shard_map/ppermute | solution.py:428
  38.1 1.1 %collective-permute-done.18.refs_6_ = bf16[144,128]{1,0:T(8,128)(2,1)S(1)} collective-permute-done((bf16[144,128]{1,0:T(8,128)(2,1)S(1)}, bf16[144,128]{1,0:T(8,128)(2,1)S(1)}, u32[]{:S(2)}, u32[]{:S(2)}) %collective-permute-start.18) | collective-permute-done | bytes 36896 | tf_op jit(solution)/shard_map/ppermute | solution.py:428
  39.1 1.0 %collective-permute-start.19 = (bf16[144,128]{1,0:T(8,128)(2,1)S(1)}, bf16[144,128]{1,0:T(8,128)(2,1)S(1)}, u32[]{:S(2)}, u32[]{:S(2)}) collective-permute-start(bf16[144,128]{1,0:T(8,128)(2,1)S(1)} %collective-permute-done.18.refs_6_), channel_id=1, source_target_pairs={{0,4},{4,0},{8,12},{12,8},{16,20},{20,16},{24,28},{28,24},{1,5},{5... | collective-permute-start | bytes 110600 | tf_op jit(solution)/shard_map/ppermute | solution.py:428
  40.2 0.0 collective-permute-done.13.refs_1_
  40.2 0.0 collective-permute-done.15.refs_3_
  40.2 0.7 %collective-permute-done.17.refs_5_ = bf16[144,128]{1,0:T(8,128)(2,1)S(1)} collective-permute-done((bf16[144,128]{1,0:T(8,128)(2,1)S(1)}, bf16[144,128]{1,0:T(8,128)(2,1)S(1)}, u32[]{:S(2)}, u32[]{:S(2)}) %collective-permute-start.17) | collective-permute-done | bytes 36896 | tf_op jit(solution)/shard_map/ppermute | solution.py:428
  40.9 2.2 %collective-permute-done.19.refs_7_ = bf16[144,128]{1,0:T(8,128)(2,1)S(1)} collective-permute-done((bf16[144,128]{1,0:T(8,128)(2,1)S(1)}, bf16[144,128]{1,0:T(8,128)(2,1)S(1)}, u32[]{:S(2)}, u32[]{:S(2)}) %collective-permute-start.19) | collective-permute-done | bytes 36896 | tf_op jit(solution)/shard_map/ppermute | solution.py:428
  43.1 1.5 %result.1 = (f32[512,128]{1,0:T(8,128)}, f32[512,128]{1,0:T(8,128)}) custom-call(bf16[144,128]{1,0:T(8,128)(2,1)S(1)} %get-tuple-element.40.refs_0_, bf16[144,128]{1,0:T(8,128)(2,1)S(1)} %collective-permute-done.13.refs_1_, bf16[144,128]{1,0:T(8,128)(2,1)S(1)} %collective-permute-done.14.refs_2_, bf16[144,128]{1,0:T(8,128)(2,1)S(1)} %collective-permute-done.15.refs_3_, ...), custom_call_target="tpu_custom_call" | custom-call | tf_op jit(solution)/shard_map/result/pallas_call | solution.py:501
Async XLA Ops:
  0.6 13.7 %copy-start = (bf16[1,1,24,2048]{3,2,1,0:T(8,128)(2,1)S(1)}, bf16[1,1,24,2048]{3,2,1,0:T(8,128)(2,1)}, u32[]{:S(2)}) copy-start(bf16[1,1,24,2048]{3,2,1,0:T(8,128)(2,1)} %param.12) | copy-start | bytes 294916
  3.0 8.6 %collective-permute-start.5 = (bf16[336,128]{1,0:T(8,128)(2,1)S(1)}, bf16[336,128]{1,0:T(8,128)(2,1)S(1)}, u32[]{:S(2)}, u32[]{:S(2)}) collective-permute-start(bf16[336,128]{1,0:T(8,128)(2,1)S(1)} %get-tuple-element.26.refs_0_.refs_4_.refs_8_), channel_id=1, source_target_pairs={{0,24},{4,28},{8,16},{12,20},{16,8},{20,12},{24,0},{28,4},{1,25},{... | collective-permute-start | bytes 258056 | tf_op jit(solution)/shard_map/ppermute | solution.py:428
  8.1 6.2 %collective-permute-start.1 = (bf16[336,128]{1,0:T(8,128)(2,1)S(1)}, bf16[336,128]{1,0:T(8,128)(2,1)S(1)}, u32[]{:S(2)}, u32[]{:S(2)}) collective-permute-start(bf16[336,128]{1,0:T(8,128)(2,1)S(1)} %get-tuple-element.26.refs_0_.refs_4_.refs_8_), channel_id=1, source_target_pairs={{0,8},{4,12},{8,0},{12,4},{16,24},{20,28},{24,16},{28,20},{1,9},{5... | collective-permute-start | bytes 258056 | tf_op jit(solution)/shard_map/ppermute | solution.py:428
  8.1 7.8 %collective-permute-start.3 = (bf16[336,128]{1,0:T(8,128)(2,1)S(1)}, bf16[336,128]{1,0:T(8,128)(2,1)S(1)}, u32[]{:S(2)}, u32[]{:S(2)}) collective-permute-start(bf16[336,128]{1,0:T(8,128)(2,1)S(1)} %get-tuple-element.26.refs_0_.refs_4_.refs_8_), channel_id=1, source_target_pairs={{0,16},{4,20},{8,24},{12,28},{16,0},{20,4},{24,8},{28,12},{1,17},{... | collective-permute-start | bytes 258056 | tf_op jit(solution)/shard_map/ppermute | solution.py:428
  8.7 7.4 %collective-permute-start = (bf16[336,128]{1,0:T(8,128)(2,1)S(1)}, bf16[336,128]{1,0:T(8,128)(2,1)S(1)}, u32[]{:S(2)}, u32[]{:S(2)}) collective-permute-start(bf16[336,128]{1,0:T(8,128)(2,1)S(1)} %get-tuple-element.26.refs_0_.refs_4_.refs_8_), channel_id=1, source_target_pairs={{0,4},{4,0},{8,12},{12,8},{16,20},{20,16},{24,28},{28,24},{1,5},{5... | collective-permute-start | bytes 258056 | tf_op jit(solution)/shard_map/ppermute | solution.py:428
  11.5 6.2 %collective-permute-start.6 = (bf16[336,128]{1,0:T(8,128)(2,1)S(1)}, bf16[336,128]{1,0:T(8,128)(2,1)S(1)}, u32[]{:S(2)}, u32[]{:S(2)}) collective-permute-start(bf16[336,128]{1,0:T(8,128)(2,1)S(1)} %collective-permute-done.5.refs_6_.refs_14_), channel_id=1, source_target_pairs={{0,4},{4,0},{8,12},{12,8},{16,20},{20,16},{24,28},{28,24},{1,5},{5... | collective-permute-start | bytes 258056 | tf_op jit(solution)/shard_map/ppermute | solution.py:428
  14.3 8.9 %collective-permute-start.7 = (bf16[24,2048]{1,0:T(8,128)(2,1)S(1)}, bf16[24,2048]{1,0:T(8,128)(2,1)S(1)}, u32[]{:S(2)}, u32[]{:S(2)}) collective-permute-start(bf16[24,2048]{1,0:T(8,128)(2,1)S(1)} %bitcast.12), channel_id=1, source_target_pairs={{0,1},{1,0},{2,3},{3,2},{4,5},{5,4},{6,7},{7,6},{8,9},{9,8},{10,11... | collective-permute-start | bytes 294920 | tf_op jit(solution)/shard_map/ppermute | solution.py:428
  14.3 8.9 %collective-permute-start.8 = (bf16[24,2048]{1,0:T(8,128)(2,1)S(1)}, bf16[24,2048]{1,0:T(8,128)(2,1)S(1)}, u32[]{:S(2)}, u32[]{:S(2)}) collective-permute-start(bf16[24,2048]{1,0:T(8,128)(2,1)S(1)} %bitcast.13), channel_id=1, source_target_pairs={{0,2},{1,3},{2,0},{3,1},{4,6},{5,7},{6,4},{7,5},{8,10},{9,11},{10,... | collective-permute-start | bytes 294920 | tf_op jit(solution)/shard_map/ppermute | solution.py:428
  15.9 7.3 %collective-permute-start.9 = (bf16[24,2048]{1,0:T(8,128)(2,1)S(1)}, bf16[24,2048]{1,0:T(8,128)(2,1)S(1)}, u32[]{:S(2)}, u32[]{:S(2)}) collective-permute-start(bf16[24,2048]{1,0:T(8,128)(2,1)S(1)} %bitcast.14), channel_id=1, source_target_pairs={{0,3},{1,2},{2,1},{3,0},{4,7},{5,6},{6,5},{7,4},{8,11},{9,10},{10,... | collective-permute-start | bytes 294920 | tf_op jit(solution)/shard_map/ppermute | solution.py:428
  16.2 5.4 %collective-permute-start.4 = (bf16[336,128]{1,0:T(8,128)(2,1)S(1)}, bf16[336,128]{1,0:T(8,128)(2,1)S(1)}, u32[]{:S(2)}, u32[]{:S(2)}) collective-permute-start(bf16[336,128]{1,0:T(8,128)(2,1)S(1)} %collective-permute-done.3.refs_4_.refs_12_), channel_id=1, source_target_pairs={{0,4},{4,0},{8,12},{12,8},{16,20},{20,16},{24,28},{28,24},{1,5},{5... | collective-permute-start | bytes 258056 | tf_op jit(solution)/shard_map/ppermute | solution.py:428
  17.8 5.5 %collective-permute-start.2 = (bf16[336,128]{1,0:T(8,128)(2,1)S(1)}, bf16[336,128]{1,0:T(8,128)(2,1)S(1)}, u32[]{:S(2)}, u32[]{:S(2)}) collective-permute-start(bf16[336,128]{1,0:T(8,128)(2,1)S(1)} %collective-permute-done.1.refs_2_.refs_10_), channel_id=1, source_target_pairs={{0,4},{4,0},{8,12},{12,8},{16,20},{20,16},{24,28},{28,24},{1,5},{5... | collective-permute-start | bytes 258056 | tf_op jit(solution)/shard_map/ppermute | solution.py:428
  24.9 3.6 %collective-permute-start.12 = (bf16[128,128]{1,0:T(8,128)(2,1)S(1)}, bf16[128,128]{1,0:T(8,128)(2,1)S(1)}, u32[]{:S(2)}, u32[]{:S(2)}) collective-permute-start(bf16[128,128]{1,0:T(8,128)(2,1)S(1)} %get-tuple-element.37.refs_0_), channel_id=1, source_target_pairs={{0,3},{1,2},{2,1},{3,0},{4,7},{5,6},{6,5},{7,4},{8,11},{9,10},{10,... | collective-permute-start | bytes 98312 | tf_op jit(solution)/shard_map/ppermute | solution.py:428
  25.2 4.2 %collective-permute-start.11 = (bf16[128,128]{1,0:T(8,128)(2,1)S(1)}, bf16[128,128]{1,0:T(8,128)(2,1)S(1)}, u32[]{:S(2)}, u32[]{:S(2)}) collective-permute-start(bf16[128,128]{1,0:T(8,128)(2,1)S(1)} %get-tuple-element.37.refs_0_), channel_id=1, source_target_pairs={{0,2},{1,3},{2,0},{3,1},{4,6},{5,7},{6,4},{7,5},{8,10},{9,11},{10,... | collective-permute-start | bytes 98312 | tf_op jit(solution)/shard_map/ppermute | solution.py:428
  26.6 2.9 %collective-permute-start.10 = (bf16[128,128]{1,0:T(8,128)(2,1)S(1)}, bf16[128,128]{1,0:T(8,128)(2,1)S(1)}, u32[]{:S(2)}, u32[]{:S(2)}) collective-permute-start(bf16[128,128]{1,0:T(8,128)(2,1)S(1)} %get-tuple-element.37.refs_0_), channel_id=1, source_target_pairs={{0,1},{1,0},{2,3},{3,2},{4,5},{5,4},{6,7},{7,6},{8,9},{9,8},{10,11... | collective-permute-start | bytes 98312 | tf_op jit(solution)/shard_map/ppermute | solution.py:428
  30.1 5.9 %collective-permute-start.14 = (bf16[144,128]{1,0:T(8,128)(2,1)S(1)}, bf16[144,128]{1,0:T(8,128)(2,1)S(1)}, u32[]{:S(2)}, u32[]{:S(2)}) collective-permute-start(bf16[144,128]{1,0:T(8,128)(2,1)S(1)} %get-tuple-element.41), channel_id=1, source_target_pairs={{0,8},{4,12},{8,0},{12,4},{16,24},{20,28},{24,16},{28,20},{1,9},{5... | collective-permute-start | bytes 110600 | tf_op jit(solution)/shard_map/ppermute | solution.py:428
  30.9 5.7 %collective-permute-start.16 = (bf16[144,128]{1,0:T(8,128)(2,1)S(1)}, bf16[144,128]{1,0:T(8,128)(2,1)S(1)}, u32[]{:S(2)}, u32[]{:S(2)}) collective-permute-start(bf16[144,128]{1,0:T(8,128)(2,1)S(1)} %get-tuple-element.42), channel_id=1, source_target_pairs={{0,16},{4,20},{8,24},{12,28},{16,0},{20,4},{24,8},{28,12},{1,17},{... | collective-permute-start | bytes 110600 | tf_op jit(solution)/shard_map/ppermute | solution.py:428
  33.4 5.8 %collective-permute-start.18 = (bf16[144,128]{1,0:T(8,128)(2,1)S(1)}, bf16[144,128]{1,0:T(8,128)(2,1)S(1)}, u32[]{:S(2)}, u32[]{:S(2)}) collective-permute-start(bf16[144,128]{1,0:T(8,128)(2,1)S(1)} %get-tuple-element.43), channel_id=1, source_target_pairs={{0,24},{4,28},{8,16},{12,20},{16,8},{20,12},{24,0},{28,4},{1,25},{... | collective-permute-start | bytes 110600 | tf_op jit(solution)/shard_map/ppermute | solution.py:428
  34.6 5.6 %collective-permute-start.13 = (bf16[144,128]{1,0:T(8,128)(2,1)S(1)}, bf16[144,128]{1,0:T(8,128)(2,1)S(1)}, u32[]{:S(2)}, u32[]{:S(2)}) collective-permute-start(bf16[144,128]{1,0:T(8,128)(2,1)S(1)} %get-tuple-element.40.refs_0_), channel_id=1, source_target_pairs={{0,4},{4,0},{8,12},{12,8},{16,20},{20,16},{24,28},{28,24},{1,5},{5... | collective-permute-start | bytes 110600 | tf_op jit(solution)/shard_map/ppermute | solution.py:428
  36.0 4.2 %collective-permute-start.15 = (bf16[144,128]{1,0:T(8,128)(2,1)S(1)}, bf16[144,128]{1,0:T(8,128)(2,1)S(1)}, u32[]{:S(2)}, u32[]{:S(2)}) collective-permute-start(bf16[144,128]{1,0:T(8,128)(2,1)S(1)} %collective-permute-done.14.refs_2_), channel_id=1, source_target_pairs={{0,4},{4,0},{8,12},{12,8},{16,20},{20,16},{24,28},{28,24},{1,5},{5... | collective-permute-start | bytes 110600 | tf_op jit(solution)/shard_map/ppermute | solution.py:428
  36.6 4.3 %collective-permute-start.17 = (bf16[144,128]{1,0:T(8,128)(2,1)S(1)}, bf16[144,128]{1,0:T(8,128)(2,1)S(1)}, u32[]{:S(2)}, u32[]{:S(2)}) collective-permute-start(bf16[144,128]{1,0:T(8,128)(2,1)S(1)} %collective-permute-done.16.refs_4_), channel_id=1, source_target_pairs={{0,4},{4,0},{8,12},{12,8},{16,20},{20,16},{24,28},{28,24},{1,5},{5... | collective-permute-start | bytes 110600 | tf_op jit(solution)/shard_map/ppermute | solution.py:428
  39.1 4.0 %collective-permute-start.19 = (bf16[144,128]{1,0:T(8,128)(2,1)S(1)}, bf16[144,128]{1,0:T(8,128)(2,1)S(1)}, u32[]{:S(2)}, u32[]{:S(2)}) collective-permute-start(bf16[144,128]{1,0:T(8,128)(2,1)S(1)} %collective-permute-done.18.refs_6_), channel_id=1, source_target_pairs={{0,4},{4,0},{8,12},{12,8},{16,20},{20,16},{24,28},{28,24},{1,5},{5... | collective-permute-start | bytes 110600 | tf_op jit(solution)/shard_map/ppermute | solution.py:428

commit v4 on v3

--- a/solution.py
+++ b/solution.py
@@ -434,10 +434,10 @@
             blocks[far] = swap(messages[far // 2], "sub", far)
         blocks[1] = swap(messages[0], "sub", 1)
         for far in reversed(range(2, line, 2)):
-            for rider, distance in riders[len(carried) : 0 if far > 2 else None]:
-                blocks[far], rider = lax.optimization_barrier((blocks[far], rider))
-                carried.append(swap(rider, "grp", distance))
             blocks[far + 1] = swap(blocks[far], "sub", 1)
+        for rider, distance in riders:
+            rider = lax.optimization_barrier([rider] + [blocks[k] for k in (1,)])[0]
+            carried.append(swap(rider, "grp", distance))
         return blocks, carried
 
     lists = (neighbors[0], rows, coarse_map[0])

time: 44.7 us -> 43.8 us (0.980)
  waiting for transfers between devices: 14 us -> 13.2 us
    ppermute x20, waiting for transfers between devices: 14 us -> 13.2 us  [swap(): lax.ppermute(value, axis, [(at, at ^ distance) for at in range(size)])]
  transfers between devices with their start and end apart: 20 -> 20, of which waited for: 9 -> 10; matrix products, arithmetic and copies ran while one was open for 0% -> 0% of each run, Pallas kernels for 0% -> 0%
where the time goes in v4:
time: 43.8 us; the launch traced here: 43.6 us
  starting transfers between devices  23.6 us (54%)
  waiting for transfers between devices  13.2 us (30%)
  Pallas kernels  6.17 us (14%)
  between operations  0.68 us (2%)
    ppermute x20, starting transfers between devices, swap(): lax.ppermute(value, axis, [(at, at ^ distance) for at in range(size)])  23.6 us
    ppermute x20, waiting for transfers between devices, swap(): lax.ppermute(value, axis, [(at, at ^ distance) for at in range(size)])  13.2 us
    pallas_call x1, Pallas kernels, line_body(): pl.pallas_call(functools.partial(prepare_kernel, plan), out_shape=(shape(...  2.34 us
    pallas_call x1, Pallas kernels, line_body(): pl.pallas_call(functools.partial(direction_kernel, plan), out_shape=(shap...  1.67 us
    pallas_call x1, Pallas kernels, line_body(): pl.pallas_call(functools.partial(result_kernel, plan), out_shape=(shape(o...  1.49 us
  transfers between devices with their start and end apart: 20, of which 10 were waited for; matrix products, arithmetic and copies ran while one was open for 0% of the time, Pallas kernels for 0%

profile of v4, /device:TPU:0, one launch (start us, length us, event | category | flops | bytes accessed | tf_op | source)
XLA Modules:
  0.0 43.6 jit_solution(9419254062985060962)
XLA Ops:
  0.6 0.0 copy-start
  0.6 2.3 %prepare.1 = (bf16[336,128]{1,0:T(8,128)(2,1)S(1)}, bf16[512,128]{1,0:T(8,128)(2,1)S(1)}, bf16[512,512]{1,0:T(8,128)(2,1)S(1)}, bf16[512,128]{1,0:T(8,128)(2,1)S...) custom-call(s32[1,6]{1,0:T(1,128)} %bitcast.21, s32[6,1,16]{2,1,0:T(1,128)} %bitcast.20, ...), custom_call_target="tpu_custom_call" | custom-call | tf_op jit(solution)/shard_map/prepare/pallas_call | solution.py:446
  3.0 5.1 %collective-permute-start.5 = (bf16[336,128]{1,0:T(8,128)(2,1)S(1)}, bf16[336,128]{1,0:T(8,128)(2,1)S(1)}, u32[]{:S(2)}, u32[]{:S(2)}) collective-permute-start(bf16[336,128]{1,0:T(8,128)(2,1)S(1)} %get-tuple-element.21.refs_0_.refs_4_.refs_8_), channel_id=1, source_target_pairs={{0,24},{4,28},{8,16},{12,20},{16,8},{20,12},{24,0},{28,4},{1,25},{... | collective-permute-start | bytes 258056 | tf_op jit(solution)/shard_map/ppermute | solution.py:428
  8.1 1.5 %collective-permute-start = (bf16[336,128]{1,0:T(8,128)(2,1)S(1)}, bf16[336,128]{1,0:T(8,128)(2,1)S(1)}, u32[]{:S(2)}, u32[]{:S(2)}) collective-permute-start(bf16[336,128]{1,0:T(8,128)(2,1)S(1)} %get-tuple-element.21.refs_0_.refs_4_.refs_8_), channel_id=1, source_target_pairs={{0,4},{4,0},{8,12},{12,8},{16,20},{20,16},{24,28},{28,24},{1,5},{5... | collective-permute-start | bytes 258056 | tf_op jit(solution)/shard_map/ppermute | solution.py:428
  9.6 0.0 collective-permute-start.3
  9.6 0.8 %collective-permute-start.1 = (bf16[336,128]{1,0:T(8,128)(2,1)S(1)}, bf16[336,128]{1,0:T(8,128)(2,1)S(1)}, u32[]{:S(2)}, u32[]{:S(2)}) collective-permute-start(bf16[336,128]{1,0:T(8,128)(2,1)S(1)} %get-tuple-element.21.refs_0_.refs_4_.refs_8_), channel_id=1, source_target_pairs={{0,8},{4,12},{8,0},{12,4},{16,24},{20,28},{24,16},{28,20},{1,9},{5... | collective-permute-start | bytes 258056 | tf_op jit(solution)/shard_map/ppermute | solution.py:428
  10.4 0.6 %collective-permute-done.5.refs_6_.refs_14_ = bf16[336,128]{1,0:T(8,128)(2,1)S(1)} collective-permute-done((bf16[336,128]{1,0:T(8,128)(2,1)S(1)}, bf16[336,128]{1,0:T(8,128)(2,1)S(1)}, u32[]{:S(2)}, u32[]{:S(2)}) %collective-permute-start.5) | collective-permute-done | bytes 86048 | tf_op jit(solution)/shard_map/ppermute | solution.py:428
  10.9 1.8 %collective-permute-start.6 = (bf16[336,128]{1,0:T(8,128)(2,1)S(1)}, bf16[336,128]{1,0:T(8,128)(2,1)S(1)}, u32[]{:S(2)}, u32[]{:S(2)}) collective-permute-start(bf16[336,128]{1,0:T(8,128)(2,1)S(1)} %collective-permute-done.5.refs_6_.refs_14_), channel_id=1, source_target_pairs={{0,4},{4,0},{8,12},{12,8},{16,20},{20,16},{24,28},{28,24},{1,5},{5... | collective-permute-start | bytes 258056 | tf_op jit(solution)/shard_map/ppermute | solution.py:428
  12.8 0.0 collective-permute-done.refs_1_.refs_9_
  12.8 0.0 copy-done
  12.8 0.0 collective-permute-start.9
  12.8 1.8 %collective-permute-start.8 = (bf16[24,2048]{1,0:T(8,128)(2,1)S(1)}, bf16[24,2048]{1,0:T(8,128)(2,1)S(1)}, u32[]{:S(2)}, u32[]{:S(2)}) collective-permute-start(bf16[24,2048]{1,0:T(8,128)(2,1)S(1)} %bitcast.13), channel_id=1, source_target_pairs={{0,2},{1,3},{2,0},{3,1},{4,6},{5,7},{6,4},{7,5},{8,10},{9,11},{10,... | collective-permute-start | bytes 294920 | tf_op jit(solution)/shard_map/ppermute | solution.py:428
  14.6 0.8 %collective-permute-done.3.refs_4_.refs_12_ = bf16[336,128]{1,0:T(8,128)(2,1)S(1)} collective-permute-done((bf16[336,128]{1,0:T(8,128)(2,1)S(1)}, bf16[336,128]{1,0:T(8,128)(2,1)S(1)}, u32[]{:S(2)}, u32[]{:S(2)}) %collective-permute-start.3) | collective-permute-done | bytes 86048 | tf_op jit(solution)/shard_map/ppermute | solution.py:428
  15.3 0.0 collective-permute-start.7
  15.3 0.0 collective-permute-done.1.refs_2_.refs_10_
  15.3 1.5 %collective-permute-start.4 = (bf16[336,128]{1,0:T(8,128)(2,1)S(1)}, bf16[336,128]{1,0:T(8,128)(2,1)S(1)}, u32[]{:S(2)}, u32[]{:S(2)}) collective-permute-start(bf16[336,128]{1,0:T(8,128)(2,1)S(1)} %collective-permute-done.3.refs_4_.refs_12_), channel_id=1, source_target_pairs={{0,4},{4,0},{8,12},{12,8},{16,20},{20,16},{24,28},{28,24},{1,5},{5... | collective-permute-start | bytes 258056 | tf_op jit(solution)/shard_map/ppermute | solution.py:428
  16.8 0.0 collective-permute-done.6.refs_7_.refs_15_
  16.8 0.6 %collective-permute-start.2 = (bf16[336,128]{1,0:T(8,128)(2,1)S(1)}, bf16[336,128]{1,0:T(8,128)(2,1)S(1)}, u32[]{:S(2)}, u32[]{:S(2)}) collective-permute-start(bf16[336,128]{1,0:T(8,128)(2,1)S(1)} %collective-permute-done.1.refs_2_.refs_10_), channel_id=1, source_target_pairs={{0,4},{4,0},{8,12},{12,8},{16,20},{20,16},{24,28},{28,24},{1,5},{5... | collective-permute-start | bytes 258056 | tf_op jit(solution)/shard_map/ppermute | solution.py:428
  17.4 3.3 %collective-permute-done.4.refs_5_.refs_13_ = bf16[336,128]{1,0:T(8,128)(2,1)S(1)} collective-permute-done((bf16[336,128]{1,0:T(8,128)(2,1)S(1)}, bf16[336,128]{1,0:T(8,128)(2,1)S(1)}, u32[]{:S(2)}, u32[]{:S(2)}) %collective-permute-start.4) | collective-permute-done | bytes 86048 | tf_op jit(solution)/shard_map/ppermute | solution.py:428
  20.7 1.5 %collective-permute-done.2.refs_3_.refs_11_ = bf16[336,128]{1,0:T(8,128)(2,1)S(1)} collective-permute-done((bf16[336,128]{1,0:T(8,128)(2,1)S(1)}, bf16[336,128]{1,0:T(8,128)(2,1)S(1)}, u32[]{:S(2)}, u32[]{:S(2)}) %collective-permute-start.2) | collective-permute-done | bytes 86048 | tf_op jit(solution)/shard_map/ppermute | solution.py:428
  22.1 0.0 collective-permute-done.9.refs_11_
  22.1 0.0 collective-permute-done.8.refs_10_
  22.1 0.0 collective-permute-done.7.refs_9_
  22.1 1.7 %direction.1 = (bf16[128,128]{1,0:T(8,128)(2,1)S(1)}, f32[512,128]{1,0:T(8,128)S(1)}, f32[512,128]{1,0:T(8,128)S(1)}, f32[512,128]{1,0:T(8,128)S(1)}, f32[128,128]{1,0:T(8,128)S(1)}) custom-call(bf16[336,128]{1,0:T(8,128)(2,1)S(1)} %get-tuple-element.21.refs_0_.refs_4_.refs_8_, bf16[336,128]{1,0:T(8,128)(2,1)S(1)} %collective-permute-done.refs_1_.refs_9_, ...), custom_call_target="tpu_custom_call" | custom-call | tf_op jit(solution)/shard_map/direction/pallas_call | solution.py:466
  23.8 0.9 %collective-permute-start.12 = (bf16[128,128]{1,0:T(8,128)(2,1)S(1)}, bf16[128,128]{1,0:T(8,128)(2,1)S(1)}, u32[]{:S(2)}, u32[]{:S(2)}) collective-permute-start(bf16[128,128]{1,0:T(8,128)(2,1)S(1)} %get-tuple-element.27.refs_0_), channel_id=1, source_target_pairs={{0,3},{1,2},{2,1},{3,0},{4,7},{5,6},{6,5},{7,4},{8,11},{9,10},{10,... | collective-permute-start | bytes 98312 | tf_op jit(solution)/shard_map/ppermute | solution.py:428
  24.7 0.7 %collective-permute-start.11 = (bf16[128,128]{1,0:T(8,128)(2,1)S(1)}, bf16[128,128]{1,0:T(8,128)(2,1)S(1)}, u32[]{:S(2)}, u32[]{:S(2)}) collective-permute-start(bf16[128,128]{1,0:T(8,128)(2,1)S(1)} %get-tuple-element.27.refs_0_), channel_id=1, source_target_pairs={{0,2},{1,3},{2,0},{3,1},{4,6},{5,7},{6,4},{7,5},{8,10},{9,11},{10,... | collective-permute-start | bytes 98312 | tf_op jit(solution)/shard_map/ppermute | solution.py:428
  25.5 0.3 collective-permute-start.10
  25.7 1.8 %collective-permute-done.12.refs_3_ = bf16[128,128]{1,0:T(8,128)(2,1)S(1)} collective-permute-done((bf16[128,128]{1,0:T(8,128)(2,1)S(1)}, bf16[128,128]{1,0:T(8,128)(2,1)S(1)}, u32[]{:S(2)}, u32[]{:S(2)}) %collective-permute-start.12) | collective-permute-done | bytes 32800 | tf_op jit(solution)/shard_map/ppermute | solution.py:428
  27.5 1.3 %collective-permute-done.11.refs_2_ = bf16[128,128]{1,0:T(8,128)(2,1)S(1)} collective-permute-done((bf16[128,128]{1,0:T(8,128)(2,1)S(1)}, bf16[128,128]{1,0:T(8,128)(2,1)S(1)}, u32[]{:S(2)}, u32[]{:S(2)}) %collective-permute-start.11) | collective-permute-done | bytes 32800 | tf_op jit(solution)/shard_map/ppermute | solution.py:428
  28.8 0.0 collective-permute-done.10.refs_1_
  28.8 0.7 %surface.1 = (bf16[512,128]{1,0:T(8,128)(2,1)S(1)}, bf16[144,128]{1,0:T(8,128)(2,1)S(1)}, bf16[144,128]{1,0:T(8,128)(2,1)S(1)}, bf16[144,128]{1,0:T(8,128)(2,1)S(1)}, bf16[144,128]{1,0:T(8,128)(2,1)S(1)}) custom-call(bf16[128,128]{1,0:T(8,128)(2,1)S(1)} %get-tuple-element.27.refs_0_, bf16[128,128]{1,0:T(8,128)(2,1)S(1)} %collective-permute-done.10.refs_1_, ...), custom_call_target="tpu_custom_call" | custom-call | tf_op jit(solution)/shard_map/surface/pallas_call | solution.py:490
  29.5 1.9 %collective-permute-start.14 = (bf16[144,128]{1,0:T(8,128)(2,1)S(1)}, bf16[144,128]{1,0:T(8,128)(2,1)S(1)}, u32[]{:S(2)}, u32[]{:S(2)}) collective-permute-start(bf16[144,128]{1,0:T(8,128)(2,1)S(1)} %get-tuple-element.31), channel_id=1, source_target_pairs={{0,8},{4,12},{8,0},{12,4},{16,24},{20,28},{24,16},{28,20},{1,9},{5... | collective-permute-start | bytes 110600 | tf_op jit(solution)/shard_map/ppermute | solution.py:428
  31.4 1.1 %collective-permute-start.16 = (bf16[144,128]{1,0:T(8,128)(2,1)S(1)}, bf16[144,128]{1,0:T(8,128)(2,1)S(1)}, u32[]{:S(2)}, u32[]{:S(2)}) collective-permute-start(bf16[144,128]{1,0:T(8,128)(2,1)S(1)} %get-tuple-element.32), channel_id=1, source_target_pairs={{0,16},{4,20},{8,24},{12,28},{16,0},{20,4},{24,8},{28,12},{1,17},{... | collective-permute-start | bytes 110600 | tf_op jit(solution)/shard_map/ppermute | solution.py:428
  32.4 1.5 %collective-permute-start.18 = (bf16[144,128]{1,0:T(8,128)(2,1)S(1)}, bf16[144,128]{1,0:T(8,128)(2,1)S(1)}, u32[]{:S(2)}, u32[]{:S(2)}) collective-permute-start(bf16[144,128]{1,0:T(8,128)(2,1)S(1)} %get-tuple-element.33), channel_id=1, source_target_pairs={{0,24},{4,28},{8,16},{12,20},{16,8},{20,12},{24,0},{28,4},{1,25},{... | collective-permute-start | bytes 110600 | tf_op jit(solution)/shard_map/ppermute | solution.py:428
  33.9 1.5 %collective-permute-start.13 = (bf16[144,128]{1,0:T(8,128)(2,1)S(1)}, bf16[144,128]{1,0:T(8,128)(2,1)S(1)}, u32[]{:S(2)}, u32[]{:S(2)}) collective-permute-start(bf16[144,128]{1,0:T(8,128)(2,1)S(1)} %get-tuple-element.30.refs_0_), channel_id=1, source_target_pairs={{0,4},{4,0},{8,12},{12,8},{16,20},{20,16},{24,28},{28,24},{1,5},{5... | collective-permute-start | bytes 110600 | tf_op jit(solution)/shard_map/ppermute | solution.py:428
  35.4 0.0 collective-permute-done.14.refs_2_
  35.4 0.5 %collective-permute-start.15 = (bf16[144,128]{1,0:T(8,128)(2,1)S(1)}, bf16[144,128]{1,0:T(8,128)(2,1)S(1)}, u32[]{:S(2)}, u32[]{:S(2)}) collective-permute-start(bf16[144,128]{1,0:T(8,128)(2,1)S(1)} %collective-permute-done.14.refs_2_), channel_id=1, source_target_pairs={{0,4},{4,0},{8,12},{12,8},{16,20},{20,16},{24,28},{28,24},{1,5},{5... | collective-permute-start | bytes 110600 | tf_op jit(solution)/shard_map/ppermute | solution.py:428
  36.0 1.2 %collective-permute-done.16.refs_4_ = bf16[144,128]{1,0:T(8,128)(2,1)S(1)} collective-permute-done((bf16[144,128]{1,0:T(8,128)(2,1)S(1)}, bf16[144,128]{1,0:T(8,128)(2,1)S(1)}, u32[]{:S(2)}, u32[]{:S(2)}) %collective-permute-start.16) | collective-permute-done | bytes 36896 | tf_op jit(solution)/shard_map/ppermute | solution.py:428
  37.2 0.3 collective-permute-start.17
  37.5 0.7 %collective-permute-done.18.refs_6_ = bf16[144,128]{1,0:T(8,128)(2,1)S(1)} collective-permute-done((bf16[144,128]{1,0:T(8,128)(2,1)S(1)}, bf16[144,128]{1,0:T(8,128)(2,1)S(1)}, u32[]{:S(2)}, u32[]{:S(2)}) %collective-permute-start.18) | collective-permute-done | bytes 36896 | tf_op jit(solution)/shard_map/ppermute | solution.py:428
  38.2 1.8 %collective-permute-start.19 = (bf16[144,128]{1,0:T(8,128)(2,1)S(1)}, bf16[144,128]{1,0:T(8,128)(2,1)S(1)}, u32[]{:S(2)}, u32[]{:S(2)}) collective-permute-start(bf16[144,128]{1,0:T(8,128)(2,1)S(1)} %collective-permute-done.18.refs_6_), channel_id=1, source_target_pairs={{0,4},{4,0},{8,12},{12,8},{16,20},{20,16},{24,28},{28,24},{1,5},{5... | collective-permute-start | bytes 110600 | tf_op jit(solution)/shard_map/ppermute | solution.py:428
  40.0 0.0 collective-permute-done.13.refs_1_
  40.0 0.0 collective-permute-done.15.refs_3_
  40.1 1.1 %collective-permute-done.17.refs_5_ = bf16[144,128]{1,0:T(8,128)(2,1)S(1)} collective-permute-done((bf16[144,128]{1,0:T(8,128)(2,1)S(1)}, bf16[144,128]{1,0:T(8,128)(2,1)S(1)}, u32[]{:S(2)}, u32[]{:S(2)}) %collective-permute-start.17) | collective-permute-done | bytes 36896 | tf_op jit(solution)/shard_map/ppermute | solution.py:428
  41.1 1.0 %collective-permute-done.19.refs_7_ = bf16[144,128]{1,0:T(8,128)(2,1)S(1)} collective-permute-done((bf16[144,128]{1,0:T(8,128)(2,1)S(1)}, bf16[144,128]{1,0:T(8,128)(2,1)S(1)}, u32[]{:S(2)}, u32[]{:S(2)}) %collective-permute-start.19) | collective-permute-done | bytes 36896 | tf_op jit(solution)/shard_map/ppermute | solution.py:428
  42.2 1.5 %result.1 = (f32[512,128]{1,0:T(8,128)}, f32[512,128]{1,0:T(8,128)}) custom-call(bf16[144,128]{1,0:T(8,128)(2,1)S(1)} %get-tuple-element.30.refs_0_, bf16[144,128]{1,0:T(8,128)(2,1)S(1)} %collective-permute-done.13.refs_1_, bf16[144,128]{1,0:T(8,128)(2,1)S(1)} %collective-permute-done.14.refs_2_, bf16[144,128]{1,0:T(8,128)(2,1)S(1)} %collective-permute-done.15.refs_3_, ...), custom_call_target="tpu_custom_call" | custom-call | tf_op jit(solution)/shard_map/result/pallas_call | solution.py:501
Async XLA Ops:
  0.6 12.2 %copy-start = (bf16[1,1,24,2048]{3,2,1,0:T(8,128)(2,1)S(1)}, bf16[1,1,24,2048]{3,2,1,0:T(8,128)(2,1)}, u32[]{:S(2)}) copy-start(bf16[1,1,24,2048]{3,2,1,0:T(8,128)(2,1)} %param.12) | copy-start | bytes 294916
  3.0 8.0 %collective-permute-start.5 = (bf16[336,128]{1,0:T(8,128)(2,1)S(1)}, bf16[336,128]{1,0:T(8,128)(2,1)S(1)}, u32[]{:S(2)}, u32[]{:S(2)}) collective-permute-start(bf16[336,128]{1,0:T(8,128)(2,1)S(1)} %get-tuple-element.21.refs_0_.refs_4_.refs_8_), channel_id=1, source_target_pairs={{0,24},{4,28},{8,16},{12,20},{16,8},{20,12},{24,0},{28,4},{1,25},{... | collective-permute-start | bytes 258056 | tf_op jit(solution)/shard_map/ppermute | solution.py:428
  8.1 4.7 %collective-permute-start = (bf16[336,128]{1,0:T(8,128)(2,1)S(1)}, bf16[336,128]{1,0:T(8,128)(2,1)S(1)}, u32[]{:S(2)}, u32[]{:S(2)}) collective-permute-start(bf16[336,128]{1,0:T(8,128)(2,1)S(1)} %get-tuple-element.21.refs_0_.refs_4_.refs_8_), channel_id=1, source_target_pairs={{0,4},{4,0},{8,12},{12,8},{16,20},{20,16},{24,28},{28,24},{1,5},{5... | collective-permute-start | bytes 258056 | tf_op jit(solution)/shard_map/ppermute | solution.py:428
  9.6 5.7 %collective-permute-start.3 = (bf16[336,128]{1,0:T(8,128)(2,1)S(1)}, bf16[336,128]{1,0:T(8,128)(2,1)S(1)}, u32[]{:S(2)}, u32[]{:S(2)}) collective-permute-start(bf16[336,128]{1,0:T(8,128)(2,1)S(1)} %get-tuple-element.21.refs_0_.refs_4_.refs_8_), channel_id=1, source_target_pairs={{0,16},{4,20},{8,24},{12,28},{16,0},{20,4},{24,8},{28,12},{1,17},{... | collective-permute-start | bytes 258056 | tf_op jit(solution)/shard_map/ppermute | solution.py:428
  9.6 5.7 %collective-permute-start.1 = (bf16[336,128]{1,0:T(8,128)(2,1)S(1)}, bf16[336,128]{1,0:T(8,128)(2,1)S(1)}, u32[]{:S(2)}, u32[]{:S(2)}) collective-permute-start(bf16[336,128]{1,0:T(8,128)(2,1)S(1)} %get-tuple-element.21.refs_0_.refs_4_.refs_8_), channel_id=1, source_target_pairs={{0,8},{4,12},{8,0},{12,4},{16,24},{20,28},{24,16},{28,20},{1,9},{5... | collective-permute-start | bytes 258056 | tf_op jit(solution)/shard_map/ppermute | solution.py:428
  10.9 5.9 %collective-permute-start.6 = (bf16[336,128]{1,0:T(8,128)(2,1)S(1)}, bf16[336,128]{1,0:T(8,128)(2,1)S(1)}, u32[]{:S(2)}, u32[]{:S(2)}) collective-permute-start(bf16[336,128]{1,0:T(8,128)(2,1)S(1)} %collective-permute-done.5.refs_6_.refs_14_), channel_id=1, source_target_pairs={{0,4},{4,0},{8,12},{12,8},{16,20},{20,16},{24,28},{28,24},{1,5},{5... | collective-permute-start | bytes 258056 | tf_op jit(solution)/shard_map/ppermute | solution.py:428
  12.8 9.3 %collective-permute-start.9 = (bf16[24,2048]{1,0:T(8,128)(2,1)S(1)}, bf16[24,2048]{1,0:T(8,128)(2,1)S(1)}, u32[]{:S(2)}, u32[]{:S(2)}) collective-permute-start(bf16[24,2048]{1,0:T(8,128)(2,1)S(1)} %bitcast.12), channel_id=1, source_target_pairs={{0,3},{1,2},{2,1},{3,0},{4,7},{5,6},{6,5},{7,4},{8,11},{9,10},{10,... | collective-permute-start | bytes 294920 | tf_op jit(solution)/shard_map/ppermute | solution.py:428
  12.8 9.3 %collective-permute-start.8 = (bf16[24,2048]{1,0:T(8,128)(2,1)S(1)}, bf16[24,2048]{1,0:T(8,128)(2,1)S(1)}, u32[]{:S(2)}, u32[]{:S(2)}) collective-permute-start(bf16[24,2048]{1,0:T(8,128)(2,1)S(1)} %bitcast.13), channel_id=1, source_target_pairs={{0,2},{1,3},{2,0},{3,1},{4,6},{5,7},{6,4},{7,5},{8,10},{9,11},{10,... | collective-permute-start | bytes 294920 | tf_op jit(solution)/shard_map/ppermute | solution.py:428
  15.3 6.8 %collective-permute-start.7 = (bf16[24,2048]{1,0:T(8,128)(2,1)S(1)}, bf16[24,2048]{1,0:T(8,128)(2,1)S(1)}, u32[]{:S(2)}, u32[]{:S(2)}) collective-permute-start(bf16[24,2048]{1,0:T(8,128)(2,1)S(1)} %bitcast.14), channel_id=1, source_target_pairs={{0,1},{1,0},{2,3},{3,2},{4,5},{5,4},{6,7},{7,6},{8,9},{9,8},{10,11... | collective-permute-start | bytes 294920 | tf_op jit(solution)/shard_map/ppermute | solution.py:428
  15.3 5.3 %collective-permute-start.4 = (bf16[336,128]{1,0:T(8,128)(2,1)S(1)}, bf16[336,128]{1,0:T(8,128)(2,1)S(1)}, u32[]{:S(2)}, u32[]{:S(2)}) collective-permute-start(bf16[336,128]{1,0:T(8,128)(2,1)S(1)} %collective-permute-done.3.refs_4_.refs_12_), channel_id=1, source_target_pairs={{0,4},{4,0},{8,12},{12,8},{16,20},{20,16},{24,28},{28,24},{1,5},{5... | collective-permute-start | bytes 258056 | tf_op jit(solution)/shard_map/ppermute | solution.py:428
  16.8 5.3 %collective-permute-start.2 = (bf16[336,128]{1,0:T(8,128)(2,1)S(1)}, bf16[336,128]{1,0:T(8,128)(2,1)S(1)}, u32[]{:S(2)}, u32[]{:S(2)}) collective-permute-start(bf16[336,128]{1,0:T(8,128)(2,1)S(1)} %collective-permute-done.1.refs_2_.refs_10_), channel_id=1, source_target_pairs={{0,4},{4,0},{8,12},{12,8},{16,20},{20,16},{24,28},{28,24},{1,5},{5... | collective-permute-start | bytes 258056 | tf_op jit(solution)/shard_map/ppermute | solution.py:428
  23.8 3.7 %collective-permute-start.12 = (bf16[128,128]{1,0:T(8,128)(2,1)S(1)}, bf16[128,128]{1,0:T(8,128)(2,1)S(1)}, u32[]{:S(2)}, u32[]{:S(2)}) collective-permute-start(bf16[128,128]{1,0:T(8,128)(2,1)S(1)} %get-tuple-element.27.refs_0_), channel_id=1, source_target_pairs={{0,3},{1,2},{2,1},{3,0},{4,7},{5,6},{6,5},{7,4},{8,11},{9,10},{10,... | collective-permute-start | bytes 98312 | tf_op jit(solution)/shard_map/ppermute | solution.py:428
  24.7 4.1 %collective-permute-start.11 = (bf16[128,128]{1,0:T(8,128)(2,1)S(1)}, bf16[128,128]{1,0:T(8,128)(2,1)S(1)}, u32[]{:S(2)}, u32[]{:S(2)}) collective-permute-start(bf16[128,128]{1,0:T(8,128)(2,1)S(1)} %get-tuple-element.27.refs_0_), channel_id=1, source_target_pairs={{0,2},{1,3},{2,0},{3,1},{4,6},{5,7},{6,4},{7,5},{8,10},{9,11},{10,... | collective-permute-start | bytes 98312 | tf_op jit(solution)/shard_map/ppermute | solution.py:428
  25.5 3.3 %collective-permute-start.10 = (bf16[128,128]{1,0:T(8,128)(2,1)S(1)}, bf16[128,128]{1,0:T(8,128)(2,1)S(1)}, u32[]{:S(2)}, u32[]{:S(2)}) collective-permute-start(bf16[128,128]{1,0:T(8,128)(2,1)S(1)} %get-tuple-element.27.refs_0_), channel_id=1, source_target_pairs={{0,1},{1,0},{2,3},{3,2},{4,5},{5,4},{6,7},{7,6},{8,9},{9,8},{10,11... | collective-permute-start | bytes 98312 | tf_op jit(solution)/shard_map/ppermute | solution.py:428
  29.5 5.9 %collective-permute-start.14 = (bf16[144,128]{1,0:T(8,128)(2,1)S(1)}, bf16[144,128]{1,0:T(8,128)(2,1)S(1)}, u32[]{:S(2)}, u32[]{:S(2)}) collective-permute-start(bf16[144,128]{1,0:T(8,128)(2,1)S(1)} %get-tuple-element.31), channel_id=1, source_target_pairs={{0,8},{4,12},{8,0},{12,4},{16,24},{20,28},{24,16},{28,20},{1,9},{5... | collective-permute-start | bytes 110600 | tf_op jit(solution)/shard_map/ppermute | solution.py:428
  31.4 5.8 %collective-permute-start.16 = (bf16[144,128]{1,0:T(8,128)(2,1)S(1)}, bf16[144,128]{1,0:T(8,128)(2,1)S(1)}, u32[]{:S(2)}, u32[]{:S(2)}) collective-permute-start(bf16[144,128]{1,0:T(8,128)(2,1)S(1)} %get-tuple-element.32), channel_id=1, source_target_pairs={{0,16},{4,20},{8,24},{12,28},{16,0},{20,4},{24,8},{28,12},{1,17},{... | collective-permute-start | bytes 110600 | tf_op jit(solution)/shard_map/ppermute | solution.py:428
  32.4 5.8 %collective-permute-start.18 = (bf16[144,128]{1,0:T(8,128)(2,1)S(1)}, bf16[144,128]{1,0:T(8,128)(2,1)S(1)}, u32[]{:S(2)}, u32[]{:S(2)}) collective-permute-start(bf16[144,128]{1,0:T(8,128)(2,1)S(1)} %get-tuple-element.33), channel_id=1, source_target_pairs={{0,24},{4,28},{8,16},{12,20},{16,8},{20,12},{24,0},{28,4},{1,25},{... | collective-permute-start | bytes 110600 | tf_op jit(solution)/shard_map/ppermute | solution.py:428
  33.9 6.1 %collective-permute-start.13 = (bf16[144,128]{1,0:T(8,128)(2,1)S(1)}, bf16[144,128]{1,0:T(8,128)(2,1)S(1)}, u32[]{:S(2)}, u32[]{:S(2)}) collective-permute-start(bf16[144,128]{1,0:T(8,128)(2,1)S(1)} %get-tuple-element.30.refs_0_), channel_id=1, source_target_pairs={{0,4},{4,0},{8,12},{12,8},{16,20},{20,16},{24,28},{28,24},{1,5},{5... | collective-permute-start | bytes 110600 | tf_op jit(solution)/shard_map/ppermute | solution.py:428
  35.4 4.6 %collective-permute-start.15 = (bf16[144,128]{1,0:T(8,128)(2,1)S(1)}, bf16[144,128]{1,0:T(8,128)(2,1)S(1)}, u32[]{:S(2)}, u32[]{:S(2)}) collective-permute-start(bf16[144,128]{1,0:T(8,128)(2,1)S(1)} %collective-permute-done.14.refs_2_), channel_id=1, source_target_pairs={{0,4},{4,0},{8,12},{12,8},{16,20},{20,16},{24,28},{28,24},{1,5},{5... | collective-permute-start | bytes 110600 | tf_op jit(solution)/shard_map/ppermute | solution.py:428
  37.2 4.0 %collective-permute-start.17 = (bf16[144,128]{1,0:T(8,128)(2,1)S(1)}, bf16[144,128]{1,0:T(8,128)(2,1)S(1)}, u32[]{:S(2)}, u32[]{:S(2)}) collective-permute-start(bf16[144,128]{1,0:T(8,128)(2,1)S(1)} %collective-permute-done.16.refs_4_), channel_id=1, source_target_pairs={{0,4},{4,0},{8,12},{12,8},{16,20},{20,16},{24,28},{28,24},{1,5},{5... | collective-permute-start | bytes 110600 | tf_op jit(solution)/shard_map/ppermute | solution.py:428
  38.2 4.0 %collective-permute-start.19 = (bf16[144,128]{1,0:T(8,128)(2,1)S(1)}, bf16[144,128]{1,0:T(8,128)(2,1)S(1)}, u32[]{:S(2)}, u32[]{:S(2)}) collective-permute-start(bf16[144,128]{1,0:T(8,128)(2,1)S(1)} %collective-permute-done.18.refs_6_), channel_id=1, source_target_pairs={{0,4},{4,0},{8,12},{12,8},{16,20},{20,16},{24,28},{28,24},{1,5},{5... | collective-permute-start | bytes 110600 | tf_op jit(solution)/shard_map/ppermute | solution.py:428

commit v5 on v4

--- a/solution.py
+++ b/solution.py
@@ -25,11 +25,14 @@
         self.last = line - 1
         self.pairs = neighbors * each
         self.wide = round_up(self.pairs, 128)
+        self.half = self.pairs // 2
+        self.spare = 128 - self.pairs
+        self.map_lane = self.pairs + self.half - self.spare
         self.image_at = self.pairs
         self.schur_at = 2 * self.pairs
-        self.coarse_at = 3 * self.pairs
-        self.tail = round_up(2 * corners, 16)
-        self.first = self.coarse_at + self.tail
+        self.edge_at = self.schur_at + self.half
+        self.coarse_at = self.edge_at + self.half
+        self.first = self.coarse_at + corners
         self.input_at = groups * corners
         self.dots_at = self.input_at + corners
         self.second = round_up(self.dots_at + 8, 16)
@@ -46,9 +49,11 @@
             and self.each % 16 == 0
             and self.columns == 128
             and self.wide == 128
-            and self.pairs + self.corners <= 128
+            and self.pairs % 32 == 0
+            and self.spare <= self.half < 2 * self.spare
+            and 2 * self.corners == self.half
+            and self.corners <= 2 * (128 - self.map_lane)
             and self.corners % 8 == 0
-            and self.corners >= 8
             and 128 % self.spread == 0
             and (self.line * self.spread) % 128 == 0
             and self.order % 128 == 0
@@ -93,9 +98,25 @@
     return 1.0 - 0.5 * dot(place, ones)
 
 
-def missing_of(plan, tail):
-    at = plan.corners + 2
-    return jnp.broadcast_to(tail[at : at + 1, plan.pairs : plan.pairs + 1], (plan.each, 128))
+def extra_rows(plan, values, missing):
+    room = 128 - plan.map_lane
+    lane = lax.broadcasted_iota(jnp.int32, (8, 128), 1)
+    near = pltpu.roll(values, plan.map_lane, 1)
+    far = pltpu.roll(values, plan.map_lane - room, 1)
+    rows = [near[0:1], far[0:1], near[1:2], far[1:2], jnp.broadcast_to(missing, (1, 128))]
+    return jnp.where(lane >= plan.map_lane, stack_rows(rows, 8), 0.0)
+
+
+def map_rows(plan, extra):
+    room = 128 - plan.map_lane
+    lane = lax.broadcasted_iota(jnp.int32, (1, 128), 1)
+    near = pltpu.roll(extra, room, 1)
+    far = pltpu.roll(extra, 2 * room, 1)
+    return [jnp.where(lane < room, near[at : at + 1], far[at + 1 : at + 2]) for at in (0, 2)]
+
+
+def missing_of(plan, extra):
+    return jnp.broadcast_to(extra[4:5, plan.map_lane : plan.map_lane + 1], (plan.each, 128))
 
 
 def last_block(plan, missing, blocks):
@@ -124,6 +145,8 @@
     flexibility_in,
     message,
     place,
+    weight_out,
+    schur_place,
     schur,
     loads,
     coupling_t,
@@ -133,7 +156,6 @@
     corner_map,
     rows_pad,
     map_pad,
-    couple_pad,
     arrived,
 ):
     me = lax.axis_index("sub")
@@ -150,7 +172,6 @@
         copy.start()
     rows_pad[...] = jnp.zeros(rows_pad.shape, jnp.int32)
     map_pad[...] = jnp.zeros(map_pad.shape, F32)
-    couple_pad[...] = jnp.zeros(couple_pad.shape, BF16)
     copies[0].wait()
     copies[1].wait()
     for k in range(plan.neighbors):
@@ -180,40 +201,40 @@
     weight_row = 1.0 - 0.5 * jnp.sum(pick_f, axis=0, keepdims=True)
     pick = pick_f.astype(BF16)[:pairs]
     weight = whole_weight(place_v)
+    weight_out[...] = weight.astype(BF16)
     copies[2].wait()
     corner_ids = corner_map[...]
     map_pad[0:1, 0:corners] = (corner_ids // 128).astype(F32)
     map_pad[1:2, 0:corners] = (corner_ids % 128).astype(F32)
-    map_pad[2:3, :] = jnp.broadcast_to(missing.astype(F32), (1, 128))
-    extra_lane = lax.broadcasted_iota(jnp.int32, (8, 128), 1)
-    extra = jnp.where(extra_lane >= pairs, pltpu.roll(map_pad[...], pairs, 1), 0.0)
+    extra = extra_rows(plan, map_pad[...], missing.astype(F32))
     copies[3].wait()
     load = loads[...]
     weighted = (weight * load.astype(F32)).astype(BF16)
     message[0:pairs, :] = dot(pick, load).astype(BF16)
     copies[4].wait()
     couple = coupling_t[...]
-    couple_w = (couple.astype(F32) * weight_row).astype(BF16)
-    room = round_up(corners, 16)
-    padded = couple
-    if room > corners:
-        zeros = jnp.zeros((room - corners, plan.order), F32)
-        padded = jnp.concatenate([couple.astype(F32), zeros], axis=0).astype(BF16)
-    couple_pad[pairs : pairs + room, :] = padded
-    edge = dot_over_lanes(pick, couple_pad[...])
+    couple_w = couple.astype(F32) * weight_row
+    edge = dot(couple, place_v)
     copies[5].wait()
-    image = dot(schur[...], jnp.concatenate([weighted, place_v], axis=1)).astype(BF16)
-    first = dot(pick, image)
-    first_c = dot(couple_w, image)
-    pair_part = 0.5 * first_c[:, 128:]
-    tail = [first_c[:, :128], pair_part[:8] + extra]
-    if corners > 8:
-        tail.append(pair_part[8:])
-    if plan.tail > 2 * corners:
-        tail.append(jnp.zeros((plan.tail - 2 * corners, 128), F32))
+    image = dot(schur[...], jnp.concatenate([weighted, place_v], axis=1))
+    schur_place[...] = (0.5 * image[:, 128:]).astype(BF16)
+    image = image.astype(BF16)
+    picks = jnp.concatenate([pick_f[:pairs], couple_w], axis=0).astype(BF16)
+    first = dot(picks, image)
+    first, first_c = first[:pairs], first[pairs:]
+    half, spare = plan.half, plan.spare
+    lane = lax.broadcasted_iota(jnp.int32, (half, 128), 1)
+    block = 0.5 * first[:, 128:]
+    upper, quarter = block[:half], block[half:]
+    upper = jnp.where(lane < pairs, upper, pltpu.roll(quarter, pairs - half, 1))
+    coarse_part = 0.5 * jnp.concatenate([first_c[:, 128:], edge], axis=0)
+    rest = jnp.where(lane < plan.map_lane, pltpu.roll(quarter, pairs - half - spare, 1), 0.0)
+    coarse_part = jnp.where(lane < pairs, coarse_part, rest)
+    coarse_part = jnp.concatenate([coarse_part[:8] + extra, coarse_part[8:]], axis=0)
     message[plan.image_at : plan.image_at + pairs, :] = first[:, :128].astype(BF16)
-    message[plan.schur_at : plan.coarse_at, :] = (0.5 * (first[:, 128:] + edge)).astype(BF16)
-    message[plan.coarse_at :, :] = jnp.concatenate(tail, axis=0).astype(BF16)
+    message[plan.schur_at : plan.edge_at, :] = upper.astype(BF16)
+    message[plan.edge_at : plan.coarse_at, :] = coarse_part.astype(BF16)
+    message[plan.coarse_at :, :] = first_c[:, :128].astype(BF16)
     copies[6].wait()
 
 
@@ -221,19 +242,21 @@
     line, pairs, corners = plan.line, plan.pairs, plan.corners
     received, refs = refs[:line], refs[line:]
     coarse_refs, refs = refs[: plan.groups], refs[plan.groups :]
-    schur, flexibility, loads, place = refs[:4]
-    message, residual, direction, local_part, far_image = refs[4:9]
-    moved, images, moved_images, inputs = refs[9:]
-    tails = [block[plan.coarse_at :, :].astype(F32) for block in received]
-    missing = [missing_of(plan, tail) for tail in tails]
+    schur, flexibility, loads, place, weight = refs[:5]
+    message, image_out, direction, local_part, far_image, schur_rows, missing_out = refs[5:12]
+    moved, images, moved_images, inputs, products = refs[12:]
+    half, spare = plan.half, plan.spare
+    extras = [block[plan.edge_at : plan.edge_at + 16, :].astype(F32) for block in received]
+    missing = [missing_of(plan, extra) for extra in extras]
+    missing_out[...] = stack_rows([value[0:1] for value in missing], line)
     codes = []
     per_tile = 128 // plan.spread
     lane = lax.broadcasted_iota(jnp.int32, (1, 128), 1)
     for first in range(0, line, per_tile):
         code = jnp.full((1, 128), -1, jnp.int32)
         for u in range(first, first + per_tile):
-            number = pltpu.roll(tails[u][corners : corners + 8], 128 - pairs, 1)
-            number = (128.0 * number[0:1] + number[1:2]).astype(jnp.int32)
+            high, low = map_rows(plan, extras[u][:8])
+            number = (128.0 * high + low).astype(jnp.int32)
             number = jnp.where(lane < corners, number, -1)
             code = jnp.maximum(code, pltpu.roll(number, (u - first) * plan.spread, 1))
         codes.append(code)
@@ -258,19 +281,33 @@
         gather_pairs(plan, t, missing, loads_block, store_loads)
         if plan.wide > pairs:
             moved[t, pairs:, :] = jnp.zeros((plan.wide - pairs, 128), BF16)
-        result = dot(received[t][plan.schur_at :, :], moved[t])
+        upper = received[t][plan.schur_at : plan.edge_at, :]
+        coarse_part = received[t][plan.edge_at : plan.coarse_at, :]
+        upper_f, coarse_f = upper.astype(F32), coarse_part.astype(F32)
+        blank = jnp.zeros((128 - half, 128), F32)
+        turned = jnp.concatenate([upper_f, blank], axis=0).T[half:pairs]
+        near = pltpu.roll(upper_f, 128 - pairs + half, 1)
+        far = pltpu.roll(coarse_f, 128 - pairs + half + spare, 1)
+        lower = jnp.where(lane < half + spare, near, far)
+        lower = jnp.where(lane < half, turned, jnp.where(lane < pairs, lower, 0.0))
+        products[t, 0:half, :] = upper
+        products[t, half:pairs, :] = lower.astype(BF16)
+        products[t, pairs:, :] = coarse_part
+        result = dot(products[t], moved[t])
         image = received[t][plan.image_at : plan.schur_at, :].astype(F32)
         images[t] = image - result[:pairs]
-        changes.append(result[pairs + corners : pairs + 2 * corners])
+        changes.append(result[pairs : pairs + corners])
     for t in range(line):
 
         def store_image(slot, value, t=t):
             moved_images[t, plan.rows(slot), :] = value
 
         gather_pairs(plan, t, missing, image_block, store_image)
-        coupled = received[t][plan.schur_at : plan.coarse_at, :]
-        edge = dot_over_rows(coupled, moved_images[t].astype(BF16))
-        entry = tails[t][:corners] - changes[t] - edge[pairs : pairs + corners]
+        if plan.wide > pairs:
+            moved_images[t, pairs:, :] = jnp.zeros((plan.wide - pairs, 128), F32)
+        edge = dot(products[t, pairs:, :], moved_images[t].astype(BF16))
+        coarse_part = received[t][plan.coarse_at :, :].astype(F32)
+        entry = coarse_part - changes[t] - edge[corners:]
         parts = [entry]
         if plan.spread > corners:
             parts.append(jnp.zeros((plan.spread - corners, 128), F32))
@@ -279,15 +316,22 @@
     coarse_out = dot(coarse_matrix, coarse_in)
 
     place_v = place[...]
-    weight = whole_weight(place_v)
+    weight = weight[...].astype(F32)
     right = loads[...].astype(F32) - dot(place_v, moved[0])
-    image = dot(schur[...], (weight * right).astype(BF16)).astype(BF16)
+    image = dot(schur[...], (weight * right).astype(BF16))
+    image_out[...] = image
+    image = image.astype(BF16)
+    for t in range(1, line):
+        if t < plan.last:
+            rows = products[t, plan.rows(t - 1), :]
+        else:
+            rows = last_block(
+                plan, missing[t], lambda slot: products[plan.last, plan.rows(slot), :].astype(F32)
+            ).astype(BF16)
+        schur_rows[plan.rows(t - 1), :] = rows
     mine = moved_images[0]
-    if plan.wide > pairs:
-        mine = jnp.concatenate([mine, jnp.zeros((plan.wide - pairs, 128), F32)], axis=0)
     far_image[...] = mine
     field = weight * (image.astype(F32) - dot(place_v, mine.astype(BF16)))
-    residual[...] = right
     direction[...] = field
     local = dot(flexibility[...], field.astype(BF16))
     local_part[...] = local
@@ -302,8 +346,8 @@
 def surface_kernel(plan, *refs):
     groups, corners, pairs = plan.groups, plan.corners, plan.pairs
     heard = [ref[...].astype(F32) for ref in refs[:groups]]
-    own_first, schur, coupling_t, place, local_part = refs[groups : groups + 5]
-    surface, messages = refs[groups + 5], refs[groups + 6 :]
+    missing_rows, schur, coupling_t, place, weight, local_part = refs[groups : groups + 6]
+    image_out, messages = refs[groups + 6], refs[groups + 7 :]
     dots = sum(block[plan.dots_at : plan.dots_at + 8] for block in heard)
     inner = dots[0:1] + dots[1:2]
     square = dots[2:3] + dots[3:4]
@@ -319,15 +363,14 @@
         entry = heard[m][plan.input_at : plan.input_at + corners]
         square = square + jnp.sum(entry * value.astype(F32), axis=0, keepdims=True)
     field = (local_part[...] + dot_over_rows(coupling_t[...], own)).astype(BF16)
-    surface[...] = field
-    place_v = place[...]
-    weight = whole_weight(place_v)
-    scaled = (weight * field.astype(F32)).astype(BF16)
-    image = dot(schur[...], scaled).astype(BF16)
-    both = dot_over_rows(place_v, jnp.concatenate([field, image], axis=1))[:pairs]
+    scaled = (weight[...].astype(F32) * field.astype(F32)).astype(BF16)
+    image = dot(schur[...], scaled)
+    image_out[...] = image
+    both = jnp.concatenate([field, image.astype(BF16)], axis=1)
+    both = dot_over_rows(place[...], both)[:pairs]
     surface_part = both[:, :128].astype(BF16)
     sums = stack_rows(split(inner) + split(square), 16).astype(BF16)
-    missing = missing_of(plan, own_first[plan.coarse_at :, :].astype(F32))
+    missing = jnp.broadcast_to(missing_rows[0:1, :], (plan.each, 128))
 
     def image_part(distance):
         if distance == 0:
@@ -345,10 +388,10 @@
 
 def result_kernel(plan, *refs):
     line, pairs, each = plan.line, plan.pairs, plan.each
-    received, first, refs = refs[:line], refs[line : 2 * line], refs[2 * line :]
-    far_image, residual, direction, surface, schur, place = refs[:6]
-    solution_out, preconditioned_out = refs[6:8]
-    moved, far_rows, solved, preconditioned, sent = refs[8:]
+    received, schur_rows, missing_rows, refs = refs[:line], refs[line], refs[line + 1], refs[line + 2 :]
+    far_image, first_image, direction, surface_image, schur_place, place, weight = refs[:7]
+    solution_out, preconditioned_out = refs[7:9]
+    moved, far_rows, solved, preconditioned, sent = refs[9:]
     sums = 0.0
     for block in received:
         sums = sums + block[plan.sums_at :, :].astype(F32)
@@ -356,7 +399,7 @@
     solved[...] = step * direction[...]
     solution_copy = pltpu.make_async_copy(solved, solution_out, sent.at[0])
     solution_copy.start()
-    missing = [missing_of(plan, block[plan.coarse_at :, :].astype(F32)) for block in first]
+    missing = [jnp.broadcast_to(missing_rows[t : t + 1, :], (each, 128)) for t in range(line)]
 
     def surface_block(d, slot):
         return received[d][plan.rows(slot), :].astype(F32)
@@ -373,13 +416,7 @@
         if t == 0:
             continue
 
-        def schur_block(slot, t=t):
-            return first[t][plan.schur_at :, :][plan.rows(slot), :].astype(F32)
-
-        if t == plan.last:
-            block = last_block(plan, missing[t], schur_block).astype(BF16)
-        else:
-            block = first[t][plan.schur_at :, :][plan.rows(t - 1), :]
+        block = schur_rows[plan.rows(t - 1), :]
         at = pairs + each * (t % 2)
         image = received[t][at : at + each, :].astype(F32)
         changes.append(image - dot(block, moved[t]))
@@ -390,12 +427,9 @@
     if plan.wide > pairs:
         far_rows[pairs:, :] = jnp.zeros((plan.wide - pairs, 128), F32)
     far = far_image[...] - step * far_rows[...]
-    place_v = place[...]
-    weight = whole_weight(place_v)
-    operated = surface[...].astype(F32) - dot(place_v, moved[0])
-    remaining = residual[...] - step * operated
-    image = dot(schur[...], (weight * remaining).astype(BF16)).astype(BF16)
-    preconditioned[...] = weight * (image.astype(F32) - dot(place_v, far.astype(BF16)))
+    change = surface_image[...] - dot(schur_place[...], moved[0])
+    remaining = first_image[...] - step * change - dot(place[...], far.astype(BF16))
+    preconditioned[...] = weight[...].astype(F32) * remaining
     last_copy = pltpu.make_async_copy(preconditioned, preconditioned_out, sent.at[1])
     last_copy.start()
     solution_copy.wait()
@@ -443,17 +477,21 @@
     lists = (neighbors[0], rows, coarse_map[0])
     kept = (dirichlet_schur[0, 0], subdomain_loads[0, 0], coupling[0, 0].T, flexibility[0, 0])
     inputs = [pltpu.with_memory_space_constraint(array, pltpu.HBM) for array in lists + kept]
-    message, place, schur, loads, coupling_t, flex = pl.pallas_call(
+    message, place, weight, schur_place, schur, loads, coupling_t, flex = pl.pallas_call(
         functools.partial(prepare_kernel, plan),
-        out_shape=(shape(plan.first, 128, kind=BF16), shape(order, plan.wide, kind=BF16))
+        out_shape=(
+            shape(plan.first, 128, kind=BF16),
+            shape(order, plan.wide, kind=BF16),
+            shape(order, 128, kind=BF16),
+            shape(order, plan.wide, kind=BF16),
+        )
         + tuple(shape(*array.shape, kind=BF16) for array in kept),
         in_specs=[outside] * 7,
-        out_specs=(whole,) * 6,
+        out_specs=(whole,) * 8,
         scratch_shapes=[pltpu.VMEM(array.shape, array.dtype) for array in lists]
         + [
             pltpu.VMEM((round_up(plan.neighbors, 8), plan.wide), jnp.int32),
             pltpu.VMEM((8, 128), F32),
-            pltpu.VMEM((plan.wide, order), BF16),
             pltpu.SemaphoreType.DMA((7,)),
         ],
         compiler_params=params,
@@ -463,7 +501,7 @@
     first, carried = line_blocks([message] * (line // 2), riders)
     coarse_all = [coarse] + carried[::-1]
 
-    message, residual, direction, local_part, far_image = pl.pallas_call(
+    message, image, direction, local_part, far_image, schur_rows, missing = pl.pallas_call(
         functools.partial(direction_kernel, plan),
         out_shape=(
             shape(plan.second, 128, kind=BF16),
@@ -471,37 +509,40 @@
             shape(order, 128),
             shape(order, 128),
             shape(plan.wide, 128),
+            shape(plan.each * (line - 1), 128, kind=BF16),
+            shape(line, 128),
         ),
-        in_specs=[whole] * (line + plan.groups + 4),
-        out_specs=(whole,) * 5,
+        in_specs=[whole] * (line + plan.groups + 5),
+        out_specs=(whole,) * 7,
         scratch_shapes=[
             pltpu.VMEM((line, plan.wide, 128), BF16),
             pltpu.VMEM((line, plan.pairs, 128), F32),
-            pltpu.VMEM((line, plan.pairs, 128), F32),
+            pltpu.VMEM((line, plan.wide, 128), F32),
             pltpu.VMEM((line, plan.spread, 128), F32),
+            pltpu.VMEM((line, plan.pairs + plan.half, 128), BF16),
         ],
         compiler_params=params,
         name="direction",
-    )(*first, *coarse_all, schur, flex, loads, place)
+    )(*first, *coarse_all, schur, flex, loads, place, weight)
     heard = [message]
     for step in range(1, plan.groups):
         heard.append(swap(message, "grp", step))
 
-    surface, *messages = pl.pallas_call(
+    surface_image, *messages = pl.pallas_call(
         functools.partial(surface_kernel, plan),
-        out_shape=(shape(order, 128, kind=BF16),)
+        out_shape=(shape(order, 128),)
         + (shape(plan.third, 128, kind=BF16),) * (line // 2),
-        in_specs=[whole] * (plan.groups + 5),
+        in_specs=[whole] * (plan.groups + 6),
         out_specs=(whole,) * (1 + line // 2),
         compiler_params=params,
         name="surface",
-    )(*heard, first[0], schur, coupling_t, place, local_part)
+    )(*heard, missing, schur, coupling_t, place, weight, local_part)
     last, _ = line_blocks(messages)
 
     solved, preconditioned = pl.pallas_call(
         functools.partial(result_kernel, plan),
         out_shape=(shape(order, 128), shape(order, 128)),
-        in_specs=[whole] * (2 * line + 6),
+        in_specs=[whole] * (line + 9),
         out_specs=(outside, outside),
         scratch_shapes=[
             pltpu.VMEM((line, plan.wide, 128), BF16),
@@ -512,7 +553,7 @@
         ],
         compiler_params=params,
         name="result",
-    )(*last, *first, far_image, residual, direction, surface, schur, place)
+    )(*last, schur_rows, missing, far_image, image, direction, surface_image, schur_place, place, weight)
     return solved[None, None], preconditioned[None, None]
 
 

time: 43.8 us -> 43 us (0.982)
  starting transfers between devices: 23.6 us -> 22.1 us
  waiting for transfers between devices: 13.2 us -> 14.2 us
    ppermute x20, starting transfers between devices: 23.6 us -> 22.1 us  [swap(): lax.ppermute(value, axis, [(at, at ^ distance) for at in range(size)])]
    ppermute x20, waiting for transfers between devices: 13.2 us -> 14.2 us  [swap(): lax.ppermute(value, axis, [(at, at ^ distance) for at in range(size)])]
  transfers between devices with their start and end apart: 20 -> 20, of which waited for: 10 -> 12; matrix products, arithmetic and copies ran while one was open for 0% -> 0% of each run, Pallas kernels for 0% -> 0%
where the time goes in v5:
time: 43 us; the launch traced here: 42.9 us
  starting transfers between devices  22.1 us (51%)
  waiting for transfers between devices  14.2 us (33%)
  Pallas kernels  5.82 us (14%)
  between operations  0.68 us (2%)
    ppermute x20, starting transfers between devices, swap(): lax.ppermute(value, axis, [(at, at ^ distance) for at in range(size)])  22.1 us
    ppermute x20, waiting for transfers between devices, swap(): lax.ppermute(value, axis, [(at, at ^ distance) for at in range(size)])  14.2 us
    pallas_call x1, Pallas kernels, line_body(): pl.pallas_call(functools.partial(prepare_kernel, plan), out_shape=(shape(...  2.21 us
    pallas_call x1, Pallas kernels, line_body(): pl.pallas_call(functools.partial(direction_kernel, plan), out_shape=(shap...  1.76 us
    pallas_call x1, Pallas kernels, line_body(): pl.pallas_call(functools.partial(result_kernel, plan), out_shape=(shape(o...  1.17 us
  transfers between devices with their start and end apart: 20, of which 12 were waited for; matrix products, arithmetic and copies ran while one was open for 0% of the time, Pallas kernels for 0%

profile of v5, /device:TPU:0, one launch (start us, length us, event | category | flops | bytes accessed | tf_op | source)
XLA Modules:
  0.0 42.9 jit_solution(18331520616788761962)
XLA Ops:
  0.6 0.0 copy-start
  0.6 2.2 %prepare.1 = (bf16[312,128]{1,0:T(8,128)(2,1)S(1)}, bf16[512,128]{1,0:T(8,128)(2,1)S(1)}, bf16[512,128]{1,0:T(8,128)(2,1)S(1)}, bf16[512,128]{1,0:T(8,128)(2,1)S...) custom-call(s32[1,6]{1,0:T(1,128)} %bitcast.21, ...), custom_call_target="tpu_custom_call" | custom-call | tf_op jit(solution)/shard_map/prepare/pallas_call | solution.py:480
  2.9 5.1 %collective-permute-start.5 = (bf16[312,128]{1,0:T(8,128)(2,1)S(1)}, bf16[312,128]{1,0:T(8,128)(2,1)S(1)}, u32[]{:S(2)}, u32[]{:S(2)}) collective-permute-start(bf16[312,128]{1,0:T(8,128)(2,1)S(1)} %get-tuple-element.25.refs_0_), channel_id=1, source_target_pairs={{0,24},{4,28},{8,16},{12,20},{16,8},{20,12},{24,0},{28,4},{1,25},{... | collective-permute-start | bytes 239624 | tf_op jit(solution)/shard_map/ppermute | solution.py:462
  8.0 1.5 %collective-permute-start = (bf16[312,128]{1,0:T(8,128)(2,1)S(1)}, bf16[312,128]{1,0:T(8,128)(2,1)S(1)}, u32[]{:S(2)}, u32[]{:S(2)}) collective-permute-start(bf16[312,128]{1,0:T(8,128)(2,1)S(1)} %get-tuple-element.25.refs_0_), channel_id=1, source_target_pairs={{0,4},{4,0},{8,12},{12,8},{16,20},{20,16},{24,28},{28,24},{1,5},{5... | collective-permute-start | bytes 239624 | tf_op jit(solution)/shard_map/ppermute | solution.py:462
  9.5 0.0 collective-permute-start.3
  9.5 0.8 %collective-permute-start.1 = (bf16[312,128]{1,0:T(8,128)(2,1)S(1)}, bf16[312,128]{1,0:T(8,128)(2,1)S(1)}, u32[]{:S(2)}, u32[]{:S(2)}) collective-permute-start(bf16[312,128]{1,0:T(8,128)(2,1)S(1)} %get-tuple-element.25.refs_0_), channel_id=1, source_target_pairs={{0,8},{4,12},{8,0},{12,4},{16,24},{20,28},{24,16},{28,20},{1,9},{5... | collective-permute-start | bytes 239624 | tf_op jit(solution)/shard_map/ppermute | solution.py:462
  10.2 0.4 %collective-permute-done.5.refs_6_ = bf16[312,128]{1,0:T(8,128)(2,1)S(1)} collective-permute-done((bf16[312,128]{1,0:T(8,128)(2,1)S(1)}, bf16[312,128]{1,0:T(8,128)(2,1)S(1)}, u32[]{:S(2)}, u32[]{:S(2)}) %collective-permute-start.5) | collective-permute-done | bytes 79904 | tf_op jit(solution)/shard_map/ppermute | solution.py:462
  10.7 1.8 %collective-permute-start.6 = (bf16[312,128]{1,0:T(8,128)(2,1)S(1)}, bf16[312,128]{1,0:T(8,128)(2,1)S(1)}, u32[]{:S(2)}, u32[]{:S(2)}) collective-permute-start(bf16[312,128]{1,0:T(8,128)(2,1)S(1)} %collective-permute-done.5.refs_6_), channel_id=1, source_target_pairs={{0,4},{4,0},{8,12},{12,8},{16,20},{20,16},{24,28},{28,24},{1,5},{5... | collective-permute-start | bytes 239624 | tf_op jit(solution)/shard_map/ppermute | solution.py:462
  12.5 0.3 collective-permute-done.refs_1_
  12.9 0.0 copy-done
  12.9 0.0 collective-permute-start.9
  12.9 1.5 %collective-permute-start.8 = (bf16[24,2048]{1,0:T(8,128)(2,1)S(1)}, bf16[24,2048]{1,0:T(8,128)(2,1)S(1)}, u32[]{:S(2)}, u32[]{:S(2)}) collective-permute-start(bf16[24,2048]{1,0:T(8,128)(2,1)S(1)} %bitcast.13), channel_id=1, source_target_pairs={{0,2},{1,3},{2,0},{3,1},{4,6},{5,7},{6,4},{7,5},{8,10},{9,11},{10,... | collective-permute-start | bytes 294920 | tf_op jit(solution)/shard_map/ppermute | solution.py:462
  14.4 0.5 %collective-permute-done.3.refs_4_ = bf16[312,128]{1,0:T(8,128)(2,1)S(1)} collective-permute-done((bf16[312,128]{1,0:T(8,128)(2,1)S(1)}, bf16[312,128]{1,0:T(8,128)(2,1)S(1)}, u32[]{:S(2)}, u32[]{:S(2)}) %collective-permute-start.3) | collective-permute-done | bytes 79904 | tf_op jit(solution)/shard_map/ppermute | solution.py:462
  14.9 0.0 collective-permute-start.7
  14.9 0.0 collective-permute-done.1.refs_2_
  14.9 1.3 %collective-permute-start.4 = (bf16[312,128]{1,0:T(8,128)(2,1)S(1)}, bf16[312,128]{1,0:T(8,128)(2,1)S(1)}, u32[]{:S(2)}, u32[]{:S(2)}) collective-permute-start(bf16[312,128]{1,0:T(8,128)(2,1)S(1)} %collective-permute-done.3.refs_4_), channel_id=1, source_target_pairs={{0,4},{4,0},{8,12},{12,8},{16,20},{20,16},{24,28},{28,24},{1,5},{5... | collective-permute-start | bytes 239624 | tf_op jit(solution)/shard_map/ppermute | solution.py:462
  16.2 0.0 collective-permute-done.6.refs_7_
  16.2 0.7 %collective-permute-start.2 = (bf16[312,128]{1,0:T(8,128)(2,1)S(1)}, bf16[312,128]{1,0:T(8,128)(2,1)S(1)}, u32[]{:S(2)}, u32[]{:S(2)}) collective-permute-start(bf16[312,128]{1,0:T(8,128)(2,1)S(1)} %collective-permute-done.1.refs_2_), channel_id=1, source_target_pairs={{0,4},{4,0},{8,12},{12,8},{16,20},{20,16},{24,28},{28,24},{1,5},{5... | collective-permute-start | bytes 239624 | tf_op jit(solution)/shard_map/ppermute | solution.py:462
  17.0 3.2 %collective-permute-done.4.refs_5_ = bf16[312,128]{1,0:T(8,128)(2,1)S(1)} collective-permute-done((bf16[312,128]{1,0:T(8,128)(2,1)S(1)}, bf16[312,128]{1,0:T(8,128)(2,1)S(1)}, u32[]{:S(2)}, u32[]{:S(2)}) %collective-permute-start.4) | collective-permute-done | bytes 79904 | tf_op jit(solution)/shard_map/ppermute | solution.py:462
  20.1 1.3 %collective-permute-done.2.refs_3_ = bf16[312,128]{1,0:T(8,128)(2,1)S(1)} collective-permute-done((bf16[312,128]{1,0:T(8,128)(2,1)S(1)}, bf16[312,128]{1,0:T(8,128)(2,1)S(1)}, u32[]{:S(2)}, u32[]{:S(2)}) %collective-permute-start.2) | collective-permute-done | bytes 79904 | tf_op jit(solution)/shard_map/ppermute | solution.py:462
  21.4 0.0 collective-permute-done.9.refs_11_
  21.4 0.0 collective-permute-done.8.refs_10_
  21.5 0.0 collective-permute-done.7.refs_9_
  21.5 1.8 %direction.1 = (bf16[128,128]{1,0:T(8,128)(2,1)S(1)}, f32[512,128]{1,0:T(8,128)S(1)}, f32[512,128]{1,0:T(8,128)S(1)}, f32[512,128]{1,0:T(8,128)S(1)}, f32[128,12...) custom-call(bf16[312,128]{1,0:T(8,128)(2,1)S(1)} %get-tuple-element.25.refs_0_, ...), custom_call_target="tpu_custom_call" | custom-call | tf_op jit(solution)/shard_map/direction/pallas_call | solution.py:504
  23.2 0.9 %collective-permute-start.12 = (bf16[128,128]{1,0:T(8,128)(2,1)S(1)}, bf16[128,128]{1,0:T(8,128)(2,1)S(1)}, u32[]{:S(2)}, u32[]{:S(2)}) collective-permute-start(bf16[128,128]{1,0:T(8,128)(2,1)S(1)} %get-tuple-element.32.refs_0_), channel_id=1, source_target_pairs={{0,3},{1,2},{2,1},{3,0},{4,7},{5,6},{6,5},{7,4},{8,11},{9,10},{10,... | collective-permute-start | bytes 98312 | tf_op jit(solution)/shard_map/ppermute | solution.py:462
  24.1 0.7 %collective-permute-start.11 = (bf16[128,128]{1,0:T(8,128)(2,1)S(1)}, bf16[128,128]{1,0:T(8,128)(2,1)S(1)}, u32[]{:S(2)}, u32[]{:S(2)}) collective-permute-start(bf16[128,128]{1,0:T(8,128)(2,1)S(1)} %get-tuple-element.32.refs_0_), channel_id=1, source_target_pairs={{0,2},{1,3},{2,0},{3,1},{4,6},{5,7},{6,4},{7,5},{8,10},{9,11},{10,... | collective-permute-start | bytes 98312 | tf_op jit(solution)/shard_map/ppermute | solution.py:462
  24.9 0.3 collective-permute-start.10
  25.1 1.8 %collective-permute-done.12.refs_3_ = bf16[128,128]{1,0:T(8,128)(2,1)S(1)} collective-permute-done((bf16[128,128]{1,0:T(8,128)(2,1)S(1)}, bf16[128,128]{1,0:T(8,128)(2,1)S(1)}, u32[]{:S(2)}, u32[]{:S(2)}) %collective-permute-start.12) | collective-permute-done | bytes 32800 | tf_op jit(solution)/shard_map/ppermute | solution.py:462
  26.9 1.3 %collective-permute-done.11.refs_2_ = bf16[128,128]{1,0:T(8,128)(2,1)S(1)} collective-permute-done((bf16[128,128]{1,0:T(8,128)(2,1)S(1)}, bf16[128,128]{1,0:T(8,128)(2,1)S(1)}, u32[]{:S(2)}, u32[]{:S(2)}) %collective-permute-start.11) | collective-permute-done | bytes 32800 | tf_op jit(solution)/shard_map/ppermute | solution.py:462
  28.2 0.0 collective-permute-done.10.refs_1_
  28.2 0.7 %surface.1 = (f32[512,128]{1,0:T(8,128)S(1)}, bf16[144,128]{1,0:T(8,128)(2,1)S(1)}, bf16[144,128]{1,0:T(8,128)(2,1)S(1)}, bf16[144,128]{1,0:T(8,128)(2,1)S(1)}, bf16[144,128]{1,0:T(8,128)(2,1)S(1)}) custom-call(bf16[128,128]{1,0:T(8,128)(2,1)S(1)} %get-tuple-element.32.refs_0_, bf16[128,128]{1,0:T(8,128)(2,1)S(1)} %collective-permute-done.10.refs_1_, ...), custom_call_target="tpu_custom_call" | custom-call | tf_op jit(solution)/shard_map/surface/pallas_call | solution.py:531
  28.9 1.5 %collective-permute-start.14 = (bf16[144,128]{1,0:T(8,128)(2,1)S(1)}, bf16[144,128]{1,0:T(8,128)(2,1)S(1)}, u32[]{:S(2)}, u32[]{:S(2)}) collective-permute-start(bf16[144,128]{1,0:T(8,128)(2,1)S(1)} %get-tuple-element.37), channel_id=1, source_target_pairs={{0,8},{4,12},{8,0},{12,4},{16,24},{20,28},{24,16},{28,20},{1,9},{5... | collective-permute-start | bytes 110600 | tf_op jit(solution)/shard_map/ppermute | solution.py:462
  30.5 1.5 %collective-permute-start.16 = (bf16[144,128]{1,0:T(8,128)(2,1)S(1)}, bf16[144,128]{1,0:T(8,128)(2,1)S(1)}, u32[]{:S(2)}, u32[]{:S(2)}) collective-permute-start(bf16[144,128]{1,0:T(8,128)(2,1)S(1)} %get-tuple-element.38), channel_id=1, source_target_pairs={{0,16},{4,20},{8,24},{12,28},{16,0},{20,4},{24,8},{28,12},{1,17},{... | collective-permute-start | bytes 110600 | tf_op jit(solution)/shard_map/ppermute | solution.py:462
  32.0 1.4 %collective-permute-start.18 = (bf16[144,128]{1,0:T(8,128)(2,1)S(1)}, bf16[144,128]{1,0:T(8,128)(2,1)S(1)}, u32[]{:S(2)}, u32[]{:S(2)}) collective-permute-start(bf16[144,128]{1,0:T(8,128)(2,1)S(1)} %get-tuple-element.39), channel_id=1, source_target_pairs={{0,24},{4,28},{8,16},{12,20},{16,8},{20,12},{24,0},{28,4},{1,25},{... | collective-permute-start | bytes 110600 | tf_op jit(solution)/shard_map/ppermute | solution.py:462
  33.4 1.2 %collective-permute-start.13 = (bf16[144,128]{1,0:T(8,128)(2,1)S(1)}, bf16[144,128]{1,0:T(8,128)(2,1)S(1)}, u32[]{:S(2)}, u32[]{:S(2)}) collective-permute-start(bf16[144,128]{1,0:T(8,128)(2,1)S(1)} %get-tuple-element.36.refs_0_), channel_id=1, source_target_pairs={{0,4},{4,0},{8,12},{12,8},{16,20},{20,16},{24,28},{28,24},{1,5},{5... | collective-permute-start | bytes 110600 | tf_op jit(solution)/shard_map/ppermute | solution.py:462
  34.6 0.0 collective-permute-done.14.refs_2_
  34.6 0.8 %collective-permute-start.15 = (bf16[144,128]{1,0:T(8,128)(2,1)S(1)}, bf16[144,128]{1,0:T(8,128)(2,1)S(1)}, u32[]{:S(2)}, u32[]{:S(2)}) collective-permute-start(bf16[144,128]{1,0:T(8,128)(2,1)S(1)} %collective-permute-done.14.refs_2_), channel_id=1, source_target_pairs={{0,4},{4,0},{8,12},{12,8},{16,20},{20,16},{24,28},{28,24},{1,5},{5... | collective-permute-start | bytes 110600 | tf_op jit(solution)/shard_map/ppermute | solution.py:462
  35.4 1.1 %collective-permute-done.16.refs_4_ = bf16[144,128]{1,0:T(8,128)(2,1)S(1)} collective-permute-done((bf16[144,128]{1,0:T(8,128)(2,1)S(1)}, bf16[144,128]{1,0:T(8,128)(2,1)S(1)}, u32[]{:S(2)}, u32[]{:S(2)}) %collective-permute-start.16) | collective-permute-done | bytes 36896 | tf_op jit(solution)/shard_map/ppermute | solution.py:462
  36.5 0.2 collective-permute-start.17
  36.6 1.1 %collective-permute-done.18.refs_6_ = bf16[144,128]{1,0:T(8,128)(2,1)S(1)} collective-permute-done((bf16[144,128]{1,0:T(8,128)(2,1)S(1)}, bf16[144,128]{1,0:T(8,128)(2,1)S(1)}, u32[]{:S(2)}, u32[]{:S(2)}) %collective-permute-start.18) | collective-permute-done | bytes 36896 | tf_op jit(solution)/shard_map/ppermute | solution.py:462
  37.7 0.8 %collective-permute-start.19 = (bf16[144,128]{1,0:T(8,128)(2,1)S(1)}, bf16[144,128]{1,0:T(8,128)(2,1)S(1)}, u32[]{:S(2)}, u32[]{:S(2)}) collective-permute-start(bf16[144,128]{1,0:T(8,128)(2,1)S(1)} %collective-permute-done.18.refs_6_), channel_id=1, source_target_pairs={{0,4},{4,0},{8,12},{12,8},{16,20},{20,16},{24,28},{28,24},{1,5},{5... | collective-permute-start | bytes 110600 | tf_op jit(solution)/shard_map/ppermute | solution.py:462
  38.5 0.0 collective-permute-done.13.refs_1_
  38.5 0.1 collective-permute-done.15.refs_3_
  38.6 1.9 %collective-permute-done.17.refs_5_ = bf16[144,128]{1,0:T(8,128)(2,1)S(1)} collective-permute-done((bf16[144,128]{1,0:T(8,128)(2,1)S(1)}, bf16[144,128]{1,0:T(8,128)(2,1)S(1)}, u32[]{:S(2)}, u32[]{:S(2)}) %collective-permute-start.17) | collective-permute-done | bytes 36896 | tf_op jit(solution)/shard_map/ppermute | solution.py:462
  40.4 1.3 %collective-permute-done.19.refs_7_ = bf16[144,128]{1,0:T(8,128)(2,1)S(1)} collective-permute-done((bf16[144,128]{1,0:T(8,128)(2,1)S(1)}, bf16[144,128]{1,0:T(8,128)(2,1)S(1)}, u32[]{:S(2)}, u32[]{:S(2)}) %collective-permute-start.19) | collective-permute-done | bytes 36896 | tf_op jit(solution)/shard_map/ppermute | solution.py:462
  41.7 1.2 %result.1 = (f32[512,128]{1,0:T(8,128)}, f32[512,128]{1,0:T(8,128)}) custom-call(bf16[144,128]{1,0:T(8,128)(2,1)S(1)} %get-tuple-element.36.refs_0_, bf16[144,128]{1,0:T(8,128)(2,1)S(1)} %collective-permute-done.13.refs_1_, bf16[144,128]{1,0:T(8,128)(2,1)S(1)} %collective-permute-done.14.refs_2_, bf16[144,128]{1,0:T(8,128)(2,1)S(1)} %collective-permute-done.15.refs_3_, ...), custom_call_target="tpu_custom_call" | custom-call | tf_op jit(solution)/shard_map/result/pallas_call | solution.py:542
Async XLA Ops:
  0.6 12.2 %copy-start = (bf16[1,1,24,2048]{3,2,1,0:T(8,128)(2,1)S(1)}, bf16[1,1,24,2048]{3,2,1,0:T(8,128)(2,1)}, u32[]{:S(2)}) copy-start(bf16[1,1,24,2048]{3,2,1,0:T(8,128)(2,1)} %param.12) | copy-start | bytes 294916
  2.9 7.8 %collective-permute-start.5 = (bf16[312,128]{1,0:T(8,128)(2,1)S(1)}, bf16[312,128]{1,0:T(8,128)(2,1)S(1)}, u32[]{:S(2)}, u32[]{:S(2)}) collective-permute-start(bf16[312,128]{1,0:T(8,128)(2,1)S(1)} %get-tuple-element.25.refs_0_), channel_id=1, source_target_pairs={{0,24},{4,28},{8,16},{12,20},{16,8},{20,12},{24,0},{28,4},{1,25},{... | collective-permute-start | bytes 239624 | tf_op jit(solution)/shard_map/ppermute | solution.py:462
  8.0 4.9 %collective-permute-start = (bf16[312,128]{1,0:T(8,128)(2,1)S(1)}, bf16[312,128]{1,0:T(8,128)(2,1)S(1)}, u32[]{:S(2)}, u32[]{:S(2)}) collective-permute-start(bf16[312,128]{1,0:T(8,128)(2,1)S(1)} %get-tuple-element.25.refs_0_), channel_id=1, source_target_pairs={{0,4},{4,0},{8,12},{12,8},{16,20},{20,16},{24,28},{28,24},{1,5},{5... | collective-permute-start | bytes 239624 | tf_op jit(solution)/shard_map/ppermute | solution.py:462
  9.5 5.5 %collective-permute-start.3 = (bf16[312,128]{1,0:T(8,128)(2,1)S(1)}, bf16[312,128]{1,0:T(8,128)(2,1)S(1)}, u32[]{:S(2)}, u32[]{:S(2)}) collective-permute-start(bf16[312,128]{1,0:T(8,128)(2,1)S(1)} %get-tuple-element.25.refs_0_), channel_id=1, source_target_pairs={{0,16},{4,20},{8,24},{12,28},{16,0},{20,4},{24,8},{28,12},{1,17},{... | collective-permute-start | bytes 239624 | tf_op jit(solution)/shard_map/ppermute | solution.py:462
  9.5 5.5 %collective-permute-start.1 = (bf16[312,128]{1,0:T(8,128)(2,1)S(1)}, bf16[312,128]{1,0:T(8,128)(2,1)S(1)}, u32[]{:S(2)}, u32[]{:S(2)}) collective-permute-start(bf16[312,128]{1,0:T(8,128)(2,1)S(1)} %get-tuple-element.25.refs_0_), channel_id=1, source_target_pairs={{0,8},{4,12},{8,0},{12,4},{16,24},{20,28},{24,16},{28,20},{1,9},{5... | collective-permute-start | bytes 239624 | tf_op jit(solution)/shard_map/ppermute | solution.py:462
  10.7 5.5 %collective-permute-start.6 = (bf16[312,128]{1,0:T(8,128)(2,1)S(1)}, bf16[312,128]{1,0:T(8,128)(2,1)S(1)}, u32[]{:S(2)}, u32[]{:S(2)}) collective-permute-start(bf16[312,128]{1,0:T(8,128)(2,1)S(1)} %collective-permute-done.5.refs_6_), channel_id=1, source_target_pairs={{0,4},{4,0},{8,12},{12,8},{16,20},{20,16},{24,28},{28,24},{1,5},{5... | collective-permute-start | bytes 239624 | tf_op jit(solution)/shard_map/ppermute | solution.py:462
  12.9 8.6 %collective-permute-start.9 = (bf16[24,2048]{1,0:T(8,128)(2,1)S(1)}, bf16[24,2048]{1,0:T(8,128)(2,1)S(1)}, u32[]{:S(2)}, u32[]{:S(2)}) collective-permute-start(bf16[24,2048]{1,0:T(8,128)(2,1)S(1)} %bitcast.12), channel_id=1, source_target_pairs={{0,3},{1,2},{2,1},{3,0},{4,7},{5,6},{6,5},{7,4},{8,11},{9,10},{10,... | collective-permute-start | bytes 294920 | tf_op jit(solution)/shard_map/ppermute | solution.py:462
  12.9 8.6 %collective-permute-start.8 = (bf16[24,2048]{1,0:T(8,128)(2,1)S(1)}, bf16[24,2048]{1,0:T(8,128)(2,1)S(1)}, u32[]{:S(2)}, u32[]{:S(2)}) collective-permute-start(bf16[24,2048]{1,0:T(8,128)(2,1)S(1)} %bitcast.13), channel_id=1, source_target_pairs={{0,2},{1,3},{2,0},{3,1},{4,6},{5,7},{6,4},{7,5},{8,10},{9,11},{10,... | collective-permute-start | bytes 294920 | tf_op jit(solution)/shard_map/ppermute | solution.py:462
  14.9 6.5 %collective-permute-start.7 = (bf16[24,2048]{1,0:T(8,128)(2,1)S(1)}, bf16[24,2048]{1,0:T(8,128)(2,1)S(1)}, u32[]{:S(2)}, u32[]{:S(2)}) collective-permute-start(bf16[24,2048]{1,0:T(8,128)(2,1)S(1)} %bitcast.14), channel_id=1, source_target_pairs={{0,1},{1,0},{2,3},{3,2},{4,5},{5,4},{6,7},{7,6},{8,9},{9,8},{10,11... | collective-permute-start | bytes 294920 | tf_op jit(solution)/shard_map/ppermute | solution.py:462
  14.9 5.2 %collective-permute-start.4 = (bf16[312,128]{1,0:T(8,128)(2,1)S(1)}, bf16[312,128]{1,0:T(8,128)(2,1)S(1)}, u32[]{:S(2)}, u32[]{:S(2)}) collective-permute-start(bf16[312,128]{1,0:T(8,128)(2,1)S(1)} %collective-permute-done.3.refs_4_), channel_id=1, source_target_pairs={{0,4},{4,0},{8,12},{12,8},{16,20},{20,16},{24,28},{28,24},{1,5},{5... | collective-permute-start | bytes 239624 | tf_op jit(solution)/shard_map/ppermute | solution.py:462
  16.2 5.2 %collective-permute-start.2 = (bf16[312,128]{1,0:T(8,128)(2,1)S(1)}, bf16[312,128]{1,0:T(8,128)(2,1)S(1)}, u32[]{:S(2)}, u32[]{:S(2)}) collective-permute-start(bf16[312,128]{1,0:T(8,128)(2,1)S(1)} %collective-permute-done.1.refs_2_), channel_id=1, source_target_pairs={{0,4},{4,0},{8,12},{12,8},{16,20},{20,16},{24,28},{28,24},{1,5},{5... | collective-permute-start | bytes 239624 | tf_op jit(solution)/shard_map/ppermute | solution.py:462
  23.2 3.7 %collective-permute-start.12 = (bf16[128,128]{1,0:T(8,128)(2,1)S(1)}, bf16[128,128]{1,0:T(8,128)(2,1)S(1)}, u32[]{:S(2)}, u32[]{:S(2)}) collective-permute-start(bf16[128,128]{1,0:T(8,128)(2,1)S(1)} %get-tuple-element.32.refs_0_), channel_id=1, source_target_pairs={{0,3},{1,2},{2,1},{3,0},{4,7},{5,6},{6,5},{7,4},{8,11},{9,10},{10,... | collective-permute-start | bytes 98312 | tf_op jit(solution)/shard_map/ppermute | solution.py:462
  24.1 4.1 %collective-permute-start.11 = (bf16[128,128]{1,0:T(8,128)(2,1)S(1)}, bf16[128,128]{1,0:T(8,128)(2,1)S(1)}, u32[]{:S(2)}, u32[]{:S(2)}) collective-permute-start(bf16[128,128]{1,0:T(8,128)(2,1)S(1)} %get-tuple-element.32.refs_0_), channel_id=1, source_target_pairs={{0,2},{1,3},{2,0},{3,1},{4,6},{5,7},{6,4},{7,5},{8,10},{9,11},{10,... | collective-permute-start | bytes 98312 | tf_op jit(solution)/shard_map/ppermute | solution.py:462
  24.9 3.3 %collective-permute-start.10 = (bf16[128,128]{1,0:T(8,128)(2,1)S(1)}, bf16[128,128]{1,0:T(8,128)(2,1)S(1)}, u32[]{:S(2)}, u32[]{:S(2)}) collective-permute-start(bf16[128,128]{1,0:T(8,128)(2,1)S(1)} %get-tuple-element.32.refs_0_), channel_id=1, source_target_pairs={{0,1},{1,0},{2,3},{3,2},{4,5},{5,4},{6,7},{7,6},{8,9},{9,8},{10,11... | collective-permute-start | bytes 98312 | tf_op jit(solution)/shard_map/ppermute | solution.py:462
  28.9 5.7 %collective-permute-start.14 = (bf16[144,128]{1,0:T(8,128)(2,1)S(1)}, bf16[144,128]{1,0:T(8,128)(2,1)S(1)}, u32[]{:S(2)}, u32[]{:S(2)}) collective-permute-start(bf16[144,128]{1,0:T(8,128)(2,1)S(1)} %get-tuple-element.37), channel_id=1, source_target_pairs={{0,8},{4,12},{8,0},{12,4},{16,24},{20,28},{24,16},{28,20},{1,9},{5... | collective-permute-start | bytes 110600 | tf_op jit(solution)/shard_map/ppermute | solution.py:462
  30.5 6.0 %collective-permute-start.16 = (bf16[144,128]{1,0:T(8,128)(2,1)S(1)}, bf16[144,128]{1,0:T(8,128)(2,1)S(1)}, u32[]{:S(2)}, u32[]{:S(2)}) collective-permute-start(bf16[144,128]{1,0:T(8,128)(2,1)S(1)} %get-tuple-element.38), channel_id=1, source_target_pairs={{0,16},{4,20},{8,24},{12,28},{16,0},{20,4},{24,8},{28,12},{1,17},{... | collective-permute-start | bytes 110600 | tf_op jit(solution)/shard_map/ppermute | solution.py:462
  32.0 5.8 %collective-permute-start.18 = (bf16[144,128]{1,0:T(8,128)(2,1)S(1)}, bf16[144,128]{1,0:T(8,128)(2,1)S(1)}, u32[]{:S(2)}, u32[]{:S(2)}) collective-permute-start(bf16[144,128]{1,0:T(8,128)(2,1)S(1)} %get-tuple-element.39), channel_id=1, source_target_pairs={{0,24},{4,28},{8,16},{12,20},{16,8},{20,12},{24,0},{28,4},{1,25},{... | collective-permute-start | bytes 110600 | tf_op jit(solution)/shard_map/ppermute | solution.py:462
  33.4 5.1 %collective-permute-start.13 = (bf16[144,128]{1,0:T(8,128)(2,1)S(1)}, bf16[144,128]{1,0:T(8,128)(2,1)S(1)}, u32[]{:S(2)}, u32[]{:S(2)}) collective-permute-start(bf16[144,128]{1,0:T(8,128)(2,1)S(1)} %get-tuple-element.36.refs_0_), channel_id=1, source_target_pairs={{0,4},{4,0},{8,12},{12,8},{16,20},{20,16},{24,28},{28,24},{1,5},{5... | collective-permute-start | bytes 110600 | tf_op jit(solution)/shard_map/ppermute | solution.py:462
  34.6 4.0 %collective-permute-start.15 = (bf16[144,128]{1,0:T(8,128)(2,1)S(1)}, bf16[144,128]{1,0:T(8,128)(2,1)S(1)}, u32[]{:S(2)}, u32[]{:S(2)}) collective-permute-start(bf16[144,128]{1,0:T(8,128)(2,1)S(1)} %collective-permute-done.14.refs_2_), channel_id=1, source_target_pairs={{0,4},{4,0},{8,12},{12,8},{16,20},{20,16},{24,28},{28,24},{1,5},{5... | collective-permute-start | bytes 110600 | tf_op jit(solution)/shard_map/ppermute | solution.py:462
  36.5 4.0 %collective-permute-start.17 = (bf16[144,128]{1,0:T(8,128)(2,1)S(1)}, bf16[144,128]{1,0:T(8,128)(2,1)S(1)}, u32[]{:S(2)}, u32[]{:S(2)}) collective-permute-start(bf16[144,128]{1,0:T(8,128)(2,1)S(1)} %collective-permute-done.16.refs_4_), channel_id=1, source_target_pairs={{0,4},{4,0},{8,12},{12,8},{16,20},{20,16},{24,28},{28,24},{1,5},{5... | collective-permute-start | bytes 110600 | tf_op jit(solution)/shard_map/ppermute | solution.py:462
  37.7 4.0 %collective-permute-start.19 = (bf16[144,128]{1,0:T(8,128)(2,1)S(1)}, bf16[144,128]{1,0:T(8,128)(2,1)S(1)}, u32[]{:S(2)}, u32[]{:S(2)}) collective-permute-start(bf16[144,128]{1,0:T(8,128)(2,1)S(1)} %collective-permute-done.18.refs_6_), channel_id=1, source_target_pairs={{0,4},{4,0},{8,12},{12,8},{16,20},{20,16},{24,28},{28,24},{1,5},{5... | collective-permute-start | bytes 110600 | tf_op jit(solution)/shard_map/ppermute | solution.py:462

commit v6 on v5

--- a/solution.py
+++ b/solution.py
@@ -146,7 +146,8 @@
     message,
     place,
     weight_out,
-    schur_place,
+    pairs_out,
+    image_out,
     schur,
     loads,
     coupling_t,
@@ -217,7 +218,9 @@
     edge = dot(couple, place_v)
     copies[5].wait()
     image = dot(schur[...], jnp.concatenate([weighted, place_v], axis=1))
-    schur_place[...] = (0.5 * image[:, 128:]).astype(BF16)
+    pairs_out[:, :128] = (weight * (0.5 * image[:, 128:])).astype(BF16)
+    pairs_out[:, 128:] = (weight * place_v.astype(F32)).astype(BF16)
+    image_out[...] = weight * image[:, :128]
     image = image.astype(BF16)
     picks = jnp.concatenate([pick_f[:pairs], couple_w], axis=0).astype(BF16)
     first = dot(picks, image)
@@ -242,9 +245,9 @@
     line, pairs, corners = plan.line, plan.pairs, plan.corners
     received, refs = refs[:line], refs[line:]
     coarse_refs, refs = refs[: plan.groups], refs[plan.groups :]
-    schur, flexibility, loads, place, weight = refs[:5]
-    message, image_out, direction, local_part, far_image, schur_rows, missing_out = refs[5:12]
-    moved, images, moved_images, inputs, products = refs[12:]
+    loads, place, weight, pair_fields, image, flexibility = refs[:6]
+    message, direction, local_part, schur_rows, missing_out = refs[6:11]
+    moved, images, moved_images, inputs, products = refs[11:]
     half, spare = plan.half, plan.spare
     extras = [block[plan.edge_at : plan.edge_at + 16, :].astype(F32) for block in received]
     missing = [missing_of(plan, extra) for extra in extras]
@@ -294,8 +297,8 @@
         products[t, half:pairs, :] = lower.astype(BF16)
         products[t, pairs:, :] = coarse_part
         result = dot(products[t], moved[t])
-        image = received[t][plan.image_at : plan.schur_at, :].astype(F32)
-        images[t] = image - result[:pairs]
+        pair_image = received[t][plan.image_at : plan.schur_at, :].astype(F32)
+        images[t] = pair_image - result[:pairs]
         changes.append(result[pairs : pairs + corners])
     for t in range(line):
 
@@ -315,12 +318,6 @@
     coarse_in = inputs[...].reshape(line * plan.spread, 128).astype(BF16)
     coarse_out = dot(coarse_matrix, coarse_in)
 
-    place_v = place[...]
-    weight = weight[...].astype(F32)
-    right = loads[...].astype(F32) - dot(place_v, moved[0])
-    image = dot(schur[...], (weight * right).astype(BF16))
-    image_out[...] = image
-    image = image.astype(BF16)
     for t in range(1, line):
         if t < plan.last:
             rows = products[t, plan.rows(t - 1), :]
@@ -329,11 +326,12 @@
                 plan, missing[t], lambda slot: products[plan.last, plan.rows(slot), :].astype(F32)
             ).astype(BF16)
         schur_rows[plan.rows(t - 1), :] = rows
-    mine = moved_images[0]
-    far_image[...] = mine
-    field = weight * (image.astype(F32) - dot(place_v, mine.astype(BF16)))
+    weight = weight[...].astype(F32)
+    right = loads[...].astype(F32) - dot(place[...], moved[0])
+    heard = jnp.concatenate([moved[0], moved_images[0].astype(BF16)], axis=0)
+    field = image[...] - dot(pair_fields[...], heard)
+    local = dot(flexibility[...], field.astype(BF16))
     direction[...] = field
-    local = dot(flexibility[...], field.astype(BF16))
     local_part[...] = local
     inner = split(jnp.sum(weight * right * field, axis=0, keepdims=True))
     square = split(jnp.sum(field * local, axis=0, keepdims=True))
@@ -343,11 +341,21 @@
     message[...] = jnp.concatenate(parts, axis=0).astype(BF16)
 
 
-def surface_kernel(plan, *refs):
+def local_kernel(plan, local_part, schur, place, weight, pair_rows):
+    local = local_part[...]
+    high, low = split(local)
+    image = dot(schur[...], (weight[...].astype(F32) * local).astype(BF16))
+    values = jnp.concatenate([high, low, image], axis=1).astype(BF16)
+    rows = dot_over_rows(place[...], values)[: plan.pairs]
+    pair_rows[:, :128] = rows[:, :128] + rows[:, 128:256]
+    pair_rows[:, 128:] = rows[:, 256:]
+
+
+def coarse_kernel(plan, *refs):
     groups, corners, pairs = plan.groups, plan.corners, plan.pairs
     heard = [ref[...].astype(F32) for ref in refs[:groups]]
-    missing_rows, schur, coupling_t, place, weight, local_part = refs[groups : groups + 6]
-    image_out, messages = refs[groups + 6], refs[groups + 7 :]
+    missing_rows, first, pair_rows = refs[groups : groups + 3]
+    own_out, messages = refs[groups + 3], refs[groups + 4 :]
     dots = sum(block[plan.dots_at : plan.dots_at + 8] for block in heard)
     inner = dots[0:1] + dots[1:2]
     square = dots[2:3] + dots[3:4]
@@ -357,17 +365,18 @@
         for d in range(groups):
             at = corners * (m ^ d)
             value = value + heard[d][at : at + corners]
-        value = value.astype(BF16)
+        value = value.astype(BF16).astype(F32)
         if m == 0:
             own = value
         entry = heard[m][plan.input_at : plan.input_at + corners]
-        square = square + jnp.sum(entry * value.astype(F32), axis=0, keepdims=True)
-    field = (local_part[...] + dot_over_rows(coupling_t[...], own)).astype(BF16)
-    scaled = (weight[...].astype(F32) * field.astype(F32)).astype(BF16)
-    image = dot(schur[...], scaled)
-    image_out[...] = image
-    both = jnp.concatenate([field, image.astype(BF16)], axis=1)
-    both = dot_over_rows(place[...], both)[:pairs]
+        square = square + jnp.sum(entry * value, axis=0, keepdims=True)
+    own_out[...] = own
+    twice, blank = 2.0 * own, jnp.zeros((corners, 128), F32)
+    values = jnp.concatenate(
+        [jnp.concatenate([blank, twice], axis=1), jnp.concatenate([twice, blank], axis=1)], axis=0
+    ).astype(BF16)
+    coupled = first[plan.edge_at : plan.coarse_at, :]
+    both = pair_rows[...] + dot_over_rows(coupled, values)[:pairs]
     surface_part = both[:, :128].astype(BF16)
     sums = stack_rows(split(inner) + split(square), 16).astype(BF16)
     missing = jnp.broadcast_to(missing_rows[0:1, :], (plan.each, 128))
@@ -386,12 +395,19 @@
         message[plan.sums_at :, :] = sums
 
 
+def surface_kernel(plan, own, schur, coupling_t, weight, local_part, image_out):
+    lifted = dot_over_rows(coupling_t[...], own[...].astype(BF16))
+    field = (local_part[...] + lifted).astype(BF16)
+    scaled = (weight[...].astype(F32) * field.astype(F32)).astype(BF16)
+    image_out[...] = weight[...].astype(F32) * dot(schur[...], scaled)
+
+
 def result_kernel(plan, *refs):
     line, pairs, each = plan.line, plan.pairs, plan.each
     received, schur_rows, missing_rows, refs = refs[:line], refs[line], refs[line + 1], refs[line + 2 :]
-    far_image, first_image, direction, surface_image, schur_place, place, weight = refs[:7]
-    solution_out, preconditioned_out = refs[7:9]
-    moved, far_rows, solved, preconditioned, sent = refs[9:]
+    direction, surface_image, pair_fields = refs[:3]
+    solution_out, preconditioned_out = refs[3:5]
+    moved, far_rows, solved, preconditioned, sent = refs[5:]
     sums = 0.0
     for block in received:
         sums = sums + block[plan.sums_at :, :].astype(F32)
@@ -426,10 +442,9 @@
         )
     if plan.wide > pairs:
         far_rows[pairs:, :] = jnp.zeros((plan.wide - pairs, 128), F32)
-    far = far_image[...] - step * far_rows[...]
-    change = surface_image[...] - dot(schur_place[...], moved[0])
-    remaining = first_image[...] - step * change - dot(place[...], far.astype(BF16))
-    preconditioned[...] = weight[...].astype(F32) * remaining
+    heard = jnp.concatenate([moved[0], far_rows[...].astype(BF16)], axis=0)
+    change = surface_image[...] - dot(pair_fields[...], heard)
+    preconditioned[...] = direction[...] - step * change
     last_copy = pltpu.make_async_copy(preconditioned, preconditioned_out, sent.at[1])
     last_copy.start()
     solution_copy.wait()
@@ -477,17 +492,18 @@
     lists = (neighbors[0], rows, coarse_map[0])
     kept = (dirichlet_schur[0, 0], subdomain_loads[0, 0], coupling[0, 0].T, flexibility[0, 0])
     inputs = [pltpu.with_memory_space_constraint(array, pltpu.HBM) for array in lists + kept]
-    message, place, weight, schur_place, schur, loads, coupling_t, flex = pl.pallas_call(
+    message, place, weight, pair_fields, image, schur, loads, coupling_t, flex = pl.pallas_call(
         functools.partial(prepare_kernel, plan),
         out_shape=(
             shape(plan.first, 128, kind=BF16),
             shape(order, plan.wide, kind=BF16),
             shape(order, 128, kind=BF16),
-            shape(order, plan.wide, kind=BF16),
+            shape(order, 2 * plan.wide, kind=BF16),
+            shape(order, 128),
         )
         + tuple(shape(*array.shape, kind=BF16) for array in kept),
         in_specs=[outside] * 7,
-        out_specs=(whole,) * 8,
+        out_specs=(whole,) * 9,
         scratch_shapes=[pltpu.VMEM(array.shape, array.dtype) for array in lists]
         + [
             pltpu.VMEM((round_up(plan.neighbors, 8), plan.wide), jnp.int32),
@@ -501,19 +517,17 @@
     first, carried = line_blocks([message] * (line // 2), riders)
     coarse_all = [coarse] + carried[::-1]
 
-    message, image, direction, local_part, far_image, schur_rows, missing = pl.pallas_call(
+    message, direction, local_part, schur_rows, missing = pl.pallas_call(
         functools.partial(direction_kernel, plan),
         out_shape=(
             shape(plan.second, 128, kind=BF16),
             shape(order, 128),
             shape(order, 128),
-            shape(order, 128),
-            shape(plan.wide, 128),
             shape(plan.each * (line - 1), 128, kind=BF16),
             shape(line, 128),
         ),
-        in_specs=[whole] * (line + plan.groups + 5),
-        out_specs=(whole,) * 7,
+        in_specs=[whole] * (line + plan.groups + 6),
+        out_specs=(whole,) * 5,
         scratch_shapes=[
             pltpu.VMEM((line, plan.wide, 128), BF16),
             pltpu.VMEM((line, plan.pairs, 128), F32),
@@ -523,26 +537,42 @@
         ],
         compiler_params=params,
         name="direction",
-    )(*first, *coarse_all, schur, flex, loads, place, weight)
+    )(*first, *coarse_all, loads, place, weight, pair_fields, image, flex)
     heard = [message]
     for step in range(1, plan.groups):
         heard.append(swap(message, "grp", step))
 
-    surface_image, *messages = pl.pallas_call(
-        functools.partial(surface_kernel, plan),
-        out_shape=(shape(order, 128),)
+    pair_rows = pl.pallas_call(
+        functools.partial(local_kernel, plan),
+        out_shape=shape(plan.pairs, 256),
+        in_specs=[whole] * 4,
+        out_specs=whole,
+        compiler_params=params,
+        name="local",
+    )(local_part, schur, place, weight)
+    own, *messages = pl.pallas_call(
+        functools.partial(coarse_kernel, plan),
+        out_shape=(shape(plan.corners, 128),)
         + (shape(plan.third, 128, kind=BF16),) * (line // 2),
-        in_specs=[whole] * (plan.groups + 6),
+        in_specs=[whole] * (plan.groups + 3),
         out_specs=(whole,) * (1 + line // 2),
         compiler_params=params,
+        name="coarse",
+    )(*heard, missing, first[0], pair_rows)
+    last, _ = line_blocks(messages)
+    surface_image = pl.pallas_call(
+        functools.partial(surface_kernel, plan),
+        out_shape=shape(order, 128),
+        in_specs=[whole] * 5,
+        out_specs=whole,
+        compiler_params=params,
         name="surface",
-    )(*heard, missing, schur, coupling_t, place, weight, local_part)
-    last, _ = line_blocks(messages)
+    )(own, schur, coupling_t, weight, local_part)
 
     solved, preconditioned = pl.pallas_call(
         functools.partial(result_kernel, plan),
         out_shape=(shape(order, 128), shape(order, 128)),
-        in_specs=[whole] * (line + 9),
+        in_specs=[whole] * (line + 5),
         out_specs=(outside, outside),
         scratch_shapes=[
             pltpu.VMEM((line, plan.wide, 128), BF16),
@@ -553,7 +583,7 @@
         ],
         compiler_params=params,
         name="result",
-    )(*last, schur_rows, missing, far_image, image, direction, surface_image, schur_place, place, weight)
+    )(*last, schur_rows, missing, direction, surface_image, pair_fields)
     return solved[None, None], preconditioned[None, None]
 
 

time: 43 us -> 42.2 us (0.981)
  waiting for transfers between devices: 14.2 us -> 13.2 us
    ppermute x20, waiting for transfers between devices: 14.2 us -> 13.2 us  [swap(): lax.ppermute(value, axis, [(at, at ^ distance) for at in range(size)])]
    pallas_call x1 -> x3, Pallas kernels: 0.68 us -> 1.2 us  [the longest x1 0.52 us: line_body(): pl.pallas_call(functools.partial(local_kernel, plan), out_shape=shape(pla...]
  transfers between devices with their start and end apart: 20 -> 20, of which waited for: 12 -> 11; matrix products, arithmetic and copies ran while one was open for 0% -> 0% of each run, Pallas kernels for 0% -> 2%
where the time goes in v6:
time: 42.2 us; the launch traced here: 42.1 us
  starting transfers between devices  22.1 us (52%)
  waiting for transfers between devices  13.2 us (31%)
  Pallas kernels  6.03 us (14%)
  between operations  0.71 us (2%)
    ppermute x20, starting transfers between devices, swap(): lax.ppermute(value, axis, [(at, at ^ distance) for at in range(size)])  22.1 us
    ppermute x20, waiting for transfers between devices, swap(): lax.ppermute(value, axis, [(at, at ^ distance) for at in range(size)])  13.2 us
    pallas_call x1, Pallas kernels, line_body(): pl.pallas_call(functools.partial(prepare_kernel, plan), out_shape=(shape(...  2.23 us
    pallas_call x1, Pallas kernels, line_body(): pl.pallas_call(functools.partial(direction_kernel, plan), out_shape=(shap...  1.42 us
    pallas_call x1, Pallas kernels, line_body(): pl.pallas_call(functools.partial(result_kernel, plan), out_shape=(shape(o...  1.19 us
  transfers between devices with their start and end apart: 20, of which 11 were waited for; matrix products, arithmetic and copies ran while one was open for 0% of the time, Pallas kernels for 2%

profile of v6, /device:TPU:0, one launch (start us, length us, event | category | flops | bytes accessed | tf_op | source)
XLA Modules:
  0.0 42.1 jit_solution(5474229487165746904)
XLA Ops:
  0.6 0.0 copy-start
  0.6 2.2 %prepare.1 = (bf16[312,128]{1,0:T(8,128)(2,1)S(1)}, bf16[512,128]{1,0:T(8,128)(2,1)S(1)}, bf16[512,128]{1,0:T(8,128)(2,1)S(1)}, bf16[512,256]{1,0:T(8,128)(2,1)S...) custom-call(s32[1,6]{1,0:T(1,128)} %bitcast.21, ...), custom_call_target="tpu_custom_call" | custom-call | tf_op jit(solution)/shard_map/prepare/pallas_call | solution.py:495
  2.9 5.1 %collective-permute-start.5 = (bf16[312,128]{1,0:T(8,128)(2,1)S(1)}, bf16[312,128]{1,0:T(8,128)(2,1)S(1)}, u32[]{:S(2)}, u32[]{:S(2)}) collective-permute-start(bf16[312,128]{1,0:T(8,128)(2,1)S(1)} %get-tuple-element.24.refs_0_.refs_5_), channel_id=1, source_target_pairs={{0,24},{4,28},{8,16},{12,20},{16,8},{20,12},{24,0},{28,4},{1,25},{... | collective-permute-start | bytes 239624 | tf_op jit(solution)/shard_map/ppermute | solution.py:477
  8.0 1.5 %collective-permute-start = (bf16[312,128]{1,0:T(8,128)(2,1)S(1)}, bf16[312,128]{1,0:T(8,128)(2,1)S(1)}, u32[]{:S(2)}, u32[]{:S(2)}) collective-permute-start(bf16[312,128]{1,0:T(8,128)(2,1)S(1)} %get-tuple-element.24.refs_0_.refs_5_), channel_id=1, source_target_pairs={{0,4},{4,0},{8,12},{12,8},{16,20},{20,16},{24,28},{28,24},{1,5},{5... | collective-permute-start | bytes 239624 | tf_op jit(solution)/shard_map/ppermute | solution.py:477
  9.5 0.0 collective-permute-start.3
  9.5 0.8 %collective-permute-start.1 = (bf16[312,128]{1,0:T(8,128)(2,1)S(1)}, bf16[312,128]{1,0:T(8,128)(2,1)S(1)}, u32[]{:S(2)}, u32[]{:S(2)}) collective-permute-start(bf16[312,128]{1,0:T(8,128)(2,1)S(1)} %get-tuple-element.24.refs_0_.refs_5_), channel_id=1, source_target_pairs={{0,8},{4,12},{8,0},{12,4},{16,24},{20,28},{24,16},{28,20},{1,9},{5... | collective-permute-start | bytes 239624 | tf_op jit(solution)/shard_map/ppermute | solution.py:477
  10.3 0.4 %collective-permute-done.5.refs_6_ = bf16[312,128]{1,0:T(8,128)(2,1)S(1)} collective-permute-done((bf16[312,128]{1,0:T(8,128)(2,1)S(1)}, bf16[312,128]{1,0:T(8,128)(2,1)S(1)}, u32[]{:S(2)}, u32[]{:S(2)}) %collective-permute-start.5) | collective-permute-done | bytes 79904 | tf_op jit(solution)/shard_map/ppermute | solution.py:477
  10.7 1.8 %collective-permute-start.6 = (bf16[312,128]{1,0:T(8,128)(2,1)S(1)}, bf16[312,128]{1,0:T(8,128)(2,1)S(1)}, u32[]{:S(2)}, u32[]{:S(2)}) collective-permute-start(bf16[312,128]{1,0:T(8,128)(2,1)S(1)} %collective-permute-done.5.refs_6_), channel_id=1, source_target_pairs={{0,4},{4,0},{8,12},{12,8},{16,20},{20,16},{24,28},{28,24},{1,5},{5... | collective-permute-start | bytes 239624 | tf_op jit(solution)/shard_map/ppermute | solution.py:477
  12.5 0.4 collective-permute-done.refs_1_
  12.9 0.0 copy-done
  12.9 0.0 collective-permute-start.9
  12.9 1.5 %collective-permute-start.8 = (bf16[24,2048]{1,0:T(8,128)(2,1)S(1)}, bf16[24,2048]{1,0:T(8,128)(2,1)S(1)}, u32[]{:S(2)}, u32[]{:S(2)}) collective-permute-start(bf16[24,2048]{1,0:T(8,128)(2,1)S(1)} %bitcast.13), channel_id=1, source_target_pairs={{0,2},{1,3},{2,0},{3,1},{4,6},{5,7},{6,4},{7,5},{8,10},{9,11},{10,... | collective-permute-start | bytes 294920 | tf_op jit(solution)/shard_map/ppermute | solution.py:477
  14.4 0.5 %collective-permute-done.3.refs_4_ = bf16[312,128]{1,0:T(8,128)(2,1)S(1)} collective-permute-done((bf16[312,128]{1,0:T(8,128)(2,1)S(1)}, bf16[312,128]{1,0:T(8,128)(2,1)S(1)}, u32[]{:S(2)}, u32[]{:S(2)}) %collective-permute-start.3) | collective-permute-done | bytes 79904 | tf_op jit(solution)/shard_map/ppermute | solution.py:477
  14.9 0.0 collective-permute-start.7
  14.9 0.0 collective-permute-done.1.refs_2_
  14.9 1.3 %collective-permute-start.4 = (bf16[312,128]{1,0:T(8,128)(2,1)S(1)}, bf16[312,128]{1,0:T(8,128)(2,1)S(1)}, u32[]{:S(2)}, u32[]{:S(2)}) collective-permute-start(bf16[312,128]{1,0:T(8,128)(2,1)S(1)} %collective-permute-done.3.refs_4_), channel_id=1, source_target_pairs={{0,4},{4,0},{8,12},{12,8},{16,20},{20,16},{24,28},{28,24},{1,5},{5... | collective-permute-start | bytes 239624 | tf_op jit(solution)/shard_map/ppermute | solution.py:477
  16.2 0.0 collective-permute-done.6.refs_7_
  16.2 0.7 %collective-permute-start.2 = (bf16[312,128]{1,0:T(8,128)(2,1)S(1)}, bf16[312,128]{1,0:T(8,128)(2,1)S(1)}, u32[]{:S(2)}, u32[]{:S(2)}) collective-permute-start(bf16[312,128]{1,0:T(8,128)(2,1)S(1)} %collective-permute-done.1.refs_2_), channel_id=1, source_target_pairs={{0,4},{4,0},{8,12},{12,8},{16,20},{20,16},{24,28},{28,24},{1,5},{5... | collective-permute-start | bytes 239624 | tf_op jit(solution)/shard_map/ppermute | solution.py:477
  17.0 3.2 %collective-permute-done.4.refs_5_ = bf16[312,128]{1,0:T(8,128)(2,1)S(1)} collective-permute-done((bf16[312,128]{1,0:T(8,128)(2,1)S(1)}, bf16[312,128]{1,0:T(8,128)(2,1)S(1)}, u32[]{:S(2)}, u32[]{:S(2)}) %collective-permute-start.4) | collective-permute-done | bytes 79904 | tf_op jit(solution)/shard_map/ppermute | solution.py:477
  20.1 1.3 %collective-permute-done.2.refs_3_ = bf16[312,128]{1,0:T(8,128)(2,1)S(1)} collective-permute-done((bf16[312,128]{1,0:T(8,128)(2,1)S(1)}, bf16[312,128]{1,0:T(8,128)(2,1)S(1)}, u32[]{:S(2)}, u32[]{:S(2)}) %collective-permute-start.2) | collective-permute-done | bytes 79904 | tf_op jit(solution)/shard_map/ppermute | solution.py:477
  21.5 0.0 collective-permute-done.9.refs_11_
  21.5 0.0 collective-permute-done.8.refs_10_
  21.5 0.0 collective-permute-done.7.refs_9_
  21.5 1.4 %direction.1 = (bf16[128,128]{1,0:T(8,128)(2,1)S(1)}, f32[512,128]{1,0:T(8,128)S(1)}, f32[512,128]{1,0:T(8,128)S(1)}, bf16[112,128]{1,0:T(8,128)(2,1)S(1)}, f32[8,128]{1,0:T(8,128)S(1)}) custom-call(bf16[312,128]{1,0:T(8,128)(2,1)S(1)} %get-tuple-element.24.refs_0_.refs_5_, bf16[312,128]{1,0:T(8,128)(2,1)S(1)} %collective-permute-done.refs_1_, ...), custom_call_target="tpu_custom_call" | custom-call | tf_op jit(solution)/shard_map/direction/pallas_call | solution.py:520
  22.9 0.9 %collective-permute-start.12 = (bf16[128,128]{1,0:T(8,128)(2,1)S(1)}, bf16[128,128]{1,0:T(8,128)(2,1)S(1)}, u32[]{:S(2)}, u32[]{:S(2)}) collective-permute-start(bf16[128,128]{1,0:T(8,128)(2,1)S(1)} %get-tuple-element.32.refs_0_), channel_id=1, source_target_pairs={{0,3},{1,2},{2,1},{3,0},{4,7},{5,6},{6,5},{7,4},{8,11},{9,10},{10,... | collective-permute-start | bytes 98312 | tf_op jit(solution)/shard_map/ppermute | solution.py:477
  23.8 0.7 %collective-permute-start.11 = (bf16[128,128]{1,0:T(8,128)(2,1)S(1)}, bf16[128,128]{1,0:T(8,128)(2,1)S(1)}, u32[]{:S(2)}, u32[]{:S(2)}) collective-permute-start(bf16[128,128]{1,0:T(8,128)(2,1)S(1)} %get-tuple-element.32.refs_0_), channel_id=1, source_target_pairs={{0,2},{1,3},{2,0},{3,1},{4,6},{5,7},{6,4},{7,5},{8,10},{9,11},{10,... | collective-permute-start | bytes 98312 | tf_op jit(solution)/shard_map/ppermute | solution.py:477
  24.6 0.3 collective-permute-start.10
  24.8 0.5 %local.1.refs_6_ = f32[96,256]{1,0:T(8,128)S(1)} custom-call(f32[512,128]{1,0:T(8,128)S(1)} %get-tuple-element.34.local_part, bf16[512,512]{1,0:T(8,128)(2,1)S(1)} %get-tuple-element.35.schur, bf16[512,128]{1,0:T(8,128)(2,1)S(1)} %get-tuple-element.27.refs_13_.place, bf16[512,128]{1,0:T(8,128)(2,1)S(1)} %get-tuple-element.28.refs_14_.weight), custom_call_target="tpu_custom_call" | custom-call | tf_op jit(solution)/shard_map/local/pallas_call | solution.py:545
  25.3 1.2 %collective-permute-done.12.refs_3_ = bf16[128,128]{1,0:T(8,128)(2,1)S(1)} collective-permute-done((bf16[128,128]{1,0:T(8,128)(2,1)S(1)}, bf16[128,128]{1,0:T(8,128)(2,1)S(1)}, u32[]{:S(2)}, u32[]{:S(2)}) %collective-permute-start.12) | collective-permute-done | bytes 32800 | tf_op jit(solution)/shard_map/ppermute | solution.py:477
  26.6 1.3 %collective-permute-done.11.refs_2_ = bf16[128,128]{1,0:T(8,128)(2,1)S(1)} collective-permute-done((bf16[128,128]{1,0:T(8,128)(2,1)S(1)}, bf16[128,128]{1,0:T(8,128)(2,1)S(1)}, u32[]{:S(2)}, u32[]{:S(2)}) %collective-permute-start.11) | collective-permute-done | bytes 32800 | tf_op jit(solution)/shard_map/ppermute | solution.py:477
  27.9 0.0 collective-permute-done.10.refs_1_
  27.9 0.2 coarse.1
  28.1 1.6 %collective-permute-start.14 = (bf16[144,128]{1,0:T(8,128)(2,1)S(1)}, bf16[144,128]{1,0:T(8,128)(2,1)S(1)}, u32[]{:S(2)}, u32[]{:S(2)}) collective-permute-start(bf16[144,128]{1,0:T(8,128)(2,1)S(1)} %get-tuple-element.37), channel_id=1, source_target_pairs={{0,8},{4,12},{8,0},{12,4},{16,24},{20,28},{24,16},{28,20},{1,9},{5... | collective-permute-start | bytes 110600 | tf_op jit(solution)/shard_map/ppermute | solution.py:477
  29.7 1.5 %collective-permute-start.16 = (bf16[144,128]{1,0:T(8,128)(2,1)S(1)}, bf16[144,128]{1,0:T(8,128)(2,1)S(1)}, u32[]{:S(2)}, u32[]{:S(2)}) collective-permute-start(bf16[144,128]{1,0:T(8,128)(2,1)S(1)} %get-tuple-element.38), channel_id=1, source_target_pairs={{0,16},{4,20},{8,24},{12,28},{16,0},{20,4},{24,8},{28,12},{1,17},{... | collective-permute-start | bytes 110600 | tf_op jit(solution)/shard_map/ppermute | solution.py:477
  31.2 1.4 %collective-permute-start.18 = (bf16[144,128]{1,0:T(8,128)(2,1)S(1)}, bf16[144,128]{1,0:T(8,128)(2,1)S(1)}, u32[]{:S(2)}, u32[]{:S(2)}) collective-permute-start(bf16[144,128]{1,0:T(8,128)(2,1)S(1)} %get-tuple-element.39), channel_id=1, source_target_pairs={{0,24},{4,28},{8,16},{12,20},{16,8},{20,12},{24,0},{28,4},{1,25},{... | collective-permute-start | bytes 110600 | tf_op jit(solution)/shard_map/ppermute | solution.py:477
  32.5 1.2 %collective-permute-start.13 = (bf16[144,128]{1,0:T(8,128)(2,1)S(1)}, bf16[144,128]{1,0:T(8,128)(2,1)S(1)}, u32[]{:S(2)}, u32[]{:S(2)}) collective-permute-start(bf16[144,128]{1,0:T(8,128)(2,1)S(1)} %get-tuple-element.36.refs_0_), channel_id=1, source_target_pairs={{0,4},{4,0},{8,12},{12,8},{16,20},{20,16},{24,28},{28,24},{1,5},{5... | collective-permute-start | bytes 110600 | tf_op jit(solution)/shard_map/ppermute | solution.py:477
  33.8 0.0 collective-permute-done.14.refs_2_
  33.8 0.8 %collective-permute-start.15 = (bf16[144,128]{1,0:T(8,128)(2,1)S(1)}, bf16[144,128]{1,0:T(8,128)(2,1)S(1)}, u32[]{:S(2)}, u32[]{:S(2)}) collective-permute-start(bf16[144,128]{1,0:T(8,128)(2,1)S(1)} %collective-permute-done.14.refs_2_), channel_id=1, source_target_pairs={{0,4},{4,0},{8,12},{12,8},{16,20},{20,16},{24,28},{28,24},{1,5},{5... | collective-permute-start | bytes 110600 | tf_op jit(solution)/shard_map/ppermute | solution.py:477
  34.6 1.1 %collective-permute-done.16.refs_4_ = bf16[144,128]{1,0:T(8,128)(2,1)S(1)} collective-permute-done((bf16[144,128]{1,0:T(8,128)(2,1)S(1)}, bf16[144,128]{1,0:T(8,128)(2,1)S(1)}, u32[]{:S(2)}, u32[]{:S(2)}) %collective-permute-start.16) | collective-permute-done | bytes 36896 | tf_op jit(solution)/shard_map/ppermute | solution.py:477
  35.7 0.2 collective-permute-start.17
  35.8 1.1 %collective-permute-done.18.refs_6_ = bf16[144,128]{1,0:T(8,128)(2,1)S(1)} collective-permute-done((bf16[144,128]{1,0:T(8,128)(2,1)S(1)}, bf16[144,128]{1,0:T(8,128)(2,1)S(1)}, u32[]{:S(2)}, u32[]{:S(2)}) %collective-permute-start.18) | collective-permute-done | bytes 36896 | tf_op jit(solution)/shard_map/ppermute | solution.py:477
  36.9 0.8 %collective-permute-start.19 = (bf16[144,128]{1,0:T(8,128)(2,1)S(1)}, bf16[144,128]{1,0:T(8,128)(2,1)S(1)}, u32[]{:S(2)}, u32[]{:S(2)}) collective-permute-start(bf16[144,128]{1,0:T(8,128)(2,1)S(1)} %collective-permute-done.18.refs_6_), channel_id=1, source_target_pairs={{0,4},{4,0},{8,12},{12,8},{16,20},{20,16},{24,28},{28,24},{1,5},{5... | collective-permute-start | bytes 110600 | tf_op jit(solution)/shard_map/ppermute | solution.py:477
  37.7 0.5 %surface.1.refs_11_ = f32[512,128]{1,0:T(8,128)S(1)} custom-call(f32[24,128]{1,0:T(8,128)S(1)} %get-tuple-element.42.own, bf16[512,512]{1,0:T(8,128)(2,1)S(1)} %get-tuple-element.35.schur, bf16[24,512]{1,0:T(8,128)(2,1)S(1)} %get-tuple-element.43.coupling_t, bf16[512,128]{1,0:T(8,128)(2,1)S(1)} %get-tuple-element.28.refs_14_.weight, ...), custom_call_target="tpu_custom_call" | custom-call | tf_op jit(solution)/shard_map/surface/pallas_call | solution.py:563
  38.2 0.0 collective-permute-done.13.refs_1_
  38.2 0.0 collective-permute-done.15.refs_3_
  38.2 1.4 %collective-permute-done.17.refs_5_ = bf16[144,128]{1,0:T(8,128)(2,1)S(1)} collective-permute-done((bf16[144,128]{1,0:T(8,128)(2,1)S(1)}, bf16[144,128]{1,0:T(8,128)(2,1)S(1)}, u32[]{:S(2)}, u32[]{:S(2)}) %collective-permute-start.17) | collective-permute-done | bytes 36896 | tf_op jit(solution)/shard_map/ppermute | solution.py:477
  39.6 1.3 %collective-permute-done.19.refs_7_ = bf16[144,128]{1,0:T(8,128)(2,1)S(1)} collective-permute-done((bf16[144,128]{1,0:T(8,128)(2,1)S(1)}, bf16[144,128]{1,0:T(8,128)(2,1)S(1)}, u32[]{:S(2)}, u32[]{:S(2)}) %collective-permute-start.19) | collective-permute-done | bytes 36896 | tf_op jit(solution)/shard_map/ppermute | solution.py:477
  40.9 1.2 %result.1 = (f32[512,128]{1,0:T(8,128)}, f32[512,128]{1,0:T(8,128)}) custom-call(bf16[144,128]{1,0:T(8,128)(2,1)S(1)} %get-tuple-element.36.refs_0_, bf16[144,128]{1,0:T(8,128)(2,1)S(1)} %collective-permute-done.13.refs_1_, bf16[144,128]{1,0:T(8,128)(2,1)S(1)} %collective-permute-done.14.refs_2_, bf16[144,128]{1,0:T(8,128)(2,1)S(1)} %collective-permute-done.15.refs_3_, ...), custom_call_target="tpu_custom_call" | custom-call | tf_op jit(solution)/shard_map/result/pallas_call | solution.py:572
Async XLA Ops:
  0.6 12.3 %copy-start = (bf16[1,1,24,2048]{3,2,1,0:T(8,128)(2,1)S(1)}, bf16[1,1,24,2048]{3,2,1,0:T(8,128)(2,1)}, u32[]{:S(2)}) copy-start(bf16[1,1,24,2048]{3,2,1,0:T(8,128)(2,1)} %param.12) | copy-start | bytes 294916
  2.9 7.8 %collective-permute-start.5 = (bf16[312,128]{1,0:T(8,128)(2,1)S(1)}, bf16[312,128]{1,0:T(8,128)(2,1)S(1)}, u32[]{:S(2)}, u32[]{:S(2)}) collective-permute-start(bf16[312,128]{1,0:T(8,128)(2,1)S(1)} %get-tuple-element.24.refs_0_.refs_5_), channel_id=1, source_target_pairs={{0,24},{4,28},{8,16},{12,20},{16,8},{20,12},{24,0},{28,4},{1,25},{... | collective-permute-start | bytes 239624 | tf_op jit(solution)/shard_map/ppermute | solution.py:477
  8.0 4.9 %collective-permute-start = (bf16[312,128]{1,0:T(8,128)(2,1)S(1)}, bf16[312,128]{1,0:T(8,128)(2,1)S(1)}, u32[]{:S(2)}, u32[]{:S(2)}) collective-permute-start(bf16[312,128]{1,0:T(8,128)(2,1)S(1)} %get-tuple-element.24.refs_0_.refs_5_), channel_id=1, source_target_pairs={{0,4},{4,0},{8,12},{12,8},{16,20},{20,16},{24,28},{28,24},{1,5},{5... | collective-permute-start | bytes 239624 | tf_op jit(solution)/shard_map/ppermute | solution.py:477
  9.5 5.5 %collective-permute-start.3 = (bf16[312,128]{1,0:T(8,128)(2,1)S(1)}, bf16[312,128]{1,0:T(8,128)(2,1)S(1)}, u32[]{:S(2)}, u32[]{:S(2)}) collective-permute-start(bf16[312,128]{1,0:T(8,128)(2,1)S(1)} %get-tuple-element.24.refs_0_.refs_5_), channel_id=1, source_target_pairs={{0,16},{4,20},{8,24},{12,28},{16,0},{20,4},{24,8},{28,12},{1,17},{... | collective-permute-start | bytes 239624 | tf_op jit(solution)/shard_map/ppermute | solution.py:477
  9.5 5.5 %collective-permute-start.1 = (bf16[312,128]{1,0:T(8,128)(2,1)S(1)}, bf16[312,128]{1,0:T(8,128)(2,1)S(1)}, u32[]{:S(2)}, u32[]{:S(2)}) collective-permute-start(bf16[312,128]{1,0:T(8,128)(2,1)S(1)} %get-tuple-element.24.refs_0_.refs_5_), channel_id=1, source_target_pairs={{0,8},{4,12},{8,0},{12,4},{16,24},{20,28},{24,16},{28,20},{1,9},{5... | collective-permute-start | bytes 239624 | tf_op jit(solution)/shard_map/ppermute | solution.py:477
  10.7 5.5 %collective-permute-start.6 = (bf16[312,128]{1,0:T(8,128)(2,1)S(1)}, bf16[312,128]{1,0:T(8,128)(2,1)S(1)}, u32[]{:S(2)}, u32[]{:S(2)}) collective-permute-start(bf16[312,128]{1,0:T(8,128)(2,1)S(1)} %collective-permute-done.5.refs_6_), channel_id=1, source_target_pairs={{0,4},{4,0},{8,12},{12,8},{16,20},{20,16},{24,28},{28,24},{1,5},{5... | collective-permute-start | bytes 239624 | tf_op jit(solution)/shard_map/ppermute | solution.py:477
  12.9 8.6 %collective-permute-start.9 = (bf16[24,2048]{1,0:T(8,128)(2,1)S(1)}, bf16[24,2048]{1,0:T(8,128)(2,1)S(1)}, u32[]{:S(2)}, u32[]{:S(2)}) collective-permute-start(bf16[24,2048]{1,0:T(8,128)(2,1)S(1)} %bitcast.12), channel_id=1, source_target_pairs={{0,3},{1,2},{2,1},{3,0},{4,7},{5,6},{6,5},{7,4},{8,11},{9,10},{10,... | collective-permute-start | bytes 294920 | tf_op jit(solution)/shard_map/ppermute | solution.py:477
  12.9 8.6 %collective-permute-start.8 = (bf16[24,2048]{1,0:T(8,128)(2,1)S(1)}, bf16[24,2048]{1,0:T(8,128)(2,1)S(1)}, u32[]{:S(2)}, u32[]{:S(2)}) collective-permute-start(bf16[24,2048]{1,0:T(8,128)(2,1)S(1)} %bitcast.13), channel_id=1, source_target_pairs={{0,2},{1,3},{2,0},{3,1},{4,6},{5,7},{6,4},{7,5},{8,10},{9,11},{10,... | collective-permute-start | bytes 294920 | tf_op jit(solution)/shard_map/ppermute | solution.py:477
  14.9 6.5 %collective-permute-start.7 = (bf16[24,2048]{1,0:T(8,128)(2,1)S(1)}, bf16[24,2048]{1,0:T(8,128)(2,1)S(1)}, u32[]{:S(2)}, u32[]{:S(2)}) collective-permute-start(bf16[24,2048]{1,0:T(8,128)(2,1)S(1)} %bitcast.14), channel_id=1, source_target_pairs={{0,1},{1,0},{2,3},{3,2},{4,5},{5,4},{6,7},{7,6},{8,9},{9,8},{10,11... | collective-permute-start | bytes 294920 | tf_op jit(solution)/shard_map/ppermute | solution.py:477
  14.9 5.2 %collective-permute-start.4 = (bf16[312,128]{1,0:T(8,128)(2,1)S(1)}, bf16[312,128]{1,0:T(8,128)(2,1)S(1)}, u32[]{:S(2)}, u32[]{:S(2)}) collective-permute-start(bf16[312,128]{1,0:T(8,128)(2,1)S(1)} %collective-permute-done.3.refs_4_), channel_id=1, source_target_pairs={{0,4},{4,0},{8,12},{12,8},{16,20},{20,16},{24,28},{28,24},{1,5},{5... | collective-permute-start | bytes 239624 | tf_op jit(solution)/shard_map/ppermute | solution.py:477
  16.2 5.2 %collective-permute-start.2 = (bf16[312,128]{1,0:T(8,128)(2,1)S(1)}, bf16[312,128]{1,0:T(8,128)(2,1)S(1)}, u32[]{:S(2)}, u32[]{:S(2)}) collective-permute-start(bf16[312,128]{1,0:T(8,128)(2,1)S(1)} %collective-permute-done.1.refs_2_), channel_id=1, source_target_pairs={{0,4},{4,0},{8,12},{12,8},{16,20},{20,16},{24,28},{28,24},{1,5},{5... | collective-permute-start | bytes 239624 | tf_op jit(solution)/shard_map/ppermute | solution.py:477
  22.9 3.7 %collective-permute-start.12 = (bf16[128,128]{1,0:T(8,128)(2,1)S(1)}, bf16[128,128]{1,0:T(8,128)(2,1)S(1)}, u32[]{:S(2)}, u32[]{:S(2)}) collective-permute-start(bf16[128,128]{1,0:T(8,128)(2,1)S(1)} %get-tuple-element.32.refs_0_), channel_id=1, source_target_pairs={{0,3},{1,2},{2,1},{3,0},{4,7},{5,6},{6,5},{7,4},{8,11},{9,10},{10,... | collective-permute-start | bytes 98312 | tf_op jit(solution)/shard_map/ppermute | solution.py:477
  23.8 4.1 %collective-permute-start.11 = (bf16[128,128]{1,0:T(8,128)(2,1)S(1)}, bf16[128,128]{1,0:T(8,128)(2,1)S(1)}, u32[]{:S(2)}, u32[]{:S(2)}) collective-permute-start(bf16[128,128]{1,0:T(8,128)(2,1)S(1)} %get-tuple-element.32.refs_0_), channel_id=1, source_target_pairs={{0,2},{1,3},{2,0},{3,1},{4,6},{5,7},{6,4},{7,5},{8,10},{9,11},{10,... | collective-permute-start | bytes 98312 | tf_op jit(solution)/shard_map/ppermute | solution.py:477
  24.6 3.3 %collective-permute-start.10 = (bf16[128,128]{1,0:T(8,128)(2,1)S(1)}, bf16[128,128]{1,0:T(8,128)(2,1)S(1)}, u32[]{:S(2)}, u32[]{:S(2)}) collective-permute-start(bf16[128,128]{1,0:T(8,128)(2,1)S(1)} %get-tuple-element.32.refs_0_), channel_id=1, source_target_pairs={{0,1},{1,0},{2,3},{3,2},{4,5},{5,4},{6,7},{7,6},{8,9},{9,8},{10,11... | collective-permute-start | bytes 98312 | tf_op jit(solution)/shard_map/ppermute | solution.py:477
  28.1 5.7 %collective-permute-start.14 = (bf16[144,128]{1,0:T(8,128)(2,1)S(1)}, bf16[144,128]{1,0:T(8,128)(2,1)S(1)}, u32[]{:S(2)}, u32[]{:S(2)}) collective-permute-start(bf16[144,128]{1,0:T(8,128)(2,1)S(1)} %get-tuple-element.37), channel_id=1, source_target_pairs={{0,8},{4,12},{8,0},{12,4},{16,24},{20,28},{24,16},{28,20},{1,9},{5... | collective-permute-start | bytes 110600 | tf_op jit(solution)/shard_map/ppermute | solution.py:477
  29.7 6.0 %collective-permute-start.16 = (bf16[144,128]{1,0:T(8,128)(2,1)S(1)}, bf16[144,128]{1,0:T(8,128)(2,1)S(1)}, u32[]{:S(2)}, u32[]{:S(2)}) collective-permute-start(bf16[144,128]{1,0:T(8,128)(2,1)S(1)} %get-tuple-element.38), channel_id=1, source_target_pairs={{0,16},{4,20},{8,24},{12,28},{16,0},{20,4},{24,8},{28,12},{1,17},{... | collective-permute-start | bytes 110600 | tf_op jit(solution)/shard_map/ppermute | solution.py:477
  31.2 5.8 %collective-permute-start.18 = (bf16[144,128]{1,0:T(8,128)(2,1)S(1)}, bf16[144,128]{1,0:T(8,128)(2,1)S(1)}, u32[]{:S(2)}, u32[]{:S(2)}) collective-permute-start(bf16[144,128]{1,0:T(8,128)(2,1)S(1)} %get-tuple-element.39), channel_id=1, source_target_pairs={{0,24},{4,28},{8,16},{12,20},{16,8},{20,12},{24,0},{28,4},{1,25},{... | collective-permute-start | bytes 110600 | tf_op jit(solution)/shard_map/ppermute | solution.py:477
  32.5 5.6 %collective-permute-start.13 = (bf16[144,128]{1,0:T(8,128)(2,1)S(1)}, bf16[144,128]{1,0:T(8,128)(2,1)S(1)}, u32[]{:S(2)}, u32[]{:S(2)}) collective-permute-start(bf16[144,128]{1,0:T(8,128)(2,1)S(1)} %get-tuple-element.36.refs_0_), channel_id=1, source_target_pairs={{0,4},{4,0},{8,12},{12,8},{16,20},{20,16},{24,28},{28,24},{1,5},{5... | collective-permute-start | bytes 110600 | tf_op jit(solution)/shard_map/ppermute | solution.py:477
  33.8 4.4 %collective-permute-start.15 = (bf16[144,128]{1,0:T(8,128)(2,1)S(1)}, bf16[144,128]{1,0:T(8,128)(2,1)S(1)}, u32[]{:S(2)}, u32[]{:S(2)}) collective-permute-start(bf16[144,128]{1,0:T(8,128)(2,1)S(1)} %collective-permute-done.14.refs_2_), channel_id=1, source_target_pairs={{0,4},{4,0},{8,12},{12,8},{16,20},{20,16},{24,28},{28,24},{1,5},{5... | collective-permute-start | bytes 110600 | tf_op jit(solution)/shard_map/ppermute | solution.py:477
  35.7 4.0 %collective-permute-start.17 = (bf16[144,128]{1,0:T(8,128)(2,1)S(1)}, bf16[144,128]{1,0:T(8,128)(2,1)S(1)}, u32[]{:S(2)}, u32[]{:S(2)}) collective-permute-start(bf16[144,128]{1,0:T(8,128)(2,1)S(1)} %collective-permute-done.16.refs_4_), channel_id=1, source_target_pairs={{0,4},{4,0},{8,12},{12,8},{16,20},{20,16},{24,28},{28,24},{1,5},{5... | collective-permute-start | bytes 110600 | tf_op jit(solution)/shard_map/ppermute | solution.py:477
  36.9 4.0 %collective-permute-start.19 = (bf16[144,128]{1,0:T(8,128)(2,1)S(1)}, bf16[144,128]{1,0:T(8,128)(2,1)S(1)}, u32[]{:S(2)}, u32[]{:S(2)}) collective-permute-start(bf16[144,128]{1,0:T(8,128)(2,1)S(1)} %collective-permute-done.18.refs_6_), channel_id=1, source_target_pairs={{0,4},{4,0},{8,12},{12,8},{16,20},{20,16},{24,28},{28,24},{1,5},{5... | collective-permute-start | bytes 110600 | tf_op jit(solution)/shard_map/ppermute | solution.py:477

commit v7 on v6

--- a/solution.py
+++ b/solution.py
@@ -173,8 +173,8 @@
         copy.start()
     rows_pad[...] = jnp.zeros(rows_pad.shape, jnp.int32)
     map_pad[...] = jnp.zeros(map_pad.shape, F32)
-    copies[0].wait()
-    copies[1].wait()
+    for copy in copies[:3]:
+        copy.wait()
     for k in range(plan.neighbors):
         rows_pad[k : k + 1, 0:each] = rows[k]
     spread = rows_pad[...]
@@ -203,21 +203,19 @@
     pick = pick_f.astype(BF16)[:pairs]
     weight = whole_weight(place_v)
     weight_out[...] = weight.astype(BF16)
-    copies[2].wait()
     corner_ids = corner_map[...]
     map_pad[0:1, 0:corners] = (corner_ids // 128).astype(F32)
     map_pad[1:2, 0:corners] = (corner_ids % 128).astype(F32)
     extra = extra_rows(plan, map_pad[...], missing.astype(F32))
-    copies[3].wait()
+    for copy in copies[3:6]:
+        copy.wait()
     load = loads[...]
     weighted = (weight * load.astype(F32)).astype(BF16)
     message[0:pairs, :] = dot(pick, load).astype(BF16)
-    copies[4].wait()
     couple = coupling_t[...]
     couple_w = couple.astype(F32) * weight_row
+    image = dot(schur[...], jnp.concatenate([weighted, place_v], axis=1))
     edge = dot(couple, place_v)
-    copies[5].wait()
-    image = dot(schur[...], jnp.concatenate([weighted, place_v], axis=1))
     pairs_out[:, :128] = (weight * (0.5 * image[:, 128:])).astype(BF16)
     pairs_out[:, 128:] = (weight * place_v.astype(F32)).astype(BF16)
     image_out[...] = weight * image[:, :128]
@@ -484,8 +482,8 @@
         blocks[1] = swap(messages[0], "sub", 1)
         for far in reversed(range(2, line, 2)):
             blocks[far + 1] = swap(blocks[far], "sub", 1)
-        for rider, distance in riders:
-            rider = lax.optimization_barrier([rider] + [blocks[k] for k in (1,)])[0]
+        for (rider, distance), k in zip(riders, (1, 2, 1)):
+            rider = lax.optimization_barrier([rider, blocks[k]])[0]
             carried.append(swap(rider, "grp", distance))
         return blocks, carried
 

time: 42.2 us -> 41.6 us (0.986)
  waiting for transfers between devices: 13.2 us -> 10.6 us
  starting transfers between devices: 22.1 us -> 24.4 us
    ppermute x20, waiting for transfers between devices: 13.2 us -> 10.6 us  [swap(): lax.ppermute(value, axis, [(at, at ^ distance) for at in range(size)])]
    ppermute x20, starting transfers between devices: 22.1 us -> 24.4 us  [swap(): lax.ppermute(value, axis, [(at, at ^ distance) for at in range(size)])]
  transfers between devices with their start and end apart: 20 -> 20, of which waited for: 11 -> 8; matrix products, arithmetic and copies ran while one was open for 0% -> 0% of each run, Pallas kernels for 2% -> 2%
where the time goes in v7:
time: 41.6 us; the launch traced here: 41.4 us
  starting transfers between devices  24.4 us (59%)
  waiting for transfers between devices  10.6 us (25%)
  Pallas kernels  5.71 us (14%)
  between operations  0.71 us (2%)
    ppermute x20, starting transfers between devices, swap(): lax.ppermute(value, axis, [(at, at ^ distance) for at in range(size)])  24.4 us
    ppermute x20, waiting for transfers between devices, swap(): lax.ppermute(value, axis, [(at, at ^ distance) for at in range(size)])  10.6 us
    pallas_call x1, Pallas kernels, line_body(): pl.pallas_call(functools.partial(prepare_kernel, plan), out_shape=(shape(...  1.91 us
    pallas_call x1, Pallas kernels, line_body(): pl.pallas_call(functools.partial(direction_kernel, plan), out_shape=(shap...  1.42 us
    pallas_call x1, Pallas kernels, line_body(): pl.pallas_call(functools.partial(result_kernel, plan), out_shape=(shape(o...  1.19 us
  transfers between devices with their start and end apart: 20, of which 8 were waited for; matrix products, arithmetic and copies ran while one was open for 0% of the time, Pallas kernels for 2%

profile of v7, /device:TPU:0, one launch (start us, length us, event | category | flops | bytes accessed | tf_op | source)
XLA Modules:
  0.0 41.4 jit_solution(18005756559669582209)
XLA Ops:
  0.6 0.0 copy-start
  0.6 1.9 %prepare.1 = (bf16[312,128]{1,0:T(8,128)(2,1)S(1)}, bf16[512,128]{1,0:T(8,128)(2,1)S(1)}, bf16[512,128]{1,0:T(8,128)(2,1)S(1)}, bf16[512,256]{1,0:T(8,128)(2,1)S...) custom-call(s32[1,6]{1,0:T(1,128)} %bitcast.21, ...), custom_call_target="tpu_custom_call" | custom-call | tf_op jit(solution)/shard_map/prepare/pallas_call | solution.py:493
  2.6 5.1 %collective-permute-start.5 = (bf16[312,128]{1,0:T(8,128)(2,1)S(1)}, bf16[312,128]{1,0:T(8,128)(2,1)S(1)}, u32[]{:S(2)}, u32[]{:S(2)}) collective-permute-start(bf16[312,128]{1,0:T(8,128)(2,1)S(1)} %get-tuple-element.25.refs_0_.refs_5_), channel_id=1, source_target_pairs={{0,24},{4,28},{8,16},{12,20},{16,8},{20,12},{24,0},{28,4},{1,25},{... | collective-permute-start | bytes 239624 | tf_op jit(solution)/shard_map/ppermute | solution.py:475
  7.7 1.5 %collective-permute-start = (bf16[312,128]{1,0:T(8,128)(2,1)S(1)}, bf16[312,128]{1,0:T(8,128)(2,1)S(1)}, u32[]{:S(2)}, u32[]{:S(2)}) collective-permute-start(bf16[312,128]{1,0:T(8,128)(2,1)S(1)} %get-tuple-element.25.refs_0_.refs_5_), channel_id=1, source_target_pairs={{0,4},{4,0},{8,12},{12,8},{16,20},{20,16},{24,28},{28,24},{1,5},{5... | collective-permute-start | bytes 239624 | tf_op jit(solution)/shard_map/ppermute | solution.py:475
  9.2 0.0 collective-permute-start.1
  9.2 0.8 %collective-permute-start.3 = (bf16[312,128]{1,0:T(8,128)(2,1)S(1)}, bf16[312,128]{1,0:T(8,128)(2,1)S(1)}, u32[]{:S(2)}, u32[]{:S(2)}) collective-permute-start(bf16[312,128]{1,0:T(8,128)(2,1)S(1)} %get-tuple-element.25.refs_0_.refs_5_), channel_id=1, source_target_pairs={{0,16},{4,20},{8,24},{12,28},{16,0},{20,4},{24,8},{28,12},{1,17},{... | collective-permute-start | bytes 239624 | tf_op jit(solution)/shard_map/ppermute | solution.py:475
  10.0 0.4 %collective-permute-done.5.refs_6_ = bf16[312,128]{1,0:T(8,128)(2,1)S(1)} collective-permute-done((bf16[312,128]{1,0:T(8,128)(2,1)S(1)}, bf16[312,128]{1,0:T(8,128)(2,1)S(1)}, u32[]{:S(2)}, u32[]{:S(2)}) %collective-permute-start.5) | collective-permute-done | bytes 79904 | tf_op jit(solution)/shard_map/ppermute | solution.py:475
  10.4 2.1 %collective-permute-start.6 = (bf16[312,128]{1,0:T(8,128)(2,1)S(1)}, bf16[312,128]{1,0:T(8,128)(2,1)S(1)}, u32[]{:S(2)}, u32[]{:S(2)}) collective-permute-start(bf16[312,128]{1,0:T(8,128)(2,1)S(1)} %collective-permute-done.5.refs_6_), channel_id=1, source_target_pairs={{0,4},{4,0},{8,12},{12,8},{16,20},{20,16},{24,28},{28,24},{1,5},{5... | collective-permute-start | bytes 239624 | tf_op jit(solution)/shard_map/ppermute | solution.py:475
  12.5 0.0 collective-permute-done.refs_1_
  12.6 0.0 copy-done
  12.6 0.0 collective-permute-start.9
  12.6 1.6 %collective-permute-start.7 = (bf16[24,2048]{1,0:T(8,128)(2,1)S(1)}, bf16[24,2048]{1,0:T(8,128)(2,1)S(1)}, u32[]{:S(2)}, u32[]{:S(2)}) collective-permute-start(bf16[24,2048]{1,0:T(8,128)(2,1)S(1)} %bitcast.13), channel_id=1, source_target_pairs={{0,1},{1,0},{2,3},{3,2},{4,5},{5,4},{6,7},{7,6},{8,9},{9,8},{10,11... | collective-permute-start | bytes 294920 | tf_op jit(solution)/shard_map/ppermute | solution.py:475
  14.2 0.0 collective-permute-done.1.refs_2_
  14.2 1.0 %collective-permute-start.8 = (bf16[24,2048]{1,0:T(8,128)(2,1)S(1)}, bf16[24,2048]{1,0:T(8,128)(2,1)S(1)}, u32[]{:S(2)}, u32[]{:S(2)}) collective-permute-start(bf16[24,2048]{1,0:T(8,128)(2,1)S(1)} %bitcast.14), channel_id=1, source_target_pairs={{0,2},{1,3},{2,0},{3,1},{4,6},{5,7},{6,4},{7,5},{8,10},{9,11},{10,... | collective-permute-start | bytes 294920 | tf_op jit(solution)/shard_map/ppermute | solution.py:475
  15.2 0.0 collective-permute-done.3.refs_4_
  15.2 1.9 %collective-permute-start.4 = (bf16[312,128]{1,0:T(8,128)(2,1)S(1)}, bf16[312,128]{1,0:T(8,128)(2,1)S(1)}, u32[]{:S(2)}, u32[]{:S(2)}) collective-permute-start(bf16[312,128]{1,0:T(8,128)(2,1)S(1)} %collective-permute-done.3.refs_4_), channel_id=1, source_target_pairs={{0,4},{4,0},{8,12},{12,8},{16,20},{20,16},{24,28},{28,24},{1,5},{5... | collective-permute-start | bytes 239624 | tf_op jit(solution)/shard_map/ppermute | solution.py:475
  17.1 0.0 collective-permute-done.6.refs_7_
  17.1 0.1 collective-permute-start.2
  17.2 2.8 %collective-permute-done.4.refs_5_ = bf16[312,128]{1,0:T(8,128)(2,1)S(1)} collective-permute-done((bf16[312,128]{1,0:T(8,128)(2,1)S(1)}, bf16[312,128]{1,0:T(8,128)(2,1)S(1)}, u32[]{:S(2)}, u32[]{:S(2)}) %collective-permute-start.4) | collective-permute-done | bytes 79904 | tf_op jit(solution)/shard_map/ppermute | solution.py:475
  20.0 1.5 %collective-permute-done.2.refs_3_ = bf16[312,128]{1,0:T(8,128)(2,1)S(1)} collective-permute-done((bf16[312,128]{1,0:T(8,128)(2,1)S(1)}, bf16[312,128]{1,0:T(8,128)(2,1)S(1)}, u32[]{:S(2)}, u32[]{:S(2)}) %collective-permute-start.2) | collective-permute-done | bytes 79904 | tf_op jit(solution)/shard_map/ppermute | solution.py:475
  21.5 0.0 collective-permute-done.9.refs_11_
  21.5 0.0 collective-permute-done.7.refs_9_
  21.5 0.0 collective-permute-done.8.refs_10_
  21.5 1.4 %direction.1 = (bf16[128,128]{1,0:T(8,128)(2,1)S(1)}, f32[512,128]{1,0:T(8,128)S(1)}, f32[512,128]{1,0:T(8,128)S(1)}, bf16[112,128]{1,0:T(8,128)(2,1)S(1)}, f32[8,128]{1,0:T(8,128)S(1)}) custom-call(bf16[312,128]{1,0:T(8,128)(2,1)S(1)} %get-tuple-element.25.refs_0_.refs_5_, bf16[312,128]{1,0:T(8,128)(2,1)S(1)} %collective-permute-done.refs_1_, ...), custom_call_target="tpu_custom_call" | custom-call | tf_op jit(solution)/shard_map/direction/pallas_call | solution.py:518
  22.9 0.1 collective-permute-start.12
  23.0 0.9 %collective-permute-start.11 = (bf16[128,128]{1,0:T(8,128)(2,1)S(1)}, bf16[128,128]{1,0:T(8,128)(2,1)S(1)}, u32[]{:S(2)}, u32[]{:S(2)}) collective-permute-start(bf16[128,128]{1,0:T(8,128)(2,1)S(1)} %get-tuple-element.34.refs_0_), channel_id=1, source_target_pairs={{0,2},{1,3},{2,0},{3,1},{4,6},{5,7},{6,4},{7,5},{8,10},{9,11},{10,... | collective-permute-start | bytes 98312 | tf_op jit(solution)/shard_map/ppermute | solution.py:475
  23.9 0.9 %collective-permute-start.10 = (bf16[128,128]{1,0:T(8,128)(2,1)S(1)}, bf16[128,128]{1,0:T(8,128)(2,1)S(1)}, u32[]{:S(2)}, u32[]{:S(2)}) collective-permute-start(bf16[128,128]{1,0:T(8,128)(2,1)S(1)} %get-tuple-element.34.refs_0_), channel_id=1, source_target_pairs={{0,1},{1,0},{2,3},{3,2},{4,5},{5,4},{6,7},{7,6},{8,9},{9,8},{10,11... | collective-permute-start | bytes 98312 | tf_op jit(solution)/shard_map/ppermute | solution.py:475
  24.8 0.5 %local.1.refs_6_ = f32[96,256]{1,0:T(8,128)S(1)} custom-call(f32[512,128]{1,0:T(8,128)S(1)} %get-tuple-element.36.local_part, bf16[512,512]{1,0:T(8,128)(2,1)S(1)} %get-tuple-element.37.schur, bf16[512,128]{1,0:T(8,128)(2,1)S(1)} %get-tuple-element.29.refs_13_.place, bf16[512,128]{1,0:T(8,128)(2,1)S(1)} %get-tuple-element.30.refs_14_.weight), custom_call_target="tpu_custom_call" | custom-call | tf_op jit(solution)/shard_map/local/pallas_call | solution.py:543
  25.4 1.0 %collective-permute-done.12.refs_3_ = bf16[128,128]{1,0:T(8,128)(2,1)S(1)} collective-permute-done((bf16[128,128]{1,0:T(8,128)(2,1)S(1)}, bf16[128,128]{1,0:T(8,128)(2,1)S(1)}, u32[]{:S(2)}, u32[]{:S(2)}) %collective-permute-start.12) | collective-permute-done | bytes 32800 | tf_op jit(solution)/shard_map/ppermute | solution.py:475
  26.3 0.9 %collective-permute-done.11.refs_2_ = bf16[128,128]{1,0:T(8,128)(2,1)S(1)} collective-permute-done((bf16[128,128]{1,0:T(8,128)(2,1)S(1)}, bf16[128,128]{1,0:T(8,128)(2,1)S(1)}, u32[]{:S(2)}, u32[]{:S(2)}) %collective-permute-start.11) | collective-permute-done | bytes 32800 | tf_op jit(solution)/shard_map/ppermute | solution.py:475
  27.2 0.0 collective-permute-done.10.refs_1_
  27.2 0.2 coarse.1
  27.4 0.2 collective-permute-start.14
  27.6 2.9 %collective-permute-start.16 = (bf16[144,128]{1,0:T(8,128)(2,1)S(1)}, bf16[144,128]{1,0:T(8,128)(2,1)S(1)}, u32[]{:S(2)}, u32[]{:S(2)}) collective-permute-start(bf16[144,128]{1,0:T(8,128)(2,1)S(1)} %get-tuple-element.40), channel_id=1, source_target_pairs={{0,16},{4,20},{8,24},{12,28},{16,0},{20,4},{24,8},{28,12},{1,17},{... | collective-permute-start | bytes 110600 | tf_op jit(solution)/shard_map/ppermute | solution.py:475
  30.5 1.4 %collective-permute-start.18 = (bf16[144,128]{1,0:T(8,128)(2,1)S(1)}, bf16[144,128]{1,0:T(8,128)(2,1)S(1)}, u32[]{:S(2)}, u32[]{:S(2)}) collective-permute-start(bf16[144,128]{1,0:T(8,128)(2,1)S(1)} %get-tuple-element.41), channel_id=1, source_target_pairs={{0,24},{4,28},{8,16},{12,20},{16,8},{20,12},{24,0},{28,4},{1,25},{... | collective-permute-start | bytes 110600 | tf_op jit(solution)/shard_map/ppermute | solution.py:475
  31.9 0.7 %collective-permute-start.13 = (bf16[144,128]{1,0:T(8,128)(2,1)S(1)}, bf16[144,128]{1,0:T(8,128)(2,1)S(1)}, u32[]{:S(2)}, u32[]{:S(2)}) collective-permute-start(bf16[144,128]{1,0:T(8,128)(2,1)S(1)} %get-tuple-element.38.refs_0_), channel_id=1, source_target_pairs={{0,4},{4,0},{8,12},{12,8},{16,20},{20,16},{24,28},{28,24},{1,5},{5... | collective-permute-start | bytes 110600 | tf_op jit(solution)/shard_map/ppermute | solution.py:475
  32.6 0.0 collective-permute-done.14.refs_2_
  32.6 1.3 %collective-permute-start.15 = (bf16[144,128]{1,0:T(8,128)(2,1)S(1)}, bf16[144,128]{1,0:T(8,128)(2,1)S(1)}, u32[]{:S(2)}, u32[]{:S(2)}) collective-permute-start(bf16[144,128]{1,0:T(8,128)(2,1)S(1)} %collective-permute-done.14.refs_2_), channel_id=1, source_target_pairs={{0,4},{4,0},{8,12},{12,8},{16,20},{20,16},{24,28},{28,24},{1,5},{5... | collective-permute-start | bytes 110600 | tf_op jit(solution)/shard_map/ppermute | solution.py:475
  33.9 0.0 collective-permute-done.16.refs_4_
  33.9 0.7 %collective-permute-start.17 = (bf16[144,128]{1,0:T(8,128)(2,1)S(1)}, bf16[144,128]{1,0:T(8,128)(2,1)S(1)}, u32[]{:S(2)}, u32[]{:S(2)}) collective-permute-start(bf16[144,128]{1,0:T(8,128)(2,1)S(1)} %collective-permute-done.16.refs_4_), channel_id=1, source_target_pairs={{0,4},{4,0},{8,12},{12,8},{16,20},{20,16},{24,28},{28,24},{1,5},{5... | collective-permute-start | bytes 110600 | tf_op jit(solution)/shard_map/ppermute | solution.py:475
  34.7 1.6 %collective-permute-done.18.refs_6_ = bf16[144,128]{1,0:T(8,128)(2,1)S(1)} collective-permute-done((bf16[144,128]{1,0:T(8,128)(2,1)S(1)}, bf16[144,128]{1,0:T(8,128)(2,1)S(1)}, u32[]{:S(2)}, u32[]{:S(2)}) %collective-permute-start.18) | collective-permute-done | bytes 36896 | tf_op jit(solution)/shard_map/ppermute | solution.py:475
  36.3 1.1 %collective-permute-start.19 = (bf16[144,128]{1,0:T(8,128)(2,1)S(1)}, bf16[144,128]{1,0:T(8,128)(2,1)S(1)}, u32[]{:S(2)}, u32[]{:S(2)}) collective-permute-start(bf16[144,128]{1,0:T(8,128)(2,1)S(1)} %collective-permute-done.18.refs_6_), channel_id=1, source_target_pairs={{0,4},{4,0},{8,12},{12,8},{16,20},{20,16},{24,28},{28,24},{1,5},{5... | collective-permute-start | bytes 110600 | tf_op jit(solution)/shard_map/ppermute | solution.py:475
  37.4 0.5 %surface.1.refs_11_ = f32[512,128]{1,0:T(8,128)S(1)} custom-call(f32[24,128]{1,0:T(8,128)S(1)} %get-tuple-element.44.own, bf16[512,512]{1,0:T(8,128)(2,1)S(1)} %get-tuple-element.37.schur, bf16[24,512]{1,0:T(8,128)(2,1)S(1)} %get-tuple-element.45.coupling_t, bf16[512,128]{1,0:T(8,128)(2,1)S(1)} %get-tuple-element.30.refs_14_.weight, ...), custom_call_target="tpu_custom_call" | custom-call | tf_op jit(solution)/shard_map/surface/pallas_call | solution.py:561
  37.9 0.0 collective-permute-done.13.refs_1_
  37.9 0.0 collective-permute-done.15.refs_3_
  37.9 0.3 collective-permute-done.17.refs_5_
  38.3 2.0 %collective-permute-done.19.refs_7_ = bf16[144,128]{1,0:T(8,128)(2,1)S(1)} collective-permute-done((bf16[144,128]{1,0:T(8,128)(2,1)S(1)}, bf16[144,128]{1,0:T(8,128)(2,1)S(1)}, u32[]{:S(2)}, u32[]{:S(2)}) %collective-permute-start.19) | collective-permute-done | bytes 36896 | tf_op jit(solution)/shard_map/ppermute | solution.py:475
  40.3 1.2 %result.1 = (f32[512,128]{1,0:T(8,128)}, f32[512,128]{1,0:T(8,128)}) custom-call(bf16[144,128]{1,0:T(8,128)(2,1)S(1)} %get-tuple-element.38.refs_0_, bf16[144,128]{1,0:T(8,128)(2,1)S(1)} %collective-permute-done.13.refs_1_, bf16[144,128]{1,0:T(8,128)(2,1)S(1)} %collective-permute-done.14.refs_2_, bf16[144,128]{1,0:T(8,128)(2,1)S(1)} %collective-permute-done.15.refs_3_, ...), custom_call_target="tpu_custom_call" | custom-call | tf_op jit(solution)/shard_map/result/pallas_call | solution.py:570
Async XLA Ops:
  0.6 11.9 %copy-start = (bf16[1,1,24,2048]{3,2,1,0:T(8,128)(2,1)S(1)}, bf16[1,1,24,2048]{3,2,1,0:T(8,128)(2,1)}, u32[]{:S(2)}) copy-start(bf16[1,1,24,2048]{3,2,1,0:T(8,128)(2,1)} %param.12) | copy-start | bytes 294916
  2.6 7.8 %collective-permute-start.5 = (bf16[312,128]{1,0:T(8,128)(2,1)S(1)}, bf16[312,128]{1,0:T(8,128)(2,1)S(1)}, u32[]{:S(2)}, u32[]{:S(2)}) collective-permute-start(bf16[312,128]{1,0:T(8,128)(2,1)S(1)} %get-tuple-element.25.refs_0_.refs_5_), channel_id=1, source_target_pairs={{0,24},{4,28},{8,16},{12,20},{16,8},{20,12},{24,0},{28,4},{1,25},{... | collective-permute-start | bytes 239624 | tf_op jit(solution)/shard_map/ppermute | solution.py:475
  7.7 4.9 %collective-permute-start = (bf16[312,128]{1,0:T(8,128)(2,1)S(1)}, bf16[312,128]{1,0:T(8,128)(2,1)S(1)}, u32[]{:S(2)}, u32[]{:S(2)}) collective-permute-start(bf16[312,128]{1,0:T(8,128)(2,1)S(1)} %get-tuple-element.25.refs_0_.refs_5_), channel_id=1, source_target_pairs={{0,4},{4,0},{8,12},{12,8},{16,20},{20,16},{24,28},{28,24},{1,5},{5... | collective-permute-start | bytes 239624 | tf_op jit(solution)/shard_map/ppermute | solution.py:475
  9.2 5.0 %collective-permute-start.1 = (bf16[312,128]{1,0:T(8,128)(2,1)S(1)}, bf16[312,128]{1,0:T(8,128)(2,1)S(1)}, u32[]{:S(2)}, u32[]{:S(2)}) collective-permute-start(bf16[312,128]{1,0:T(8,128)(2,1)S(1)} %get-tuple-element.25.refs_0_.refs_5_), channel_id=1, source_target_pairs={{0,8},{4,12},{8,0},{12,4},{16,24},{20,28},{24,16},{28,20},{1,9},{5... | collective-permute-start | bytes 239624 | tf_op jit(solution)/shard_map/ppermute | solution.py:475
  9.2 6.0 %collective-permute-start.3 = (bf16[312,128]{1,0:T(8,128)(2,1)S(1)}, bf16[312,128]{1,0:T(8,128)(2,1)S(1)}, u32[]{:S(2)}, u32[]{:S(2)}) collective-permute-start(bf16[312,128]{1,0:T(8,128)(2,1)S(1)} %get-tuple-element.25.refs_0_.refs_5_), channel_id=1, source_target_pairs={{0,16},{4,20},{8,24},{12,28},{16,0},{20,4},{24,8},{28,12},{1,17},{... | collective-permute-start | bytes 239624 | tf_op jit(solution)/shard_map/ppermute | solution.py:475
  10.4 6.7 %collective-permute-start.6 = (bf16[312,128]{1,0:T(8,128)(2,1)S(1)}, bf16[312,128]{1,0:T(8,128)(2,1)S(1)}, u32[]{:S(2)}, u32[]{:S(2)}) collective-permute-start(bf16[312,128]{1,0:T(8,128)(2,1)S(1)} %collective-permute-done.5.refs_6_), channel_id=1, source_target_pairs={{0,4},{4,0},{8,12},{12,8},{16,20},{20,16},{24,28},{28,24},{1,5},{5... | collective-permute-start | bytes 239624 | tf_op jit(solution)/shard_map/ppermute | solution.py:475
  12.6 8.9 %collective-permute-start.9 = (bf16[24,2048]{1,0:T(8,128)(2,1)S(1)}, bf16[24,2048]{1,0:T(8,128)(2,1)S(1)}, u32[]{:S(2)}, u32[]{:S(2)}) collective-permute-start(bf16[24,2048]{1,0:T(8,128)(2,1)S(1)} %bitcast.12), channel_id=1, source_target_pairs={{0,3},{1,2},{2,1},{3,0},{4,7},{5,6},{6,5},{7,4},{8,11},{9,10},{10,... | collective-permute-start | bytes 294920 | tf_op jit(solution)/shard_map/ppermute | solution.py:475
  12.6 8.9 %collective-permute-start.7 = (bf16[24,2048]{1,0:T(8,128)(2,1)S(1)}, bf16[24,2048]{1,0:T(8,128)(2,1)S(1)}, u32[]{:S(2)}, u32[]{:S(2)}) collective-permute-start(bf16[24,2048]{1,0:T(8,128)(2,1)S(1)} %bitcast.13), channel_id=1, source_target_pairs={{0,1},{1,0},{2,3},{3,2},{4,5},{5,4},{6,7},{7,6},{8,9},{9,8},{10,11... | collective-permute-start | bytes 294920 | tf_op jit(solution)/shard_map/ppermute | solution.py:475
  14.2 7.3 %collective-permute-start.8 = (bf16[24,2048]{1,0:T(8,128)(2,1)S(1)}, bf16[24,2048]{1,0:T(8,128)(2,1)S(1)}, u32[]{:S(2)}, u32[]{:S(2)}) collective-permute-start(bf16[24,2048]{1,0:T(8,128)(2,1)S(1)} %bitcast.14), channel_id=1, source_target_pairs={{0,2},{1,3},{2,0},{3,1},{4,6},{5,7},{6,4},{7,5},{8,10},{9,11},{10,... | collective-permute-start | bytes 294920 | tf_op jit(solution)/shard_map/ppermute | solution.py:475
  15.2 4.8 %collective-permute-start.4 = (bf16[312,128]{1,0:T(8,128)(2,1)S(1)}, bf16[312,128]{1,0:T(8,128)(2,1)S(1)}, u32[]{:S(2)}, u32[]{:S(2)}) collective-permute-start(bf16[312,128]{1,0:T(8,128)(2,1)S(1)} %collective-permute-done.3.refs_4_), channel_id=1, source_target_pairs={{0,4},{4,0},{8,12},{12,8},{16,20},{20,16},{24,28},{28,24},{1,5},{5... | collective-permute-start | bytes 239624 | tf_op jit(solution)/shard_map/ppermute | solution.py:475
  17.1 4.4 %collective-permute-start.2 = (bf16[312,128]{1,0:T(8,128)(2,1)S(1)}, bf16[312,128]{1,0:T(8,128)(2,1)S(1)}, u32[]{:S(2)}, u32[]{:S(2)}) collective-permute-start(bf16[312,128]{1,0:T(8,128)(2,1)S(1)} %collective-permute-done.1.refs_2_), channel_id=1, source_target_pairs={{0,4},{4,0},{8,12},{12,8},{16,20},{20,16},{24,28},{28,24},{1,5},{5... | collective-permute-start | bytes 239624 | tf_op jit(solution)/shard_map/ppermute | solution.py:475
  22.9 3.4 %collective-permute-start.12 = (bf16[128,128]{1,0:T(8,128)(2,1)S(1)}, bf16[128,128]{1,0:T(8,128)(2,1)S(1)}, u32[]{:S(2)}, u32[]{:S(2)}) collective-permute-start(bf16[128,128]{1,0:T(8,128)(2,1)S(1)} %get-tuple-element.34.refs_0_), channel_id=1, source_target_pairs={{0,3},{1,2},{2,1},{3,0},{4,7},{5,6},{6,5},{7,4},{8,11},{9,10},{10,... | collective-permute-start | bytes 98312 | tf_op jit(solution)/shard_map/ppermute | solution.py:475
  23.0 4.3 %collective-permute-start.11 = (bf16[128,128]{1,0:T(8,128)(2,1)S(1)}, bf16[128,128]{1,0:T(8,128)(2,1)S(1)}, u32[]{:S(2)}, u32[]{:S(2)}) collective-permute-start(bf16[128,128]{1,0:T(8,128)(2,1)S(1)} %get-tuple-element.34.refs_0_), channel_id=1, source_target_pairs={{0,2},{1,3},{2,0},{3,1},{4,6},{5,7},{6,4},{7,5},{8,10},{9,11},{10,... | collective-permute-start | bytes 98312 | tf_op jit(solution)/shard_map/ppermute | solution.py:475
  23.9 3.3 %collective-permute-start.10 = (bf16[128,128]{1,0:T(8,128)(2,1)S(1)}, bf16[128,128]{1,0:T(8,128)(2,1)S(1)}, u32[]{:S(2)}, u32[]{:S(2)}) collective-permute-start(bf16[128,128]{1,0:T(8,128)(2,1)S(1)} %get-tuple-element.34.refs_0_), channel_id=1, source_target_pairs={{0,1},{1,0},{2,3},{3,2},{4,5},{5,4},{6,7},{7,6},{8,9},{9,8},{10,11... | collective-permute-start | bytes 98312 | tf_op jit(solution)/shard_map/ppermute | solution.py:475
  27.4 5.2 %collective-permute-start.14 = (bf16[144,128]{1,0:T(8,128)(2,1)S(1)}, bf16[144,128]{1,0:T(8,128)(2,1)S(1)}, u32[]{:S(2)}, u32[]{:S(2)}) collective-permute-start(bf16[144,128]{1,0:T(8,128)(2,1)S(1)} %get-tuple-element.39), channel_id=1, source_target_pairs={{0,8},{4,12},{8,0},{12,4},{16,24},{20,28},{24,16},{28,20},{1,9},{5... | collective-permute-start | bytes 110600 | tf_op jit(solution)/shard_map/ppermute | solution.py:475
  27.6 6.3 %collective-permute-start.16 = (bf16[144,128]{1,0:T(8,128)(2,1)S(1)}, bf16[144,128]{1,0:T(8,128)(2,1)S(1)}, u32[]{:S(2)}, u32[]{:S(2)}) collective-permute-start(bf16[144,128]{1,0:T(8,128)(2,1)S(1)} %get-tuple-element.40), channel_id=1, source_target_pairs={{0,16},{4,20},{8,24},{12,28},{16,0},{20,4},{24,8},{28,12},{1,17},{... | collective-permute-start | bytes 110600 | tf_op jit(solution)/shard_map/ppermute | solution.py:475
  30.5 5.8 %collective-permute-start.18 = (bf16[144,128]{1,0:T(8,128)(2,1)S(1)}, bf16[144,128]{1,0:T(8,128)(2,1)S(1)}, u32[]{:S(2)}, u32[]{:S(2)}) collective-permute-start(bf16[144,128]{1,0:T(8,128)(2,1)S(1)} %get-tuple-element.41), channel_id=1, source_target_pairs={{0,24},{4,28},{8,16},{12,20},{16,8},{20,12},{24,0},{28,4},{1,25},{... | collective-permute-start | bytes 110600 | tf_op jit(solution)/shard_map/ppermute | solution.py:475
  31.9 6.0 %collective-permute-start.13 = (bf16[144,128]{1,0:T(8,128)(2,1)S(1)}, bf16[144,128]{1,0:T(8,128)(2,1)S(1)}, u32[]{:S(2)}, u32[]{:S(2)}) collective-permute-start(bf16[144,128]{1,0:T(8,128)(2,1)S(1)} %get-tuple-element.38.refs_0_), channel_id=1, source_target_pairs={{0,4},{4,0},{8,12},{12,8},{16,20},{20,16},{24,28},{28,24},{1,5},{5... | collective-permute-start | bytes 110600 | tf_op jit(solution)/shard_map/ppermute | solution.py:475
  32.6 5.3 %collective-permute-start.15 = (bf16[144,128]{1,0:T(8,128)(2,1)S(1)}, bf16[144,128]{1,0:T(8,128)(2,1)S(1)}, u32[]{:S(2)}, u32[]{:S(2)}) collective-permute-start(bf16[144,128]{1,0:T(8,128)(2,1)S(1)} %collective-permute-done.14.refs_2_), channel_id=1, source_target_pairs={{0,4},{4,0},{8,12},{12,8},{16,20},{20,16},{24,28},{28,24},{1,5},{5... | collective-permute-start | bytes 110600 | tf_op jit(solution)/shard_map/ppermute | solution.py:475
  33.9 4.3 %collective-permute-start.17 = (bf16[144,128]{1,0:T(8,128)(2,1)S(1)}, bf16[144,128]{1,0:T(8,128)(2,1)S(1)}, u32[]{:S(2)}, u32[]{:S(2)}) collective-permute-start(bf16[144,128]{1,0:T(8,128)(2,1)S(1)} %collective-permute-done.16.refs_4_), channel_id=1, source_target_pairs={{0,4},{4,0},{8,12},{12,8},{16,20},{20,16},{24,28},{28,24},{1,5},{5... | collective-permute-start | bytes 110600 | tf_op jit(solution)/shard_map/ppermute | solution.py:475
  36.3 4.0 %collective-permute-start.19 = (bf16[144,128]{1,0:T(8,128)(2,1)S(1)}, bf16[144,128]{1,0:T(8,128)(2,1)S(1)}, u32[]{:S(2)}, u32[]{:S(2)}) collective-permute-start(bf16[144,128]{1,0:T(8,128)(2,1)S(1)} %collective-permute-done.18.refs_6_), channel_id=1, source_target_pairs={{0,4},{4,0},{8,12},{12,8},{16,20},{20,16},{24,28},{28,24},{1,5},{5... | collective-permute-start | bytes 110600 | tf_op jit(solution)/shard_map/ppermute | solution.py:475
